TPU v7x, 32 devices: a whole 2x2x4 slice. The times are simulated.
32 devices in a mesh: dp: 8 (over z, y), fsdp: 4 (over x, core).
Axes of the slice: x: 2, y: 2, z: 4, core: 2. Of those that a mesh axis runs over, the one named last changes fastest.
Arguments:
- frames_in: bfloat16 [64, 16, 32, 256], P(('dp', 'fsdp')), may hold values from -40 to 40
- domain: int32 [64], P(('dp', 'fsdp')), may hold values from 0 to 1, as said below
- kernel_one: bfloat16 [2304, 512], P('dp', 'fsdp'), may hold values from -0.125 to 0.125
- kernel_two: bfloat16 [4608, 512], P('dp', 'fsdp'), may hold values from -0.09375 to 0.09375
- kernel_three: bfloat16 [4608, 512], P('dp', 'fsdp'), may hold values from -0.09375 to 0.09375
- attn_enc: bfloat16 [512, 1536], P('dp', 'fsdp'), may hold values from -0.25 to 0.25
- kernel_four: bfloat16 [4608, 512], P('dp', 'fsdp'), may hold values from -0.09375 to 0.09375
- kernel_five: bfloat16 [4608, 512], P('dp', 'fsdp'), may hold values from -0.09375 to 0.09375
- kernel_six: bfloat16 [4608, 256], P('dp', 'fsdp'), may hold values from -0.09375 to 0.09375
- attn_dec: bfloat16 [512, 768], P('dp', 'fsdp'), may hold values from -0.25 to 0.25
- gains: float32 [5120], P(('dp', 'fsdp')), may hold values from 0.5 to 1.5
- biases: float32 [5120], P(('dp', 'fsdp')), may hold values from -3 to 3
- enc_cot: bfloat16 [64, 8, 16, 3, 512], P(('dp', 'fsdp')), may hold values from -40 to 40
- dec_cot: bfloat16 [64, 16, 32, 3, 256], P(('dp', 'fsdp')), may hold values from -40 to 40
Outputs:
- task_features: float32 [64, 8, 16, 3, 512], P(('dp', 'fsdp'))
- task_maps: float32 [64, 16, 32, 3, 256], P(('dp', 'fsdp'))
- frames_grad: float32 [64, 16, 32, 256], P(('dp', 'fsdp'))
- kernel_one_grad: float32 [2304, 512], P('dp', 'fsdp')
- kernel_two_grad: float32 [4608, 512], P('dp', 'fsdp')
- kernel_three_grad: float32 [4608, 512], P('dp', 'fsdp')
- attn_enc_grad: float32 [512, 1536], P('dp', 'fsdp')
- kernel_four_grad: float32 [4608, 512], P('dp', 'fsdp')
- kernel_five_grad: float32 [4608, 512], P('dp', 'fsdp')
- kernel_six_grad: float32 [4608, 256], P('dp', 'fsdp')
- attn_dec_grad: float32 [512, 768], P('dp', 'fsdp')
- gains_grad: float32 [5120], P(('dp', 'fsdp'))
- biases_grad: float32 [5120], P(('dp', 'fsdp'))
Inputs may be any that keep to these rules, and one draw needn't show every extreme that they name: Exactly 40 frames have domain 0 and the others domain 1; which frames is drawn.
All inputs are finite; a program needn't handle non-finite values.
Results may differ from a plain program's by a relative error of at most 0.025.
Values may be sent and summed in bfloat16 or wider, within the bound.
No kernel may reach another device: no remote copies, remote signals or barrier semaphores. Data moves between devices by JAX's collectives and lax.ppermute only.
A program may use at most 256 MiB of HBM per device.

v0:
```python
import jax
import jax.numpy as jnp
from jax import lax
from jax.sharding import PartitionSpec as P

C_IN = 256
C_MID = 512
C_DEC = 256
TASKS = 3


eps = 1e-05
HIGH = lax.Precision.HIGHEST


def conv_apply(source, kernel):
    frame_count, grid_rows, grid_cols, chans_in = source.shape
    padded = jnp.pad(source, ((0, 0), (1, 1), (1, 1), (0, 0)))
    summed = jnp.zeros((frame_count * grid_rows * grid_cols, kernel.shape[1]), jnp.float32)
    for offset in range(9):
        row_at = offset // 3
        col_at = offset % 3
        window = padded[:, row_at : row_at + grid_rows, col_at : col_at + grid_cols, :]
        summed = summed + jnp.dot(
            window.reshape(-1, chans_in),
            kernel[offset * chans_in : (offset + 1) * chans_in],
            preferred_element_type=jnp.float32,
        )
    return summed.reshape(frame_count, grid_rows, grid_cols, kernel.shape[1])


def conv_input_grad(upstream, kernel, chans_in):
    frame_count, grid_rows, grid_cols, chans_out = upstream.shape
    padded = jnp.pad(upstream, ((0, 0), (1, 1), (1, 1), (0, 0)))
    summed = jnp.zeros((frame_count * grid_rows * grid_cols, chans_in), jnp.float32)
    for offset in range(9):
        row_at = 2 - offset // 3
        col_at = 2 - offset % 3
        window = padded[:, row_at : row_at + grid_rows, col_at : col_at + grid_cols, :]
        summed = summed + lax.dot_general(
            window.reshape(-1, chans_out),
            kernel[offset * chans_in : (offset + 1) * chans_in],
            (((1,), (1,)), ((), ())),
            preferred_element_type=jnp.float32,
        )
    return summed.reshape(frame_count, grid_rows, grid_cols, chans_in)


def conv_kernel_grad(source, upstream):
    frame_count, grid_rows, grid_cols, chans_in = source.shape
    padded = jnp.pad(source, ((0, 0), (1, 1), (1, 1), (0, 0)))
    upstream_flat = upstream.reshape(-1, upstream.shape[-1])
    pieces = []
    for offset in range(9):
        row_at = offset // 3
        col_at = offset % 3
        window = padded[:, row_at : row_at + grid_rows, col_at : col_at + grid_cols, :]
        pieces.append(
            lax.dot_general(
                window.reshape(-1, chans_in),
                upstream_flat,
                (((0,), (0,)), ((), ())),
                preferred_element_type=jnp.float32,
            )
        )
    return jnp.concatenate(pieces, 0)


def silu_slope(pre):
    sigmoid_at = jax.nn.sigmoid(pre)
    return sigmoid_at * (1.0 + pre * (1.0 - sigmoid_at))


def domain_sums(onehot, values):
    return jnp.einsum("fd,fpc->dc", onehot, values, precision=HIGH)


def spread(onehot, table):
    return jnp.dot(onehot, table, precision=HIGH)[:, None, :]


def norm_layer(values, gain, bias, onehot, counts):
    shaped = values.reshape(values.shape[0], -1, values.shape[-1])
    first_sum, second_sum = lax.psum(
        (domain_sums(onehot, shaped), domain_sums(onehot, shaped * shaped)), ("dp", "fsdp")
    )
    average = first_sum / counts[:, None]
    variance = second_sum / counts[:, None] - average * average
    inverse = spread(onehot, lax.rsqrt(variance + eps))
    normed = (shaped - spread(onehot, average)) * inverse
    return ((normed * gain + bias).reshape(values.shape), normed, inverse)


def norm_back(upstream, normed, inverse, gain, onehot, counts):
    shaped = upstream.reshape(normed.shape)
    sum_grad, sum_cross = lax.psum(
        (domain_sums(onehot, shaped), domain_sums(onehot, shaped * normed)), ("dp", "fsdp")
    )
    centred = (
        shaped
        - spread(onehot, sum_grad / counts[:, None])
        - normed * spread(onehot, sum_cross / counts[:, None])
    )
    return (inverse * gain * centred, jnp.sum(sum_cross, 0), jnp.sum(sum_grad, 0))


def pool_mask(top, mask):
    frame_count, grid_rows, grid_cols, chans = top.shape
    blocks = top.reshape(frame_count, grid_rows // 2, 2, grid_cols // 2, 2, chans)
    exponent = jnp.exp(blocks)
    weights = exponent / jnp.sum(exponent, axis=(2, 4), keepdims=True)
    pooled = jnp.sum(weights * blocks, axis=(2, 4))
    attended = (
        mask.reshape(frame_count, grid_rows // 2, 2, grid_cols // 2, 2, TASKS, chans)
        * blocks[:, :, :, :, :, None, :]
    )
    task_out = jnp.sum(attended * weights[:, :, :, :, :, None, :], axis=(2, 4))
    unpooled = (weights * pooled[:, :, None, :, None, :]).reshape(top.shape)
    return (task_out, unpooled)


def gather_section(first, second, third, fourth):
    by_columns = (
        lax.all_gather(first, "fsdp", axis=1, tiled=True),
        lax.all_gather(second, "fsdp", axis=1, tiled=True),
        lax.all_gather(third, "fsdp", axis=1, tiled=True),
        lax.all_gather(fourth, "fsdp", axis=1, tiled=True),
    )
    return (
        lax.all_gather(by_columns[0], "dp", axis=0, tiled=True),
        lax.all_gather(by_columns[1], "dp", axis=0, tiled=True),
        lax.all_gather(by_columns[2], "dp", axis=0, tiled=True),
        lax.all_gather(by_columns[3], "dp", axis=0, tiled=True),
    )


def reduce_section(first, second, third, fourth):
    by_rows = (
        lax.psum_scatter(first, "dp", scatter_dimension=0, tiled=True),
        lax.psum_scatter(second, "dp", scatter_dimension=0, tiled=True),
        lax.psum_scatter(third, "dp", scatter_dimension=0, tiled=True),
        lax.psum_scatter(fourth, "dp", scatter_dimension=0, tiled=True),
    )
    return (
        lax.psum_scatter(
            by_rows[0].astype(jnp.bfloat16), "fsdp", scatter_dimension=1, tiled=True
        ).astype(jnp.float32),
        lax.psum_scatter(
            by_rows[1].astype(jnp.bfloat16), "fsdp", scatter_dimension=1, tiled=True
        ).astype(jnp.float32),
        lax.psum_scatter(
            by_rows[2].astype(jnp.bfloat16), "fsdp", scatter_dimension=1, tiled=True
        ).astype(jnp.float32),
        lax.psum_scatter(
            by_rows[3].astype(jnp.bfloat16), "fsdp", scatter_dimension=1, tiled=True
        ).astype(jnp.float32),
    )


def body(
    frames_in,
    domain,
    kernel_one,
    kernel_two,
    kernel_three,
    attn_enc,
    kernel_four,
    kernel_five,
    kernel_six,
    attn_dec,
    gains,
    biases,
    enc_cot,
    dec_cot,
):
    onehot = (domain[:, None] == jnp.arange(2, dtype=jnp.int32)[None, :]).astype(jnp.float32)
    total_frames = domain.shape[0] * lax.axis_size(("dp", "fsdp"))
    first_count = total_frames * 5 // 8
    pixel_count = frames_in.shape[1] * frames_in.shape[2]
    counts = jnp.array(
        [first_count * pixel_count, (total_frames - first_count) * pixel_count], jnp.float32
    )
    all_gains, all_biases = (
        lax.all_gather(gains, ("dp", "fsdp"), axis=0, tiled=True),
        lax.all_gather(biases, ("dp", "fsdp"), axis=0, tiled=True),
    )
    widths_list = [C_MID, C_MID, C_MID, TASKS * C_MID, C_MID, C_MID, C_DEC, TASKS * C_DEC]
    gain_list = []
    bias_list = []
    position = 0
    for extent in widths_list:
        gain_list.append(all_gains[position : position + extent])
        bias_list.append(all_biases[position : position + extent])
        position = position + extent
    frame_count, grid_rows, grid_cols = (frames_in.shape[0], frames_in.shape[1], frames_in.shape[2])
    full_one, full_two, full_three, full_attn = gather_section(
        kernel_one, kernel_two, kernel_three, attn_enc
    )
    pre_one = conv_apply(frames_in, full_one)
    act_one, normed_one, inverse_one = norm_layer(
        pre_one, gain_list[0], bias_list[0], onehot, counts
    )
    enc_one = jax.nn.silu(act_one).astype(jnp.bfloat16)
    pre_two = conv_apply(enc_one, full_two)
    act_two, normed_two, inverse_two = norm_layer(
        pre_two, gain_list[1], bias_list[1], onehot, counts
    )
    enc_two = jax.nn.silu(act_two).astype(jnp.bfloat16)
    pre_three = conv_apply(enc_two, full_three)
    act_three, normed_three, inverse_three = norm_layer(
        pre_three, gain_list[2], bias_list[2], onehot, counts
    )
    top = jax.nn.silu(act_three)
    pre_attend = jnp.dot(enc_two.reshape(-1, C_MID), full_attn, preferred_element_type=jnp.float32)
    pre_attend = pre_attend.reshape(frame_count, grid_rows, grid_cols, TASKS * C_MID)
    act_attend, normed_attend, inverse_attend = norm_layer(
        pre_attend, gain_list[3], bias_list[3], onehot, counts
    )
    mask = jax.nn.sigmoid(act_attend)
    middle_out, middle_back = jax.vjp(pool_mask, top, mask)
    task_features = middle_out[0]
    unpooled = middle_out[1].astype(jnp.bfloat16)
    full_four, full_five, full_six, full_gate = gather_section(
        kernel_four, kernel_five, kernel_six, attn_dec
    )
    pre_four = conv_apply(unpooled, full_four)
    act_four, normed_four, inverse_four = norm_layer(
        pre_four, gain_list[4], bias_list[4], onehot, counts
    )
    dec_one = jax.nn.silu(act_four).astype(jnp.bfloat16)
    pre_five = conv_apply(dec_one, full_five)
    act_five, normed_five, inverse_five = norm_layer(
        pre_five, gain_list[5], bias_list[5], onehot, counts
    )
    dec_two = jax.nn.silu(act_five).astype(jnp.bfloat16)
    pre_six = conv_apply(dec_two, full_six)
    act_six, normed_six, inverse_six = norm_layer(
        pre_six, gain_list[6], bias_list[6], onehot, counts
    )
    bottom = jax.nn.silu(act_six)
    pre_gate = jnp.dot(dec_one.reshape(-1, C_MID), full_gate, preferred_element_type=jnp.float32)
    pre_gate = pre_gate.reshape(frame_count, grid_rows, grid_cols, TASKS * C_DEC)
    act_gate, normed_gate, inverse_gate = norm_layer(
        pre_gate, gain_list[7], bias_list[7], onehot, counts
    )
    gate = jax.nn.sigmoid(act_gate)
    gate_tasks = gate.reshape(frame_count, grid_rows, grid_cols, TASKS, C_DEC)
    task_maps = gate_tasks * bottom[:, :, :, None, :]
    upstream = dec_cot.astype(jnp.float32)
    grad_gate = (upstream * bottom[:, :, :, None, :]).reshape(pre_gate.shape)
    grad_bottom = jnp.sum(upstream * gate_tasks, axis=3)
    grad_pre_gate, gain_grad_gate, bias_grad_gate = norm_back(
        grad_gate * gate * (1.0 - gate), normed_gate, inverse_gate, gain_list[7], onehot, counts
    )
    low_gate = grad_pre_gate.reshape(-1, TASKS * C_DEC).astype(jnp.bfloat16)
    grad_pre_six, gain_grad_six, bias_grad_six = norm_back(
        grad_bottom * silu_slope(act_six), normed_six, inverse_six, gain_list[6], onehot, counts
    )
    low_six = grad_pre_six.reshape(pre_six.shape).astype(jnp.bfloat16)
    grad_kernel_six = conv_kernel_grad(dec_two, low_six)
    grad_dec_two = conv_input_grad(low_six, full_six, C_MID)
    grad_pre_five, gain_grad_five, bias_grad_five = norm_back(
        grad_dec_two * silu_slope(act_five), normed_five, inverse_five, gain_list[5], onehot, counts
    )
    low_five = grad_pre_five.reshape(pre_five.shape).astype(jnp.bfloat16)
    grad_kernel_five = conv_kernel_grad(dec_one, low_five)
    grad_dec_one = conv_input_grad(low_five, full_five, C_MID) + lax.dot_general(
        low_gate, full_gate, (((1,), (1,)), ((), ())), preferred_element_type=jnp.float32
    ).reshape(pre_five.shape)
    grad_attn_dec = lax.dot_general(
        dec_one.reshape(-1, C_MID),
        low_gate,
        (((0,), (0,)), ((), ())),
        preferred_element_type=jnp.float32,
    )
    grad_pre_four, gain_grad_four, bias_grad_four = norm_back(
        grad_dec_one * silu_slope(act_four), normed_four, inverse_four, gain_list[4], onehot, counts
    )
    low_four = grad_pre_four.reshape(pre_four.shape).astype(jnp.bfloat16)
    grad_kernel_four = conv_kernel_grad(unpooled, low_four)
    grad_unpooled = conv_input_grad(low_four, full_four, C_MID)
    dec_grads = reduce_section(grad_kernel_four, grad_kernel_five, grad_kernel_six, grad_attn_dec)
    grad_top, grad_mask = middle_back((enc_cot.astype(jnp.float32), grad_unpooled))
    grad_pre_attend, gain_grad_attend, bias_grad_attend = norm_back(
        grad_mask * mask * (1.0 - mask), normed_attend, inverse_attend, gain_list[3], onehot, counts
    )
    low_attend = grad_pre_attend.reshape(-1, TASKS * C_MID).astype(jnp.bfloat16)
    grad_pre_three, gain_grad_three, bias_grad_three = norm_back(
        grad_top * silu_slope(act_three), normed_three, inverse_three, gain_list[2], onehot, counts
    )
    low_three = grad_pre_three.reshape(pre_three.shape).astype(jnp.bfloat16)
    grad_kernel_three = conv_kernel_grad(enc_two, low_three)
    grad_enc_two = conv_input_grad(low_three, full_three, C_MID) + lax.dot_general(
        low_attend, full_attn, (((1,), (1,)), ((), ())), preferred_element_type=jnp.float32
    ).reshape(pre_two.shape)
    grad_attn_enc = lax.dot_general(
        enc_two.reshape(-1, C_MID),
        low_attend,
        (((0,), (0,)), ((), ())),
        preferred_element_type=jnp.float32,
    )
    grad_pre_two, gain_grad_two, bias_grad_two = norm_back(
        grad_enc_two * silu_slope(act_two), normed_two, inverse_two, gain_list[1], onehot, counts
    )
    low_two = grad_pre_two.reshape(pre_two.shape).astype(jnp.bfloat16)
    grad_kernel_two = conv_kernel_grad(enc_one, low_two)
    grad_enc_one = conv_input_grad(low_two, full_two, C_MID)
    grad_pre_one, gain_grad_one, bias_grad_one = norm_back(
        grad_enc_one * silu_slope(act_one), normed_one, inverse_one, gain_list[0], onehot, counts
    )
    low_one = grad_pre_one.reshape(pre_one.shape).astype(jnp.bfloat16)
    grad_kernel_one = conv_kernel_grad(frames_in, low_one)
    frames_grad = conv_input_grad(low_one, full_one, C_IN)
    enc_grads = reduce_section(grad_kernel_one, grad_kernel_two, grad_kernel_three, grad_attn_enc)
    full_gain_grad = jnp.concatenate(
        [
            gain_grad_one,
            gain_grad_two,
            gain_grad_three,
            gain_grad_attend,
            gain_grad_four,
            gain_grad_five,
            gain_grad_six,
            gain_grad_gate,
        ],
        0,
    )
    full_bias_grad = jnp.concatenate(
        [
            bias_grad_one,
            bias_grad_two,
            bias_grad_three,
            bias_grad_attend,
            bias_grad_four,
            bias_grad_five,
            bias_grad_six,
            bias_grad_gate,
        ],
        0,
    )
    shard_len = gains.shape[0]
    shard_start = lax.axis_index(("dp", "fsdp")) * shard_len
    gains_grad = lax.dynamic_slice_in_dim(full_gain_grad, shard_start, shard_len)
    biases_grad = lax.dynamic_slice_in_dim(full_bias_grad, shard_start, shard_len)
    return (
        task_features,
        task_maps,
        frames_grad,
        enc_grads[0],
        enc_grads[1],
        enc_grads[2],
        enc_grads[3],
        dec_grads[0],
        dec_grads[1],
        dec_grads[2],
        dec_grads[3],
        gains_grad,
        biases_grad,
    )


def solution(mesh):
    return jax.shard_map(
        body,
        mesh=mesh,
        in_specs=(
            P(("dp", "fsdp"), None, None, None),
            P(("dp", "fsdp")),
            P("dp", "fsdp"),
            P("dp", "fsdp"),
            P("dp", "fsdp"),
            P("dp", "fsdp"),
            P("dp", "fsdp"),
            P("dp", "fsdp"),
            P("dp", "fsdp"),
            P("dp", "fsdp"),
            P(("dp", "fsdp")),
            P(("dp", "fsdp")),
            P(("dp", "fsdp"), None, None, None, None),
            P(("dp", "fsdp"), None, None, None, None),
        ),
        out_specs=(
            P(("dp", "fsdp"), None, None, None, None),
            P(("dp", "fsdp"), None, None, None, None),
            P(("dp", "fsdp"), None, None, None),
            P("dp", "fsdp"),
            P("dp", "fsdp"),
            P("dp", "fsdp"),
            P("dp", "fsdp"),
            P("dp", "fsdp"),
            P("dp", "fsdp"),
            P("dp", "fsdp"),
            P("dp", "fsdp"),
            P(("dp", "fsdp")),
            P(("dp", "fsdp")),
        ),
        check_vma=False,
    )
```

profile of v0, /device:TPU:0, one launch (start us, length us, event | category | flops | bytes accessed | tf_op | source)
XLA Modules:
  0.0 2082.2 jit_solution(9772535230332163681)
XLA Ops:
  70.9 36.6 %all_gather.67 = bf16[512,768]{1,0:T(8,128)(2,1)} all-gather(bf16[64,768]{1,0:T(8,128)(2,1)S(1)} %bitcast.1023), channel_id=1, replica_groups=mesh['dp'=8,'fsdp'=4] {'dp'}, dimensions={0}, use_global_device_ids=true | all-gather | bytes 884736 | tf_op jit(solution)/shard_map/all_gather | solution.py:133
  118.9 41.5 %all-reduce.25 = (f32[5120]{0:T(1024)S(1)}, f32[5120]{0:T(1024)S(1)}, f32[2,512]{1,0:T(2,128)S(1)}, f32[2,512]{1,0:T(2,128)S(1)}) all-reduce(f32[5120]{0:T(1024)S(1)} %dynamic-update-slice.1, f32[5120]{0:T(1024)S(1)} %dynamic-update-slice, f32[2,512]{1,0:T(2,128)S(1)} %fusion.439, ...), channel_id=1, replica_groups=mesh['dp'=8,'fsdp'=4] {'dp','fsdp'}, use_global_device_ids=true, to_apply=%add.13 | all-reduce | flops 12288 | bytes 98304
  183.5 44.0 %all-reduce.24 = (f32[2,512]{1,0:T(2,128)S(1)}, f32[2,512]{1,0:T(2,128)S(1)}) all-reduce(f32[2,512]{1,0:T(2,128)S(1)} %fusion.437, f32[2,512]{1,0:T(2,128)S(1)} %fusion.438), channel_id=1, replica_groups=mesh['dp'=8,'fsdp'=4] {'dp','fsdp'}, use_global_device_ids=true, to_apply=%region_7.8 | all-reduce | flops 2048 | bytes 16384 | tf_op jit(solution)/shard_map/psum | solution.py:84
  251.3 40.3 %all-reduce.23 = (f32[2,512]{1,0:T(2,128)S(1)}, f32[2,512]{1,0:T(2,128)S(1)}) all-reduce(f32[2,512]{1,0:T(2,128)S(1)} %fusion.433, f32[2,512]{1,0:T(2,128)S(1)} %fusion.434), channel_id=1, replica_groups=mesh['dp'=8,'fsdp'=4] {'dp','fsdp'}, use_global_device_ids=true, to_apply=%region_15.16 | all-reduce | flops 2048 | bytes 16384 | tf_op jit(solution)/shard_map/psum | solution.py:84
  348.7 42.2 %all-reduce.22 = (f32[2,512]{1,0:T(2,128)S(1)}, f32[2,512]{1,0:T(2,128)S(1)}) all-reduce(f32[2,512]{1,0:T(2,128)S(1)} %fusion.431, f32[2,512]{1,0:T(2,128)S(1)} %fusion.432), channel_id=1, replica_groups=mesh['dp'=8,'fsdp'=4] {'dp','fsdp'}, use_global_device_ids=true, to_apply=%region_22.23 | all-reduce | flops 2048 | bytes 16384 | tf_op jit(solution)/shard_map/psum | solution.py:84
  413.0 41.6 %all-reduce.21 = (f32[2,512]{1,0:T(2,128)S(1)}, f32[2,512]{1,0:T(2,128)S(1)}) all-reduce(f32[2,512]{1,0:T(2,128)S(1)} %fusion.427, f32[2,512]{1,0:T(2,128)S(1)} %fusion.428), channel_id=1, replica_groups=mesh['dp'=8,'fsdp'=4] {'dp','fsdp'}, use_global_device_ids=true, to_apply=%region_30.31 | all-reduce | flops 2048 | bytes 16384 | tf_op jit(solution)/shard_map/psum | solution.py:84
  475.7 40.6 %all-reduce.20 = (f32[2,768]{1,0:T(2,128)S(1)}, f32[2,768]{1,0:T(2,128)S(1)}, f32[2,256]{1,0:T(2,128)S(1)}, f32[2,256]{1,0:T(2,128)S(1)}) all-reduce(f32[2,768]{1,0:T(2,128)S(1)} %fusion.429, f32[2,768]{1,0:T(2,128)S(1)} %fusion.430, f32[2,256]{1,0:T(2,128)S(1)} %fusion.425, ...), channel_id=1, replica_groups=mesh['dp'=8,'fsdp'=4] {'dp','fsdp'}, use_global_device_ids=true, to_apply=%region_26.27 | all-reduce | flops 4096 | bytes 32768 | tf_op jit(solution)/shard_map/psum | solution.py:84
  550.2 40.5 %all-reduce.19 = (f32[2,256]{1,0:T(2,128)S(1)}, f32[2,256]{1,0:T(2,128)S(1)}) all-reduce(f32[2,256]{1,0:T(2,128)S(1)} %fusion.423, f32[2,256]{1,0:T(2,128)S(1)} %fusion.424), channel_id=1, replica_groups=mesh['dp'=8,'fsdp'=4] {'dp','fsdp'}, use_global_device_ids=true, to_apply=%region_40.41 | all-reduce | flops 1024 | bytes 8192 | tf_op jit(solution)/shard_map/psum | solution.py:96
  602.2 40.0 %all-reduce.18 = (f32[2,512]{1,0:T(2,128)S(1)}, f32[2,512]{1,0:T(2,128)S(1)}, f32[2,768]{1,0:T(2,128)S(1)}, f32[2,768]{1,0:T(2,128)S(1)}) all-reduce(f32[2,512]{1,0:T(2,128)S(1)} %fusion.421, f32[2,512]{1,0:T(2,128)S(1)} %fusion.422, f32[2,768]{1,0:T(2,128)S(1)} %fusion.419, ...), channel_id=1, replica_groups=mesh['dp'=8,'fsdp'=4] {'dp','fsdp'}, use_global_device_ids=true, to_apply=%region_44.45 | all-reduce | flops 5120 | bytes 40960 | tf_op jit(solution)/shard_map/psum | solution.py:96
  672.1 41.3 %all-reduce.17 = (f32[2,1536]{1,0:T(2,128)S(1)}, f32[2,1536]{1,0:T(2,128)S(1)}, f32[2,512]{1,0:T(2,128)S(1)}, f32[2,512]{1,0:T(2,128)S(1)}) all-reduce(f32[2,1536]{1,0:T(2,128)S(1)} %fusion.435, f32[2,1536]{1,0:T(2,128)S(1)} %fusion.436, f32[2,512]{1,0:T(2,128)S(1)} %fusion.417, ...), channel_id=1, replica_groups=mesh['dp'=8,'fsdp'=4] {'dp','fsdp'}, use_global_device_ids=true, to_apply=%region_11.12 | all-reduce | flops 8192 | bytes 65536 | tf_op jit(solution)/shard_map/psum | solution.py:84
  818.4 40.1 %all-reduce.16 = (f32[2,512]{1,0:T(2,128)S(1)}, f32[2,512]{1,0:T(2,128)S(1)}, f32[2,1536]{1,0:T(2,128)S(1)}, f32[2,1536]{1,0:T(2,128)S(1)}) all-reduce(f32[2,512]{1,0:T(2,128)S(1)} %fusion.415, f32[2,512]{1,0:T(2,128)S(1)} %fusion.416, f32[2,1536]{1,0:T(2,128)S(1)} %fusion.413, ...), channel_id=1, replica_groups=mesh['dp'=8,'fsdp'=4] {'dp','fsdp'}, use_global_device_ids=true, to_apply=%region_59.60 | all-reduce | flops 8192 | bytes 65536 | tf_op jit(solution)/shard_map/psum | solution.py:96
  941.8 42.8 %all-reduce.15 = (f32[2,512]{1,0:T(2,128)S(1)}, f32[2,512]{1,0:T(2,128)S(1)}) all-reduce(f32[2,512]{1,0:T(2,128)S(1)} %fusion.411, f32[2,512]{1,0:T(2,128)S(1)} %fusion.412), channel_id=1, replica_groups=mesh['dp'=8,'fsdp'=4] {'dp','fsdp'}, use_global_device_ids=true, to_apply=%region_67.68 | all-reduce | flops 2048 | bytes 16384 | tf_op jit(solution)/shard_map/psum | solution.py:96
  1013.5 41.9 %all-reduce.14 = (f32[2,512]{1,0:T(2,128)S(1)}, f32[2,512]{1,0:T(2,128)S(1)}) all-reduce(f32[2,512]{1,0:T(2,128)S(1)} %fusion.409, f32[2,512]{1,0:T(2,128)S(1)} %fusion.410), channel_id=1, replica_groups=mesh['dp'=8,'fsdp'=4] {'dp','fsdp'}, use_global_device_ids=true, to_apply=%region_71.72 | all-reduce | flops 2048 | bytes 16384 | tf_op jit(solution)/shard_map/psum | solution.py:96
  1150.7 65.3 %reduce-scatter.33.cloned.1.call-done = f32[288,512]{1,0:T(8,128)} async-done(((f32[2304,512]{1,0:T(8,128)}), f32[288,512]{1,0:T(8,128)}) %reduce-scatter.33.cloned.1.call-update) | async-done | bytes 589840 | tf_op jit(solution)/shard_map/reduce_scatter | solution.py:139
  1218.3 164.8 %reduce-scatter.43.cloned.1.call-done = f32[576,512]{1,0:T(8,128)} async-done(((f32[4608,512]{1,0:T(8,128)}), f32[576,512]{1,0:T(8,128)}) %reduce-scatter.43.cloned.1.call-update) | async-done | bytes 1179664 | tf_op jit(solution)/shard_map/reduce_scatter | solution.py:140
  1386.1 163.4 %reduce-scatter.41.cloned.1.call-done = f32[576,512]{1,0:T(8,128)} async-done(((f32[4608,512]{1,0:T(8,128)}), f32[576,512]{1,0:T(8,128)}) %reduce-scatter.41.cloned.1.call-update) | async-done | bytes 1179664 | tf_op jit(solution)/shard_map/reduce_scatter | solution.py:139
  1569.8 146.0 %reduce-scatter.37.cloned.1.call-done = f32[576,512]{1,0:T(8,128)} async-done(((f32[4608,512]{1,0:T(8,128)}), f32[576,512]{1,0:T(8,128)}) %reduce-scatter.37.cloned.1.call-update) | async-done | bytes 1179664 | tf_op jit(solution)/shard_map/reduce_scatter | solution.py:141
  1725.7 156.4 %reduce-scatter.35.cloned.1.call-done = f32[576,512]{1,0:T(8,128)} async-done(((f32[4608,512]{1,0:T(8,128)}), f32[576,512]{1,0:T(8,128)}) %reduce-scatter.35.cloned.1.call-update) | async-done | bytes 1179664 | tf_op jit(solution)/shard_map/reduce_scatter | solution.py:140
  1905.5 21.8 %reduce-scatter.55.cloned.1.call-done = bf16[384,64]{1,0:T(8,128)(2,1)} async-done(((bf16[1536,64]{1,0:T(8,128)(2,1)}), bf16[384,64]{1,0:T(8,128)(2,1)}) %reduce-scatter.55.cloned.1.call-update) | async-done | bytes 49168
  1952.2 21.5 %reduce-scatter.49.cloned.1.call-done = bf16[128,288]{1,0:T(8,128)(2,1)} async-done(((bf16[512,288]{1,0:T(8,128)(2,1)}), bf16[128,288]{1,0:T(8,128)(2,1)}) %reduce-scatter.49.cloned.1.call-update) | async-done | bytes 73744
  1975.4 23.2 %reduce-scatter.59.cloned.1.call-done = bf16[128,576]{1,0:T(8,128)(2,1)} async-done(((bf16[512,576]{1,0:T(8,128)(2,1)}), bf16[128,576]{1,0:T(8,128)(2,1)}) %reduce-scatter.59.cloned.1.call-update) | async-done | bytes 147472
  2000.4 23.2 %reduce-scatter.57.cloned.1.call-done = bf16[128,576]{1,0:T(8,128)(2,1)} async-done(((bf16[512,576]{1,0:T(8,128)(2,1)}), bf16[128,576]{1,0:T(8,128)(2,1)}) %reduce-scatter.57.cloned.1.call-update) | async-done | bytes 147472
  2025.4 23.2 %reduce-scatter.53.cloned.1.call-done = bf16[128,576]{1,0:T(8,128)(2,1)} async-done(((bf16[512,576]{1,0:T(8,128)(2,1)}), bf16[128,576]{1,0:T(8,128)(2,1)}) %reduce-scatter.53.cloned.1.call-update) | async-done | bytes 147472
  2050.4 23.2 %reduce-scatter.51.cloned.1.call-done = bf16[128,576]{1,0:T(8,128)(2,1)} async-done(((bf16[512,576]{1,0:T(8,128)(2,1)}), bf16[128,576]{1,0:T(8,128)(2,1)}) %reduce-scatter.51.cloned.1.call-update) | async-done | bytes 147472
  (899 shorter events, 699.3 us)
Async XLA Ops:
  7.2 103.9 %all-gather.9.cloned.1.call-start = ((), (), s32[]{:S(2)}) async-start(), calls=%async_computation.16 | async-start | bytes 2654208 | tf_op jit(solution)/shard_map/all_gather | solution.py:130
  16.4 153.5 %all-gather.11.cloned.1.call-start = ((), (), s32[]{:S(2)}) async-start(), calls=%async_computation.17 | async-start | bytes 5308416 | tf_op jit(solution)/shard_map/all_gather | solution.py:131
  25.2 212.5 %all-gather.15.cloned.1.call-start = ((), (), s32[]{:S(2)}) async-start(), calls=%async_computation.19 | async-start | bytes 5308416 | tf_op jit(solution)/shard_map/all_gather | solution.py:132
  33.4 301.1 %all-gather.17.cloned.1.call-start = ((), (), s32[]{:S(2)}) async-start(), calls=%async_computation.20 | async-start | bytes 5308416 | tf_op jit(solution)/shard_map/all_gather | solution.py:130
  41.7 357.7 %all-gather.19.cloned.1.call-start = ((), (), s32[]{:S(2)}) async-start(), calls=%async_computation.21 | async-start | bytes 5308416 | tf_op jit(solution)/shard_map/all_gather | solution.py:131
  49.9 412.6 %all-gather.21.cloned.1.call-start = ((), (), s32[]{:S(2)}) async-start(), calls=%async_computation.22 | async-start | bytes 2654208 | tf_op jit(solution)/shard_map/all_gather | solution.py:132
  57.1 608.3 %all-gather.13.cloned.1.call-start = ((), (), s32[]{:S(2)}) async-start(), calls=%async_computation.18 | async-start | bytes 1769472 | tf_op jit(solution)/shard_map/all_gather | solution.py:133
  63.3 1081.5 %reduce-scatter.47.cloned.1.call-start = ((), (), s32[]{:S(2)}) async-start(), calls=%async_computation.30 | async-start | bytes 1769472 | tf_op jit(solution)/shard_map/reduce_scatter | solution.py:142
  873.7 272.9 %reduce-scatter.39.cloned.1.call-start = ((), (), s32[]{:S(2)}) async-start(), calls=%async_computation.26 | async-start | bytes 3538944 | tf_op jit(solution)/shard_map/reduce_scatter | solution.py:142
  912.0 236.6 %reduce-scatter.45.cloned.1.call-start = ((), (), s32[]{:S(2)}) async-start(), calls=%async_computation.29 | async-start | bytes 5308416 | tf_op jit(solution)/shard_map/reduce_scatter | solution.py:141
  997.4 218.7 %reduce-scatter.33.cloned.1.call-start = ((), (), s32[]{:S(2)}) async-start(), calls=%async_computation.23 | async-start | bytes 5308416 | tf_op jit(solution)/shard_map/reduce_scatter | solution.py:139
  1070.3 312.8 %reduce-scatter.43.cloned.1.call-start = ((), (), s32[]{:S(2)}) async-start(), calls=%async_computation.28 | async-start | bytes 10616832 | tf_op jit(solution)/shard_map/reduce_scatter | solution.py:140
  1087.4 462.1 %reduce-scatter.41.cloned.1.call-start = ((), (), s32[]{:S(2)}) async-start(), calls=%async_computation.27 | async-start | bytes 10616832 | tf_op jit(solution)/shard_map/reduce_scatter | solution.py:139
  1104.7 611.0 %reduce-scatter.37.cloned.1.call-start = ((), (), s32[]{:S(2)}) async-start(), calls=%async_computation.25 | async-start | bytes 10616832 | tf_op jit(solution)/shard_map/reduce_scatter | solution.py:141
  1127.2 754.9 %reduce-scatter.35.cloned.1.call-start = ((), (), s32[]{:S(2)}) async-start(), calls=%async_computation.24 | async-start | bytes 10616832 | tf_op jit(solution)/shard_map/reduce_scatter | solution.py:140
  1144.7 759.3 %reduce-scatter.63.cloned.1.call-start = ((), (), s32[]{:S(2)}) async-start(), calls=%async_computation.38 | async-start | bytes 245760
  1146.5 780.8 %reduce-scatter.55.cloned.1.call-start = ((), (), s32[]{:S(2)}) async-start(), calls=%async_computation.34 | async-start | bytes 491520
  1148.6 801.8 %reduce-scatter.61.cloned.1.call-start = ((), (), s32[]{:S(2)}) async-start(), calls=%async_computation.37 | async-start | bytes 409600
  1150.7 823.0 %reduce-scatter.49.cloned.1.call-start = ((), (), s32[]{:S(2)}) async-start(), calls=%async_computation.31 | async-start | bytes 491520
  1218.2 167.7 %copy-start.192 = (f32[2,512]{1,0:T(2,128)S(1)}, f32[2,512]{1,0:T(2,128)}, u32[]{:S(2)}) copy-start(f32[2,512]{1,0:T(2,128)} %copy-done.191) | copy-start | bytes 12292
  1218.2 780.4 %reduce-scatter.59.cloned.1.call-start = ((), (), s32[]{:S(2)}) async-start(), calls=%async_computation.36 | async-start | bytes 819200
  1385.5 638.1 %reduce-scatter.57.cloned.1.call-start = ((), (), s32[]{:S(2)}) async-start(), calls=%async_computation.35 | async-start | bytes 819200
  1552.0 496.7 %reduce-scatter.53.cloned.1.call-start = ((), (), s32[]{:S(2)}) async-start(), calls=%async_computation.33 | async-start | bytes 819200
  1720.1 353.5 %reduce-scatter.51.cloned.1.call-start = ((), (), s32[]{:S(2)}) async-start(), calls=%async_computation.32 | async-start | bytes 819200
  (218 other events, 4806.5 us)
Sparse Core Ops, SparseCore 0:
  16.5 52.4 all-gather.8
  71.2 85.5 all-gather.10
  158.9 78.7 all-gather.14
  239.7 78.9 all-gather.16
  320.7 78.6 all-gather.18
  402.0 50.2 all-gather.20
  454.5 44.0 all-gather.12
  873.9 64.7 reduce-scatter.46
  942.7 74.6 reduce-scatter.38
  1021.3 95.4 reduce-scatter.44
  1120.9 95.1 reduce-scatter.32
  1219.9 163.0 reduce-scatter.42
  1387.1 162.3 reduce-scatter.40
  1553.4 162.3 reduce-scatter.36
  1719.7 162.4 reduce-scatter.34
  1885.1 18.8 reduce-scatter.62
  1906.5 20.8 reduce-scatter.54
  1929.8 20.4 reduce-scatter.60
  1952.9 20.8 reduce-scatter.48
  1976.1 22.4 reduce-scatter.58
  2001.1 22.4 reduce-scatter.56
  2026.1 22.4 reduce-scatter.52
  2051.1 22.4 reduce-scatter.50
where the time goes:
time: 2090 us; the launch traced here: 2080 us
  waiting for transfers between devices  872 us (42%)
  blocking collectives  593 us (28%)
  matrix products  239 us (11%)
  local copies, waits for them, and re-layouts  199 us (10%)
  other arithmetic  160 us (8%)
    reduce_scatter x2, waiting for transfers between devices, reduce_section(): lax.psum_scatter(second, 'dp', scatter_dimension=0, tiled=True)  321 us
    psum x6, blocking collectives, norm_layer(): lax.psum((domain_sums(onehot, shaped), domain_sums(onehot, shaped * shape...  250 us
    reduce_scatter x2, waiting for transfers between devices, reduce_section(): lax.psum_scatter(first, 'dp', scatter_dimension=0, tiled=True)  229 us
    psum x5, blocking collectives, norm_back(): lax.psum((domain_sums(onehot, shaped), domain_sums(onehot, shaped * norme...  205 us
    unnamed x31, waiting for transfers between devices  172 us
    reduce_scatter x2, waiting for transfers between devices, reduce_section(): lax.psum_scatter(third, 'dp', scatter_dimension=0, tiled=True)  146 us
    dot_general x54, matrix products, conv_kernel_grad(): lax.dot_general(window.reshape(-1, chans_in), upstream_flat, (((0,), (0,)...  86.8 us
    dot_general x54, matrix products, conv_apply(): jnp.dot(window.reshape(-1, chans_in), kernel[offset * chans_in:(offset +...  58.3 us
  transfers between devices with their start and end apart: 23, of which 15 were waited for; matrix products, arithmetic and copies ran while one was open for 21% of the time, Pallas kernels for 0%

commit v1 on v0

v1 whole, which is shorter than its diff:
```python
import functools

import jax
import jax.numpy as jnp
from jax import lax
from jax.experimental import pallas as pl
from jax.experimental.pallas import tpu as pltpu
from jax.sharding import PartitionSpec as P

C_IN = 256
C_MID = 512
C_DEC = 256
TASKS = 3
EPS = 1e-05
LANES = 128
F32 = jnp.float32
BF16 = jnp.bfloat16
VMEM_LIMIT = 56 * 1024 * 1024


def params(grid_dims=0):
    return pltpu.CompilerParams(
        vmem_limit_bytes=VMEM_LIMIT,
        dimension_semantics=("arbitrary",) * grid_dims if grid_dims else None,
    )


def whole(shape):
    zeros = (0,) * len(shape)
    return pl.BlockSpec(shape, lambda *_: zeros)


SCALARS = pl.BlockSpec(memory_space=pltpu.SMEM)


def sds(shape, dtype):
    return jax.ShapeDtypeStruct(shape, dtype)


def sigmoid(v):
    return 0.5 * jnp.tanh(0.5 * v) + 0.5


def frame_tables(stats, domain_at, counts):
    first = domain_at == 0
    share = jnp.where(first, 1.0 / counts[0], 1.0 / counts[1])
    average = jnp.where(first, stats[0:1], stats[1:2]) * share
    square = jnp.where(first, stats[2:3], stats[3:4]) * share
    return average, lax.rsqrt(square - average * average + EPS)


def grad_tables(sums, domain_at, counts):
    first = domain_at == 0
    share = jnp.where(first, 1.0 / counts[0], 1.0 / counts[1])
    return (
        jnp.where(first, sums[0:1], sums[1:2]) * share,
        jnp.where(first, sums[2:3], sums[3:4]) * share,
    )


def by_domain(first, second, domain_ref):
    rows = []
    for per_frame in (first, second):
        for d in (0, 1):
            total = None
            for f, value in enumerate(per_frame):
                term = jnp.where(domain_ref[f] == d, value, jnp.zeros_like(value))
                total = term if total is None else total + term
            rows.append(total)
    return jnp.concatenate(rows, 0)


def fold(x):
    return jnp.sum(x.reshape(-1, 8, x.shape[-1]), 0)


def put_windows(win_ref, f, row, value, cols):
    col = lax.broadcasted_iota(jnp.int32, value.shape, 0)
    left = jnp.where(col == 0, 0.0, pltpu.roll(value, 1, 0))
    right = jnp.where(col == cols - 1, 0.0, pltpu.roll(value, cols - 1, 0))
    win_ref[0, f, row + 1] = left.astype(BF16)
    win_ref[1, f, row + 1] = value.astype(BF16)
    win_ref[2, f, row + 1] = right.astype(BF16)


def clear_edges(win_ref, rows):
    shape = win_ref.shape
    for b in range(3):
        for f in range(shape[1]):
            win_ref[b, f, 0] = jnp.zeros(shape[3:], BF16)
            win_ref[b, f, rows + 1] = jnp.zeros(shape[3:], BF16)


def window(win_ref, b, row_at, rows):
    part = win_ref[b, :, pl.ds(row_at, rows)]
    return part.reshape(-1, part.shape[-1])


def column_sums(ref, f, pixels, lanes, step=64):
    def add(i, carry):
        part = ref[pl.ds(f * pixels + i * step, step), lanes]
        return carry[0] + fold(part), carry[1] + fold(part * part)

    width = lanes.stop - lanes.start
    zero = jnp.zeros((8, width), F32)
    one, two = lax.fori_loop(0, pixels // step, add, (zero, zero), unroll=2)
    return jnp.sum(one, 0, keepdims=True), jnp.sum(two, 0, keepdims=True)


class Pieces:
    def __init__(self, member, parts, me, sources):
        self.member, self.parts, self.me, self.sources = member, parts, me, sources
        self.shape = member.shape


def span(start, size):
    return pl.ds(start if isinstance(start, int) else pl.multiple_of(start, size & -size), size)


def fetch(member, parts, me_ref, sources, dst_ref, sem):
    me = me_ref[0]
    for (first, size, masks), src in zip(parts, sources):
        for q in range(src.shape[0]):
            d = q if masks is None else me ^ masks[q]
            for at, row, col in member.spots(d >> 2, d & 3):
                low, high = max(at, first), min(at + member.vr, first + size)
                if low < high:
                    pltpu.make_async_copy(
                        src.at[q, pl.ds(low - first, high - low)],
                        dst_ref.at[span(row + (low - at), high - low), span(col, LANES)],
                        sem,
                    ).start()


def arrived(ref, sem):
    pltpu.make_async_copy(ref, ref, sem).wait()


def forward_kernel(geom, normed, pieces, *refs):
    frames, rows, cols, counts = geom
    pixels = rows * cols
    refs = list(refs)
    domain_ref = refs.pop(0)
    source_ref = refs.pop(0)
    if normed:
        stats_ref, gain_ref, bias_ref = refs.pop(0), refs.pop(0), refs.pop(0)
    if pieces:
        me_ref = refs.pop(0)
        sources = [refs.pop(0) for _ in pieces[1]]
    else:
        kernel_ref = refs.pop(0)
    out_ref = refs.pop(0)
    sums_ref = refs.pop(0)
    act_ref = refs.pop(0) if normed else None
    if pieces:
        matrix_ref = refs.pop(0)
    win_ref = refs.pop(0)
    if pieces:
        held_ref, sem = refs.pop(0), refs.pop(0)
    step = pl.program_id(0)
    chans = win_ref.shape[-1]

    @pl.when(step == 0)
    def _():
        if pieces:
            fetch(*pieces, me_ref, sources, held_ref, sem.at[0])
        clear_edges(win_ref, rows)
        for f in range(frames):
            if normed:
                average, inverse = frame_tables(stats_ref[...], domain_ref[f], counts)
                scale = inverse * gain_ref[...]
                shift = bias_ref[...] - average * scale

            def one_row(r, _):
                at = pl.multiple_of(f * pixels + r * cols, cols)
                value = source_ref[pl.ds(at, cols), :].astype(F32)
                if normed:
                    act = value * scale + shift
                    value = act * sigmoid(act)
                    act_ref[pl.ds(at, cols), :] = value.astype(BF16)
                put_windows(win_ref, f, r, value, cols)
                return 0

            lax.fori_loop(0, rows, one_row, 0, unroll=2)
        if pieces:
            arrived(held_ref, sem.at[0])
            pltpu.make_async_copy(held_ref, matrix_ref, sem.at[1]).start()

    source = jnp.concatenate([window(win_ref, b, step, rows) for b in range(3)], 1)
    if pieces:
        matrix = held_ref[pl.ds(pl.multiple_of(step * 3 * chans, 3 * chans), 3 * chans), :]
    else:
        matrix = kernel_ref[...]
    part = jnp.dot(source, matrix, preferred_element_type=F32)

    @pl.when(step == 0)
    def _():
        out_ref[...] = part

    @pl.when(step > 0)
    def _():
        out_ref[...] += part

    @pl.when(step == 2)
    def _():
        for lane in range(0, out_ref.shape[-1], 256):
            lanes = slice(lane, lane + 256)
            pairs = [column_sums(out_ref, f, pixels, lanes) for f in range(frames)]
            sums_ref[:, lanes] = by_domain([p[0] for p in pairs], [p[1] for p in pairs], domain_ref)
        if pieces:
            pltpu.make_async_copy(held_ref, matrix_ref, sem.at[1]).wait()


ANYWHERE = pl.BlockSpec(memory_space=pl.ANY)


def forward_layer(geom, domain, source, kernel, norm=None):
    frames, rows, cols, _ = geom
    pix, chans = source.shape
    width = kernel.shape[1]
    pieces = isinstance(kernel, Pieces)
    args, specs = [domain, source], [SCALARS, whole(source.shape)]
    if norm is not None:
        args += list(norm)
        specs += [whole(x.shape) for x in norm]
    if pieces:
        args += [kernel.me, *kernel.sources]
        specs += [SCALARS] + [ANYWHERE] * len(kernel.sources)
    else:
        args.append(kernel)
        specs.append(pl.BlockSpec((3 * chans, width), lambda a: (a, 0)))
    outs, out_specs = [sds((pix, width), F32)], [whole((pix, width))]
    outs.append(sds((4, width), F32))
    out_specs.append(whole((4, width)))
    if norm is not None:
        outs.append(sds((pix, chans), BF16))
        out_specs.append(whole((pix, chans)))
    scratch = [pltpu.VMEM((3, frames, rows + 2, cols, chans), BF16)]
    if pieces:
        outs.append(sds(kernel.shape, BF16))
        out_specs.append(ANYWHERE)
        scratch += [pltpu.VMEM(kernel.shape, BF16), pltpu.SemaphoreType.DMA((2,))]
    size = kernel.shape[0] * kernel.shape[1]
    return pl.pallas_call(
        functools.partial(forward_kernel, geom, norm is not None, (kernel.member, kernel.parts) if pieces else None),
        grid=(3,),
        in_specs=specs,
        out_specs=out_specs,
        out_shape=outs,
        scratch_shapes=scratch,
        compiler_params=params(1),
        cost_estimate=pl.CostEstimate(flops=2 * pix * size, bytes_accessed=size * 2 + pix * 4096, transcendentals=0),
    )(*args)


def pair_sum(x, cols):
    even = lax.broadcasted_iota(jnp.int32, x.shape, 0) % 2 == 0
    return x + jnp.where(even, pltpu.roll(x, cols - 1, 0), pltpu.roll(x, 1, 0))


def softmax_window(top, cols):
    exps = [jnp.exp(t) for t in top]
    share = 1.0 / pair_sum(exps[0] + exps[1], cols)
    return [e * share for e in exps]


def spread_cols(scr_ref, x):
    half = x.shape[0]
    scr_ref[pl.ds(0, half, stride=2), :] = x
    scr_ref[pl.ds(1, half, stride=2), :] = x
    return scr_ref[...]


def top_rows(top_ref, at, cols, lanes, scale, shift):
    top = []
    for a in at:
        act = top_ref[pl.ds(a, cols), lanes] * scale + shift
        top.append(act * sigmoid(act))
    return top


def pool_kernel(geom, domain_ref, top_ref, top_st, gain_t, bias_t, un_ref):
    frames, rows, cols, counts = geom
    pixels = rows * cols
    for f in range(frames):
        for lane in range(0, top_ref.shape[-1], LANES):
            lanes = slice(lane, lane + LANES)
            average, inverse = frame_tables(top_st[:, lanes], domain_ref[f], counts)
            scale = inverse * gain_t[:, lanes]
            shift = bias_t[:, lanes] - average * scale

            def one(i, _):
                at = [pl.multiple_of(f * pixels + (2 * i + h) * cols, cols) for h in (0, 1)]
                top = top_rows(top_ref, at, cols, lanes, scale, shift)
                weight = softmax_window(top, cols)
                pooled = pair_sum(weight[0] * top[0] + weight[1] * top[1], cols)
                for h in (0, 1):
                    un_ref[pl.ds(at[h], cols), lanes] = (weight[h] * pooled).astype(BF16)
                return 0

            lax.fori_loop(0, rows // 2, one, 0, unroll=2)


def pool_layer(geom, domain, top, top_st, gain_t, bias_t):
    pix, chans = top.shape
    args = (domain, top, top_st, gain_t, bias_t)
    return pl.pallas_call(
        functools.partial(pool_kernel, geom),
        in_specs=[SCALARS] + [whole(x.shape) for x in args[1:]],
        out_specs=whole((pix, chans)),
        out_shape=sds((pix, chans), BF16),
        compiler_params=params(),
        cost_estimate=pl.CostEstimate(flops=pix * chans * 20, bytes_accessed=pix * chans * 6, transcendentals=pix * chans * 2),
    )(*args)


def task_kernel(geom, domain_ref, top_ref, top_st, wide_ref, wide_st, gain_t, bias_t, gain_w, bias_w, task_ref, scr_ref):
    frames, rows, cols, counts = geom
    pixels = rows * cols
    chans = top_ref.shape[-1]
    for f in range(frames):
        for lane in range(0, chans, LANES):
            lanes = slice(lane, lane + LANES)

            def table(st, gain, bias, sl):
                average, inverse = frame_tables(st[:, sl], domain_ref[f], counts)
                scale = inverse * gain[:, sl]
                return scale, bias[:, sl] - average * scale

            t_scale, t_shift = table(top_st, gain_t, bias_t, lanes)
            wide = []
            for k in range(TASKS):
                sl = slice(k * chans + lane, k * chans + lane + LANES)
                wide.append((sl, *table(wide_st, gain_w, bias_w, sl)))

            def one(i, _):
                at = [pl.multiple_of(f * pixels + (2 * i + h) * cols, cols) for h in (0, 1)]
                top = top_rows(top_ref, at, cols, lanes, t_scale, t_shift)
                weight = softmax_window(top, cols)
                held = [w * t for w, t in zip(weight, top)]
                for k in range(TASKS):
                    sl, scale, shift = wide[k]
                    total = None
                    for h in (0, 1):
                        mask = sigmoid(wide_ref[pl.ds(at[h], cols), sl] * scale + shift)
                        term = mask * held[h]
                        total = term if total is None else total + term
                    scr_ref[k] = total
                    even = scr_ref[k, pl.ds(0, cols // 2, stride=2), :]
                    odd = scr_ref[k, pl.ds(1, cols // 2, stride=2), :]
                    task_ref[f, i, k, :, lanes] = even + odd
                return 0

            lax.fori_loop(0, rows // 2, one, 0, unroll=2)


def task_layer(geom, domain, top, top_st, wide, wide_st, gain_t, bias_t, gain_w, bias_w):
    frames, rows, cols, _ = geom
    pix, chans = top.shape
    task_shape = (frames, rows // 2, TASKS, cols // 2, chans)
    args = (domain, top, top_st, wide, wide_st, gain_t, bias_t, gain_w, bias_w)
    return pl.pallas_call(
        functools.partial(task_kernel, geom),
        in_specs=[SCALARS] + [whole(x.shape) for x in args[1:]],
        out_specs=whole(task_shape),
        out_shape=sds(task_shape, F32),
        scratch_shapes=[pltpu.VMEM((TASKS, cols, LANES), F32)],
        compiler_params=params(),
        cost_estimate=pl.CostEstimate(flops=pix * chans * 60, bytes_accessed=pix * chans * 28, transcendentals=pix * chans * 5),
    )(*args)


def pool_early_kernel(geom, domain_ref, top_ref, top_st, wide_ref, wide_st, gain_t, bias_t, gain_w, bias_w, cot_ref,
                      mix_ref, gw_ref, sums_ref, scr_ref):
    frames, rows, cols, counts = geom
    pixels = rows * cols
    chans = top_ref.shape[-1]
    for lane in range(0, chans, LANES):
        lanes = slice(lane, lane + LANES)
        sums = []
        for f in range(frames):
            average, inverse = frame_tables(top_st[:, lanes], domain_ref[f], counts)
            t_scale = inverse * gain_t[:, lanes]
            t_shift = bias_t[:, lanes] - average * t_scale
            wide = []
            for k in range(TASKS):
                sl = slice(k * chans + lane, k * chans + lane + LANES)
                wide.append((sl, *frame_tables(wide_st[:, sl], domain_ref[f], counts)))

            def one(i, carry):
                at = [pl.multiple_of(f * pixels + (2 * i + h) * cols, cols) for h in (0, 1)]
                top = []
                for h in (0, 1):
                    act = top_ref[pl.ds(at[h], cols), lanes] * t_scale + t_shift
                    top.append(act * sigmoid(act))
                weight = softmax_window(top, cols)
                held = [w * t for w, t in zip(weight, top)]
                mix = [None, None]
                new = []
                for k in range(TASKS):
                    sl, average, inverse = wide[k]
                    cot = spread_cols(scr_ref, cot_ref[f, i, k, :, lanes].astype(F32))
                    one_sum, two_sum = carry[2 * k], carry[2 * k + 1]
                    for h in (0, 1):
                        xhat = (wide_ref[pl.ds(at[h], cols), sl] - average) * inverse
                        mask = sigmoid(xhat * gain_w[:, sl] + bias_w[:, sl])
                        part = cot * mask
                        mix[h] = part if mix[h] is None else mix[h] + part
                        g = part * held[h] * (1.0 - mask)
                        gw_ref[pl.ds(at[h], cols), sl] = g
                        one_sum = one_sum + fold(g)
                        two_sum = two_sum + fold(g * xhat)
                    new += [one_sum, two_sum]
                for h in (0, 1):
                    mix_ref[pl.ds(at[h], cols), lanes] = mix[h]
                return tuple(new)

            zero = jnp.zeros((8, LANES), F32)
            sums.append(lax.fori_loop(0, rows // 2, one, (zero,) * (2 * TASKS)))
        for k in range(TASKS):
            first = [jnp.sum(s[2 * k], 0, keepdims=True) for s in sums]
            second = [jnp.sum(s[2 * k + 1], 0, keepdims=True) for s in sums]
            sl = slice(k * chans + lane, k * chans + lane + LANES)
            sums_ref[:, sl] = by_domain(first, second, domain_ref)


def pool_early(geom, domain, top, top_st, wide, wide_st, gain_t, bias_t, gain_w, bias_w, cot):
    _, _, cols, _ = geom
    pix, chans = top.shape
    args = (domain, top, top_st, wide, wide_st, gain_t, bias_t, gain_w, bias_w, cot)
    outs = [sds((pix, chans), F32), sds((pix, TASKS * chans), F32), sds((4, TASKS * chans), F32)]
    return pl.pallas_call(
        functools.partial(pool_early_kernel, geom),
        in_specs=[SCALARS] + [whole(x.shape) for x in args[1:]],
        out_specs=[whole(o.shape) for o in outs],
        out_shape=outs,
        scratch_shapes=[pltpu.VMEM((cols, LANES), F32)],
        compiler_params=params(),
        cost_estimate=pl.CostEstimate(flops=pix * chans * 90, bytes_accessed=pix * chans * 40, transcendentals=pix * chans * 5),
    )(*args)


def head_kernel(geom, domain_ref, bot_ref, bot_st, gate_ref, gate_st, gain_b, bias_b, gain_g, bias_g, cot_ref,
                maps_ref, gb_ref, gg_ref, sums_ref):
    frames, rows, cols, counts = geom
    pixels = rows * cols
    chans = bot_ref.shape[-1]
    for lane in range(0, chans, LANES):
        lanes = slice(lane, lane + LANES)
        sums = []
        for f in range(frames):
            b_mean, b_inv = frame_tables(bot_st[:, lanes], domain_ref[f], counts)
            gate = []
            for k in range(TASKS):
                sl = slice(k * chans + lane, k * chans + lane + LANES)
                gate.append((sl, *frame_tables(gate_st[:, sl], domain_ref[f], counts)))

            def one(r, carry):
                at = pl.multiple_of(f * pixels + r * cols, cols)
                b_hat = (bot_ref[pl.ds(at, cols), lanes] - b_mean) * b_inv
                act = b_hat * gain_b[:, lanes] + bias_b[:, lanes]
                s = sigmoid(act)
                bottom = act * s
                back = None
                new = []
                for k in range(TASKS):
                    sl, mean, inv = gate[k]
                    xhat = (gate_ref[pl.ds(at, cols), sl] - mean) * inv
                    value = sigmoid(xhat * gain_g[:, sl] + bias_g[:, sl])
                    maps_ref[k, pl.ds(at, cols), lanes] = value * bottom
                    cot = cot_ref[k, pl.ds(at, cols), lanes].astype(F32)
                    part = cot * value
                    back = part if back is None else back + part
                    g = part * bottom * (1.0 - value)
                    gg_ref[pl.ds(at, cols), sl] = g
                    new += [carry[2 * k] + fold(g), carry[2 * k + 1] + fold(g * xhat)]
                g = back * (s * (1.0 + act * (1.0 - s)))
                gb_ref[pl.ds(at, cols), lanes] = g
                new += [carry[-2] + fold(g), carry[-1] + fold(g * b_hat)]
                return tuple(new)

            zero = jnp.zeros((8, LANES), F32)
            sums.append(lax.fori_loop(0, rows, one, (zero,) * (2 * TASKS + 2), unroll=2))
        for k in range(TASKS + 1):
            first = [jnp.sum(s[2 * k], 0, keepdims=True) for s in sums]
            second = [jnp.sum(s[2 * k + 1], 0, keepdims=True) for s in sums]
            at = chans + k * chans + lane if k < TASKS else lane
            sums_ref[:, at : at + LANES] = by_domain(first, second, domain_ref)


def head_layer(geom, domain, bot, bot_st, gate, gate_st, gain_b, bias_b, gain_g, bias_g, cot):
    pix, chans = bot.shape
    args = (domain, bot, bot_st, gate, gate_st, gain_b, bias_b, gain_g, bias_g, cot)
    outs = [sds((TASKS, pix, chans), F32), sds((pix, chans), F32), sds((pix, TASKS * chans), F32),
            sds((4, (TASKS + 1) * chans), F32)]
    return pl.pallas_call(
        functools.partial(head_kernel, geom),
        in_specs=[SCALARS] + [whole(x.shape) for x in args[1:]],
        out_specs=[whole(o.shape) for o in outs],
        out_shape=outs,
        compiler_params=params(),
        cost_estimate=pl.CostEstimate(flops=pix * chans * 80, bytes_accessed=pix * chans * 44, transcendentals=pix * chans * 4),
    )(*args)


def norm_back_rows(g, pre, tables):
    mean, inv, scale, g_mean, g_cross = tables
    xhat = (pre - mean) * inv
    return scale * (g - g_mean - xhat * g_cross)


def back_tables(stats_ref, sums_ref, gain_ref, domain_at, counts):
    mean, inv = frame_tables(stats_ref[...], domain_at, counts)
    g_mean, g_cross = grad_tables(sums_ref[...], domain_at, counts)
    return mean, inv, inv * gain_ref[...], g_mean, g_cross


def backward_kernel(geom, added, epilogue, *refs):
    frames, rows, cols, counts = geom
    pixels = rows * cols
    refs = list(refs)
    domain_ref = refs.pop(0)
    g_ref, pre_ref, st_ref, sm_ref, gain_ref = (refs.pop(0) for _ in range(5))
    kernel_ref = refs.pop(0)
    add_ref = refs.pop(0) if added else None
    if epilogue in ("silu", "pool"):
        lpre_ref, lst_ref, lgain_ref, lbias_ref = (refs.pop(0) for _ in range(4))
    if epilogue == "pool":
        mix_ref = refs.pop(0)
    win_ref = refs.pop(0)
    out_ref = refs.pop(0)
    if epilogue != "none":
        sums_ref = refs.pop(0)
    step = pl.program_id(0)
    chans = kernel_ref.shape[0] // 3

    @pl.when(step == 0)
    def _():
        clear_edges(win_ref, rows)
        for f in range(frames):
            tables = back_tables(st_ref, sm_ref, gain_ref, domain_ref[f], counts)

            def one_row(r, _):
                at = pl.multiple_of(f * pixels + r * cols, cols)
                low = norm_back_rows(g_ref[pl.ds(at, cols), :], pre_ref[pl.ds(at, cols), :], tables)
                put_windows(win_ref, f, r, low, cols)
                return 0

            lax.fori_loop(0, rows, one_row, 0, unroll=2)

    source = jnp.concatenate([window(win_ref, 2 - b, 2 - step, rows) for b in range(3)], 1)
    weight = jnp.concatenate([kernel_ref[b * chans : (b + 1) * chans, :] for b in range(3)], 1)
    nt = (((1,), (1,)), ((), ()))
    part = lax.dot_general(source, weight, nt, preferred_element_type=F32)

    @pl.when(step == 0)
    def _():
        out_ref[...] = part + add_ref[...] if added else part

    @pl.when(step > 0)
    def _():
        out_ref[...] += part

    if epilogue == "none":
        return

    @pl.when(step == 2)
    def _():
        for lane in range(0, chans, LANES):
            lanes = slice(lane, lane + LANES)
            sums = []
            for f in range(frames):
                mean, inv = frame_tables(lst_ref[:, lanes], domain_ref[f], counts)

                def slope(at):
                    xhat = (lpre_ref[pl.ds(at, cols), lanes] - mean) * inv
                    act = xhat * lgain_ref[:, lanes] + lbias_ref[:, lanes]
                    s = sigmoid(act)
                    return xhat, act * s, s * (1.0 + act * (1.0 - s))

                def finish(at, g, xhat, carry):
                    out_ref[pl.ds(at, cols), lanes] = g
                    return carry[0] + fold(g), carry[1] + fold(g * xhat)

                def one_row(r, carry):
                    at = pl.multiple_of(f * pixels + r * cols, cols)
                    xhat, _, steep = slope(at)
                    return finish(at, out_ref[pl.ds(at, cols), lanes] * steep, xhat, carry)

                def one_pair(i, carry):
                    at = [pl.multiple_of(f * pixels + (2 * i + h) * cols, cols) for h in (0, 1)]
                    xhat, top, steep = zip(*(slope(a) for a in at))
                    weight = softmax_window(top, cols)
                    up = [out_ref[pl.ds(a, cols), lanes] for a in at]
                    mix = [mix_ref[pl.ds(a, cols), lanes] for a in at]
                    pooled = pair_sum(weight[0] * top[0] + weight[1] * top[1], cols)
                    d_pool = pair_sum(weight[0] * up[0] + weight[1] * up[1], cols)
                    flow = [m + d_pool for m in mix]
                    d_w = [u * pooled + fl * t for u, fl, t in zip(up, flow, top)]
                    centre = pair_sum(weight[0] * d_w[0] + weight[1] * d_w[1], cols)
                    for h in (0, 1):
                        d_top = weight[h] * (flow[h] + d_w[h] - centre)
                        carry = finish(at[h], d_top * steep[h], xhat[h], carry)
                    return carry

                zero = jnp.zeros((8, LANES), F32)
                if epilogue == "silu":
                    sums.append(lax.fori_loop(0, rows, one_row, (zero, zero), unroll=2))
                else:
                    sums.append(lax.fori_loop(0, rows // 2, one_pair, (zero, zero)))
            sums_ref[:, lanes] = by_domain(
                [jnp.sum(s[0], 0, keepdims=True) for s in sums],
                [jnp.sum(s[1], 0, keepdims=True) for s in sums],
                domain_ref,
            )


def backward_layer(geom, domain, top, kernel, added=None, lower=None, mix=None):
    frames, rows, cols, _ = geom
    pix, width = top[0].shape
    chans = kernel.shape[0] // 9
    args = [domain, *top, kernel]
    specs = [SCALARS] + [whole(x.shape) for x in top] + [pl.BlockSpec((3 * chans, width), lambda a: (a, 0))]
    win = (3, frames, rows + 2, cols, width)
    outs = [sds(win, BF16), sds((pix, chans), F32)]
    extra = [] if added is None else [added]
    epilogue = "none"
    if lower is not None:
        epilogue = "silu" if mix is None else "pool"
        extra += list(lower) + ([] if mix is None else [mix])
        outs.append(sds((4, chans), F32))
    return pl.pallas_call(
        functools.partial(backward_kernel, geom, added is not None, epilogue),
        grid=(3,),
        in_specs=specs + [whole(x.shape) for x in extra],
        out_specs=[whole(o.shape) for o in outs],
        out_shape=outs,
        compiler_params=params(1),
        cost_estimate=pl.CostEstimate(flops=2 * pix * kernel.size, bytes_accessed=kernel.size * 2 + pix * 10240, transcendentals=0),
    )(*args, *extra)


class Member:
    def __init__(self, at, shape, dp, fsdp, split=False):
        self.at, self.shape, self.split = at, shape, split
        self.vr = shape[0] // dp // (2 if split else 1)
        self.blocks = shape[1] // fsdp * (2 if split else 1) // LANES
        self.rows = self.vr * self.blocks

    def spots(self, i, j):
        if self.split:
            row, col = i * 2 * self.vr + (j & 1) * self.vr, (j >> 1) * self.blocks * LANES
        else:
            row, col = i * self.vr, j * self.blocks * LANES
        for k in range(self.blocks):
            yield self.at + k * self.vr, row, col + k * LANES


def collect_kernel(member, parts, me_ref, *refs):
    out_ref, sem = refs[-2:]
    fetch(member, parts, me_ref, refs[:-2], out_ref, sem)
    arrived(out_ref, sem)


def collect(pieces):
    return pl.pallas_call(
        functools.partial(collect_kernel, pieces.member, pieces.parts),
        in_specs=[SCALARS] + [ANYWHERE] * len(pieces.sources),
        out_specs=whole(pieces.shape),
        out_shape=sds(pieces.shape, BF16),
        scratch_shapes=[pltpu.SemaphoreType.DMA],
        grid=(1,),
        compiler_params=params(1),
        cost_estimate=pl.CostEstimate(flops=0, bytes_accessed=4 * pieces.shape[0] * pieces.shape[1], transcendentals=0),
    )(pieces.me, *pieces.sources)


def weight_parts(geom, step, act_ref, low_ref, tr_ref):
    rows = geom[1]

    @pl.when(step == 0)
    def _():
        tr_ref[...] = act_ref[...].astype(F32).T.astype(BF16)

    if len(low_ref.shape) == 5:
        for b in range(3):
            yield jnp.dot(tr_ref[...], window(low_ref, 2 - b, 2 - step, rows), preferred_element_type=F32)
    else:
        yield jnp.dot(tr_ref[...], low_ref[...], preferred_element_type=F32)


def weight_kernel(geom, act_ref, low_ref, out_ref, tr_ref):
    chans = tr_ref.shape[0]
    for b, part in enumerate(weight_parts(geom, pl.program_id(0), act_ref, low_ref, tr_ref)):
        out_ref[b * chans : (b + 1) * chans, :] = part.astype(BF16)


def weight_layer(geom, act, low):
    pix, chans = act.shape
    win = low.ndim == 5
    width = low.shape[-1]
    steps = 3 if win else 1
    out = sds((9 * chans if win else chans, width), BF16)
    return pl.pallas_call(
        functools.partial(weight_kernel, geom),
        grid=(steps,),
        in_specs=[whole(act.shape), whole(low.shape)],
        out_specs=pl.BlockSpec((out.shape[0] // steps, width), lambda a: (a, 0)),
        out_shape=out,
        scratch_shapes=[pltpu.VMEM((chans, pix), BF16)],
        compiler_params=params(1),
        cost_estimate=pl.CostEstimate(flops=2 * pix * out.size, bytes_accessed=out.size * 2 + pix * 4096, transcendentals=0),
    )(act, low)


def weight_blocks_kernel(geom, member, steps, far, aliased, *refs):
    refs = list(refs)
    me_ref, act_ref, low_ref = (refs.pop(0) for _ in range(3))
    if aliased:
        refs.pop(0)
    outs = [refs.pop(0) for _ in range(3 if far else 1)]
    scr_ref, tr_ref, sem = refs
    step = pl.program_id(0)
    chans = tr_ref.shape[0]
    for b, part in enumerate(weight_parts(geom, step, act_ref, low_ref, tr_ref)):
        scr_ref[pl.ds(pl.multiple_of(step * 3 * chans, chans) + b * chans, chans), :] = part.astype(BF16)

    def copies(i):
        if not far:
            for j in range(4):
                for at, row, col in member.spots(i, j):
                    yield scr_ref.at[pl.ds(row, member.vr), pl.ds(col, LANES)], outs[0].at[i * 4 + j, pl.ds(at, member.vr)]
            return
        me = me_ref[0]
        e = i ^ (me >> 2)
        q = ((e & 1) << 2) | (e & 2) | (e >> 2)
        for jd in range(4):
            dst = outs[2].at[jd >> 1, q] if jd & 1 else outs[jd >> 1].at[q]
            for at, row, col in member.spots(i, (me & 3) ^ jd):
                yield scr_ref.at[span(row, member.vr), span(col, LANES)], dst.at[pl.ds(at, member.vr)]

    share = member.shape[0] // 8
    done = 0
    for s in range(steps):
        ready = member.shape[0] * (s + 1) // steps // share

        @pl.when(step == s)
        def _(done=done, ready=ready):
            for i in range(done, ready):
                for src, dst in copies(i):
                    pltpu.make_async_copy(src, dst, sem).start()

        done = ready

    @pl.when(step == steps - 1)
    def _():
        pltpu.make_async_copy(scr_ref, scr_ref, sem).wait()


def weight_blocks(geom, me, act, low, member, rows, far, buffer=None):
    pix, chans = act.shape
    win = low.ndim == 5
    steps = 3 if win else 1
    shard = (rows, LANES)
    outs = [sds((8, *shard), BF16)] * 2 + [sds((2, 8, *shard), BF16)] if far else [sds((32, *shard), BF16)]
    args = [me, act, low] + ([] if buffer is None else [buffer])
    size = member.shape[0] * member.shape[1]
    got = pl.pallas_call(
        functools.partial(weight_blocks_kernel, geom, member, steps, far, buffer is not None),
        grid=(steps,),
        in_specs=[SCALARS, whole(act.shape), whole(low.shape)] + [ANYWHERE] * (buffer is not None),
        out_specs=[ANYWHERE] * len(outs),
        out_shape=outs,
        scratch_shapes=[pltpu.VMEM(member.shape, BF16), pltpu.VMEM((chans, pix), BF16), pltpu.SemaphoreType.DMA],
        input_output_aliases={} if buffer is None else {3: 0},
        compiler_params=params(1),
        cost_estimate=pl.CostEstimate(flops=2 * pix * size, bytes_accessed=size * 2 + pix * 4096, transcendentals=0),
    )(*args)
    return got if far else got[0]


def point_kernel(geom, pieces, *refs):
    frames, rows, cols, _ = geom
    pixels = rows * cols
    refs = list(refs)
    domain_ref, act_ref = refs.pop(0), refs.pop(0)
    if pieces:
        out_ref, sums_ref, matrix_ref, sem = refs[-4:]
        fetch(*pieces, refs[0], refs[1:-4], matrix_ref, sem)
        arrived(matrix_ref, sem)
    else:
        matrix_ref, out_ref, sums_ref = refs
    for lane in range(0, out_ref.shape[-1], 256):
        lanes = slice(lane, lane + 256)
        out_ref[:, lanes] = jnp.dot(act_ref[...], matrix_ref[:, lanes], preferred_element_type=F32)
        pairs = [column_sums(out_ref, f, pixels, lanes) for f in range(frames)]
        sums_ref[:, lanes] = by_domain([p[0] for p in pairs], [p[1] for p in pairs], domain_ref)


def point_layer(geom, domain, act, mat):
    pix, chans = act.shape
    width = mat.shape[1]
    pieces = isinstance(mat, Pieces)
    outs = [sds((pix, width), F32), sds((4, width), F32)] + [sds(mat.shape, BF16)] * pieces
    args = [domain, act] + ([mat.me, *mat.sources] if pieces else [mat])
    specs = [SCALARS, whole(act.shape)]
    specs += [SCALARS] + [ANYWHERE] * len(mat.sources) if pieces else [whole(mat.shape)]
    return pl.pallas_call(
        functools.partial(point_kernel, geom, (mat.member, mat.parts) if pieces else None),
        in_specs=specs,
        out_specs=[whole(o.shape) for o in outs],
        out_shape=outs,
        scratch_shapes=[pltpu.SemaphoreType.DMA] * pieces,
        grid=(1,),
        compiler_params=params(1),
        cost_estimate=pl.CostEstimate(flops=2 * pix * chans * width, bytes_accessed=chans * width * 2 + pix * width * 4, transcendentals=0),
    )(*args)


def point_back_kernel(geom, domain_ref, g_ref, pre_ref, st_ref, sm_ref, gain_ref, mat_ref, low_ref, out_ref):
    frames, rows, cols, counts = geom
    pixels = rows * cols
    for f in range(frames):
        tables = back_tables(st_ref, sm_ref, gain_ref, domain_ref[f], counts)

        def one_row(r, _):
            at = pl.multiple_of(f * pixels + r * cols, cols)
            low = norm_back_rows(g_ref[pl.ds(at, cols), :], pre_ref[pl.ds(at, cols), :], tables)
            low_ref[pl.ds(at, cols), :] = low.astype(BF16)
            return 0

        lax.fori_loop(0, rows, one_row, 0, unroll=2)
    part = lax.dot_general(low_ref[...], mat_ref[...], (((1,), (1,)), ((), ())), preferred_element_type=F32)

    @pl.when(pl.program_id(0) == 0)
    def _():
        out_ref[...] = part

    @pl.when(pl.program_id(0) > 0)
    def _():
        out_ref[...] += part


def point_back(geom, domain, g, pre, stats, sums, gain, mat):
    pix, width = g.shape
    chans = mat.shape[0]
    block = min(width, 512)
    while width % block:
        block -= 256
    col = lambda n: (0, n)
    specs = [SCALARS, pl.BlockSpec((pix, block), col), pl.BlockSpec((pix, block), col)]
    specs += [pl.BlockSpec((4, block), col)] * 2 + [pl.BlockSpec((1, block), col), pl.BlockSpec((chans, block), col)]
    outs = [sds((pix, width), BF16), sds((pix, chans), F32)]
    return pl.pallas_call(
        functools.partial(point_back_kernel, geom),
        grid=(width // block,),
        in_specs=specs,
        out_specs=[pl.BlockSpec((pix, block), col), whole((pix, chans))],
        out_shape=outs,
        compiler_params=params(1),
        cost_estimate=pl.CostEstimate(flops=2 * pix * mat.size, bytes_accessed=mat.size * 2 + pix * width * 10, transcendentals=0),
    )(domain, g, pre, stats, sums, gain, mat)


AXES = ("dp", "fsdp")
CORE, X, Y, Z_NEAR, Z_FAR = range(5)


def swap(x, bit):
    n = lax.axis_size(AXES)
    return lax.ppermute(x, AXES, [(i, i ^ (1 << bit)) for i in range(n)])


def bit_of(bit):
    return (lax.axis_index(AXES) >> bit) & 1


def all_bits():
    return range(lax.axis_size(AXES).bit_length() - 1)


def tied(value, to):
    return lax.optimization_barrier((value, to))[0]


class Links:
    def __init__(self):
        self.under_way = {}

    def busy(self, bit, *values):
        self.under_way.setdefault(bit, []).extend(values)

    def total(self, x, after=None):
        for bit in all_bits():
            for value in self.under_way.pop(bit, ()):
                x = tied(x, value)
            x = x + swap(x, bit)
            for start in (after or {}).get(bit, ()):
                start(x)
        return x


def half_rows(rows):
    return rows // 32 * 16


class Gather:
    def __init__(self, links, shard):
        self.links, self.shard, self.cut = links, shard, half_rows(shard.shape[0])

    def far(self, to=None):
        self.z = self.shard if to is None else tied(self.shard, to)
        self.seen = swap(self.z, Z_FAR)

    def near(self, to=None):
        z = jnp.stack([self.z, self.seen])
        z = z if to is None else tied(z, to)
        self.seen = swap(z, Z_NEAR)
        z = jnp.concatenate([z, self.seen])
        self.a, self.b = z[:, : self.cut], z[:, self.cut :]

    def first(self, to=None):
        a, b = (self.a, self.b) if to is None else (tied(self.a, to), tied(self.b, to))
        self.seen = swap(a, Y), swap(b, X)
        self.a, self.b = jnp.concatenate([a, self.seen[0]]), jnp.concatenate([b, self.seen[1]])

    def second(self, to=None):
        a, b = (self.a, self.b) if to is None else (tied(self.a, to), tied(self.b, to))
        self.seen = swap(a, X), swap(b, Y)
        self.held = [a, self.seen[0], b, self.seen[1]]

    def busy(self):
        self.links.busy(X, self.seen[0])
        self.links.busy(Y, self.seen[1])

    def finish(self, to=None):
        rows = self.shard.shape[0]
        self.sources, self.parts = [], []
        for core in (0, 1):
            for n, value in enumerate(self.held):
                z = [8 * (k >> 1) + 16 * (k & 1) for k in range(4)]
                if n < 2:
                    masks = [core + 2 * n + 4 * y + m for y in (0, 1) for m in z]
                else:
                    masks = [core + 4 * (n - 2) + 2 * x + m for x in (0, 1) for m in z]
                self.parts.append((0, self.cut, masks) if n < 2 else (self.cut, rows - self.cut, masks))
                self.sources.append(swap(value, CORE) if core else value)

    def pieces(self, member):
        return Pieces(member, self.parts, number(1), self.sources)


def number(entries):
    return jnp.full((entries,), lax.axis_index(AXES), jnp.int32)


def plus(a, b):
    return (a.astype(F32) + b.astype(F32)).astype(BF16)


class Scatter:
    def __init__(self, links, blocks):
        self.links = links
        near, far, send = blocks
        self.cut = half_rows(near.shape[1])
        got = swap(send, CORE)
        cut = self.cut
        self.a = [plus(near[:, :cut], got[0, :, :cut]), plus(far[:, :cut], got[1, :, :cut])]
        self.b = [
            jnp.stack([plus(near[s, cut:], got[0, s, cut:]), plus(far[s, cut:], got[1, s, cut:])])
            for s in (slice(0, 4), slice(4, 8))
        ]

    def first(self, to=None):
        send_a, send_b = self.a[1], self.b[1]
        if to is not None:
            send_a, send_b = tied(send_a, to), tied(send_b, to)
        got_a, got_b = swap(send_a, X), swap(send_b, Y)
        self.a = [plus(self.a[0][:4], got_a[:4]), plus(self.a[0][4:], got_a[4:])]
        self.b = [plus(self.b[0][0], got_b[0]), plus(self.b[0][1], got_b[1])]

    def second(self):
        got_a, got_b = swap(self.a[1], Y), swap(self.b[1], X)
        self.links.busy(Y, got_a)
        self.links.busy(X, got_b)
        self.z = [
            jnp.concatenate([plus(self.a[0][s], got_a[s]), plus(self.b[0][s], got_b[s])], 1)
            for s in (slice(0, 2), slice(2, 4))
        ]

    def along_z(self, to=None):
        send = self.z[1] if to is None else tied(self.z[1], to)
        got = swap(send, Z_NEAR)
        keep, send = plus(self.z[0][0], got[0]), plus(self.z[0][1], got[1])
        got = swap(send, Z_FAR)
        self.links.busy(Z_NEAR, got)
        self.out = keep.astype(F32) + got.astype(F32)


def rows_of_chip(shard):
    half = shard.shape[0] // 2
    odd = bit_of(CORE) == 1
    mine = jnp.where(odd, shard[half:], shard[:half])
    got = swap(jnp.where(odd, shard[:half], shard[half:]), CORE)
    return jnp.concatenate([jnp.where(odd, got, mine), jnp.where(odd, mine, got)], 1)


def columns_of_core(rows):
    half = rows.shape[1] // 2
    odd = bit_of(CORE) == 1
    mine = jnp.where(odd, rows[:, half:], rows[:, :half])
    got = swap(jnp.where(odd, rows[:, :half], rows[:, half:]), CORE)
    return jnp.concatenate([jnp.where(odd, got, mine), jnp.where(odd, mine, got)], 0)


def pack(x):
    return jnp.concatenate([x[:, k : k + LANES] for k in range(0, x.shape[1], LANES)], 0)


def unpack(x, blocks):
    rows = x.shape[0] // blocks
    return jnp.concatenate([x[k * rows : (k + 1) * rows] for k in range(blocks)], 1)


def in_three(x):
    high = lax.reduce_precision(x, 8, 7)
    middle = lax.reduce_precision(x - high, 8, 7)
    return jnp.stack([high, middle, x - high - middle]).astype(BF16)


def gather(x):
    x = x[None]
    for bit in all_bits():
        other = swap(x, bit)
        high = bit_of(bit) == 1
        x = jnp.concatenate([jnp.where(high, other, x), jnp.where(high, x, other)], 0)
    return x


def scatter(x):
    for bit in reversed(all_bits()):
        half = x.shape[0] // 2
        high = bit_of(bit) == 1
        send = jnp.where(high, x[:half], x[half:])
        keep = jnp.where(high, x[half:], x[:half])
        x = plus(keep, swap(send, bit))
    return x[0]


def gather_matrix(shard):
    dp, fsdp = lax.axis_size("dp"), lax.axis_size("fsdp")
    rows, cols = shard.shape
    full = gather(shard).reshape(dp, fsdp, rows, cols)
    return full.transpose(0, 2, 1, 3).reshape(dp * rows, fsdp * cols)


def scatter_matrix(full):
    dp, fsdp = lax.axis_size("dp"), lax.axis_size("fsdp")
    rows, cols = full.shape[0] // dp, full.shape[1] // fsdp
    parts = full.reshape(dp, rows, fsdp, cols).transpose(0, 2, 1, 3)
    return scatter(parts.reshape(dp * fsdp, rows, cols)).astype(F32)


class AnyMesh:
    def __init__(self, links, geom, weights, gains, biases):
        self.geom = geom
        self.mats = {name: gather_matrix(w) for name, w in weights.items()}
        self.affine = gather(jnp.stack([gains, biases])).transpose(1, 0, 2).reshape(2, 1, -1)
        self.grads = {}

    def get(self, name):
        return self.mats[name]

    def put(self, name, matrix):
        pass

    def during(self, point):
        return {}

    def add(self, name, act, low):
        self.grads[name] = scatter_matrix(weight_layer(self.geom, act, low))

    def step(self, point, value=None):
        pass


class ThisMesh:
    def __init__(self, links, geom, weights, gains, biases):
        self.geom, self.links = geom, links
        self.me = number(1)
        sizes = (8, 4)
        full = {n: (w.shape[0] * 8, w.shape[1] * 4) for n, w in weights.items()}
        at, packed, self.rest = 0, [], {}
        for name in ("six", "gating", "attend", "five", "four"):
            split = name in ("six", "gating")
            member = Member(at, full[name], *sizes, split=split)
            packed.append(pack(rows_of_chip(weights[name]) if split else weights[name]))
            self.rest[name] = member
            at += member.rows
        self.rest_rows = at
        self.rest_packed = jnp.concatenate(packed)
        self.lone = {n: Member(0, full[n], *sizes) for n in ("one", "two", "three")}
        affine = in_three(jnp.stack([gains, biases])).reshape(-1)
        affine = jnp.pad(affine, (0, 2048 - affine.shape[0])).reshape(16, LANES)
        two = self.lone["two"].rows
        self.g1 = Gather(links, weights["one"])
        self.g2 = Gather(links, jnp.concatenate([weights["two"], affine]))
        self.g3 = Gather(links, weights["three"])
        g1, g2, g3 = self.g1, self.g2, self.g3
        g1.far()
        g1.near()
        g2.far(g1.seen)
        g1.first()
        g2.near(g1.seen)
        g1.second()
        g1.finish()
        g3.far(g2.seen)
        g2.first(g1.seen)
        self.shards = lax.all_gather(tied(self.rest_packed, g1.seen), AXES)
        g3.near(g2.seen)
        g2.second()
        g2.busy()
        self.mats = {"one": g1.pieces(self.lone["one"])}
        self.grads, self.buffer, self.pending = {}, None, {}

    def get(self, name):
        if name in self.mats:
            return self.mats[name]
        if name == "two":
            self.g2.finish()
            rows = self.lone["two"].rows
            self.mats[name] = self.g2.pieces(self.lone["two"])
            flat = collect(self.g2.pieces(FlatMember(rows, 16)))
            parts = flat.reshape(32, 2048)[:, :960].astype(F32).reshape(32, 3, 2, 160)
            self.affine = (parts[:, 0] + parts[:, 1] + parts[:, 2]).transpose(1, 0, 2).reshape(2, 1, -1)
        elif name == "three":
            self.g3.finish()
            self.mats[name] = self.g3.pieces(self.lone["three"])
        else:
            self.mats[name] = Pieces(self.rest[name], [(0, self.rest_rows, None)], self.me, [self.shards])
        return self.mats[name]

    def put(self, name, matrix):
        self.mats[name] = matrix

    def during(self, point):
        if point == 1:

            def start(x):
                self.g3.first(x)
                self.g3.second()
                self.g3.busy()

            return {Y: [start]}
        if point == 12 and "three" in self.pending:

            def start(x):
                self.pending["three"].first(x)
                self.pending["three"].second()

            return {Y: [start]}
        return {}

    def add(self, name, act, low):
        if name in self.rest:
            self.buffer = weight_blocks(self.geom, self.me, act, low, self.rest[name], self.rest_rows, False, self.buffer)
            if name == "four":
                out = lax.psum_scatter(self.buffer, AXES, tiled=False)
                for n, m in self.rest.items():
                    value = unpack(out[m.at : m.at + m.rows], m.blocks)
                    self.grads[n] = (columns_of_core(value) if m.split else value).astype(F32)
        else:
            m = self.lone[name]
            blocks = weight_blocks(self.geom, self.me, act, low, m, m.rows, True)
            self.pending[name] = Scatter(self.links, blocks)

    def step(self, point, value=None):
        if point == "last":
            for name in ("two", "one"):
                s = self.pending[name]
                s.first()
                s.second()
            for name in ("three", "two", "one"):
                s = self.pending[name]
                s.along_z()
                self.grads[name] = s.out


class FlatMember:
    def __init__(self, at, rows):
        self.at, self.vr, self.rows, self.blocks, self.shape = at, rows, rows, 1, (32 * rows, LANES)

    def spots(self, i, j):
        yield self.at, (i * 4 + j) * self.vr, 0


def body(
    frames_in,
    domain,
    kernel_one,
    kernel_two,
    kernel_three,
    attn_enc,
    kernel_four,
    kernel_five,
    kernel_six,
    attn_dec,
    gains,
    biases,
    enc_cot,
    dec_cot,
):
    frames, rows, cols, _ = frames_in.shape
    total_frames = frames * lax.axis_size(AXES)
    first = total_frames * 5 // 8
    counts = (float(first * rows * cols), float((total_frames - first) * rows * cols))
    geom = (frames, rows, cols, counts)
    pix = frames * rows * cols
    source = frames_in.reshape(pix, C_IN)
    enc_cot = enc_cot.transpose(0, 1, 3, 2, 4)
    dec_cot = dec_cot.reshape(pix, TASKS, C_DEC).transpose(1, 0, 2)
    weights = dict(
        one=kernel_one, two=kernel_two, three=kernel_three, attend=attn_enc,
        four=kernel_four, five=kernel_five, six=kernel_six, gating=attn_dec,
    )
    links = Links()
    this = lax.axis_size("dp") == 8 and lax.axis_size("fsdp") == 4
    w = (ThisMesh if this else AnyMesh)(links, geom, weights, gains, biases)

    def forward(name, source, norm=None):
        got = forward_layer(geom, domain, source, w.get(name), norm)
        w.put(name, got[-1])
        return got[:3] if norm is not None else got[:2]

    def point(name, act):
        got = point_layer(geom, domain, act, w.get(name))
        w.put(name, got[-1])
        return got[:2]

    pre_1, local = forward("one", source)
    st_1 = links.total(local, w.during(1))
    w.get("two")
    widths = (C_MID, C_MID, C_MID, TASKS * C_MID, C_MID, C_MID, C_DEC, TASKS * C_DEC)
    gain, bias, at = [], [], 0
    for width in widths:
        gain.append(w.affine[0, :, at : at + width])
        bias.append(w.affine[1, :, at : at + width])
        at += width
    pre_2, local, act_1 = forward("two", pre_1, (st_1, gain[0], bias[0]))
    st_2 = links.total(local)
    pre_3, local, act_2 = forward("three", pre_2, (st_2, gain[1], bias[1]))
    st_3 = links.total(local)
    unpooled = pool_layer(geom, domain, pre_3, st_3, gain[2], bias[2])
    pre_4, local = forward("four", unpooled)
    st_4 = links.total(local)
    pre_5, local, act_4 = forward("five", pre_4, (st_4, gain[4], bias[4]))
    st_5 = links.total(local)
    pre_g, local_g = point("gating", act_4)
    pre_a, local_a = point("attend", act_2)
    pre_6, local, act_5 = forward("six", pre_5, (st_5, gain[5], bias[5]))
    both = links.total(jnp.concatenate([local, local_g, local_a], 1))
    st_6, st_g, st_a = both[:, :C_DEC], both[:, C_DEC : 4 * C_DEC], both[:, 4 * C_DEC :]
    task_maps, g_6, g_g, local = head_layer(
        geom, domain, pre_6, st_6, pre_g, st_g, gain[6], bias[6], gain[7], bias[7], dec_cot
    )
    both = links.total(local)
    sm_6, sm_g = both[:, :C_DEC], both[:, C_DEC:]
    pool_args = (geom, domain, pre_3, st_3, pre_a, st_a, gain[2], bias[2], gain[3], bias[3])
    mix, g_a, sums_a = pool_early(*pool_args, enc_cot)
    task_features = task_layer(*pool_args)

    win_6, g_5, local = backward_layer(
        geom, domain, (g_6, pre_6, st_6, sm_6, gain[6]), w.get("six"), lower=(pre_5, st_5, gain[5], bias[5])
    )
    both = links.total(jnp.concatenate([local, sums_a], 1))
    sm_5, sm_a = both[:, :C_MID], both[:, C_MID:]
    w.add("six", act_5, win_6)
    low_g, add_4 = point_back(geom, domain, g_g, pre_g, st_g, sm_g, gain[7], w.get("gating"))
    w.add("gating", act_4, low_g)
    win_5, g_4, local = backward_layer(
        geom, domain, (g_5, pre_5, st_5, sm_5, gain[5]), w.get("five"), added=add_4, lower=(pre_4, st_4, gain[4], bias[4])
    )
    sm_4 = links.total(local)
    low_a, add_2 = point_back(geom, domain, g_a, pre_a, st_a, sm_a, gain[3], w.get("attend"))
    w.add("attend", act_2, low_a)
    w.add("five", act_4, win_5)
    win_4, g_3, local = backward_layer(
        geom, domain, (g_4, pre_4, st_4, sm_4, gain[4]), w.get("four"), lower=(pre_3, st_3, gain[2], bias[2]), mix=mix
    )
    sm_3 = links.total(local)
    w.add("four", unpooled, win_4)
    win_3, g_2, local = backward_layer(
        geom, domain, (g_3, pre_3, st_3, sm_3, gain[2]), w.get("three"), added=add_2, lower=(pre_2, st_2, gain[1], bias[1])
    )
    sm_2 = links.total(local)
    w.add("three", act_2, win_3)
    win_2, g_1, local = backward_layer(
        geom, domain, (g_2, pre_2, st_2, sm_2, gain[1]), w.get("two"), lower=(pre_1, st_1, gain[0], bias[0])
    )
    sm_1 = links.total(local, w.during(12))
    w.add("two", act_1, win_2)
    win_1, frames_grad = backward_layer(geom, domain, (g_1, pre_1, st_1, sm_1, gain[0]), w.get("one"))
    w.add("one", source, win_1)
    w.step("last")

    sums = jnp.concatenate([sm_1, sm_2, sm_3, sm_a, sm_4, sm_5, sm_6, sm_g], 1)
    shard = gains.shape[0]
    mine = lax.dynamic_slice_in_dim(sums, lax.axis_index(AXES) * shard, shard, 1)
    return (
        task_features.transpose(0, 1, 3, 2, 4),
        task_maps.transpose(1, 0, 2).reshape(frames, rows, cols, TASKS, C_DEC),
        frames_grad.reshape(frames, rows, cols, C_IN),
        *(w.grads[n] for n in ("one", "two", "three", "attend", "four", "five", "six", "gating")),
        mine[2] + mine[3],
        mine[0] + mine[1],
    )


def solution(mesh):
    whole_split = P(AXES)
    matrix = P("dp", "fsdp")
    return jax.shard_map(
        body,
        mesh=mesh,
        in_specs=(whole_split, whole_split) + (matrix,) * 8 + (whole_split,) * 4,
        out_specs=(whole_split,) * 3 + (matrix,) * 8 + (whole_split,) * 2,
        check_vma=False,
    )
```

time: 2090 us -> 716 us (0.34)
  waiting for transfers between devices: 872 us -> 241 us
  blocking collectives: 593 us -> 0 us
  Pallas kernels: 0 us -> 281 us
  matrix products: 239 us -> 0 us
  local copies, waits for them, and re-layouts: 199 us -> 22.6 us
  other arithmetic: 160 us -> 24.3 us
  starting transfers between devices: 1.6 us -> 127 us
    reduce_scatter x8 -> x1, waiting for transfers between devices: 696 us -> 0.01 us  [add(): out = lax.psum_scatter(self.buffer, AXES, tiled=False)]
    psum x11 -> x0, blocking collectives: 455 us -> none  [the longest x6 250 us: norm_layer(): lax.psum((domain_sums(onehot, shaped), domain_sums(onehot, shaped * shape...]
    pallas_call x0 -> x29, Pallas kernels: none -> 281 us  [the longest x6 86.5 us: backward_layer(): pl.pallas_call(functools.partial(backward_kernel, geom, added is not None...]
    ppermute x0 -> x115, waiting for transfers between devices: none -> 241 us  [swap(): return lax.ppermute(x, AXES, [(i, i ^ 1 << bit) for i in range(n)])]
    dot_general x232 -> x0, matrix products: 239 us -> none  [the longest x54 86.8 us: conv_kernel_grad(): lax.dot_general(window.reshape(-1, chans_in), upstream_flat, (((0,), (0,)...]
    unnamed x31 -> x2, waiting for transfers between devices: 172 us -> 0.03 us
    ppermute x0 -> x115, starting transfers between devices: none -> 127 us  [swap(): return lax.ppermute(x, AXES, [(i, i ^ 1 << bit) for i in range(n)])]
    all_gather x9 -> x0, blocking collectives: 96.5 us -> none  [the longest x1 36.6 us: gather_section(): lax.all_gather(by_columns[3], 'dp', axis=0, tiled=True)]
  transfers between devices with their start and end apart: 23 -> 117, of which waited for: 15 -> 74; matrix products, arithmetic and copies ran while one was open for 21% -> 4% of each run, Pallas kernels for 0% -> 26%
where the time goes in v1:
time: 716 us; the launch traced here: 711 us
  Pallas kernels  281 us (39%)
  waiting for transfers between devices  241 us (34%)
  starting transfers between devices  127 us (18%)
  other arithmetic  24.3 us (3%)
  local copies, waits for them, and re-layouts  22.6 us (3%)
  between operations  15.6 us (2%)
    ppermute x115, waiting for transfers between devices, swap(): return lax.ppermute(x, AXES, [(i, i ^ 1 << bit) for i in range(n)])  241 us
    ppermute x115, starting transfers between devices, swap(): return lax.ppermute(x, AXES, [(i, i ^ 1 << bit) for i in range(n)])  127 us
    pallas_call x6, Pallas kernels, backward_layer(): pl.pallas_call(functools.partial(backward_kernel, geom, added is not None...  86.5 us
    pallas_call x6, Pallas kernels, forward_layer(): pl.pallas_call(functools.partial(forward_kernel, geom, norm is not None,...  64.3 us
    pallas_call x8, Pallas kernels, weight_blocks(): pl.pallas_call(functools.partial(weight_blocks_kernel, geom, member, step...  59.8 us
    pallas_call x2, Pallas kernels, point_layer(): pl.pallas_call(functools.partial(point_kernel, geom, (mat.member, mat.par...  17.7 us
    pallas_call x2, Pallas kernels, point_back(): pl.pallas_call(functools.partial(point_back_kernel, geom), grid=(width //...  17.4 us
  transfers between devices with their start and end apart: 117, of which 74 were waited for; matrix products, arithmetic and copies ran while one was open for 4% of the time, Pallas kernels for 26%

profile of v1, /device:TPU:0, one launch (start us, length us, event | category | flops | bytes accessed | tf_op | source)
XLA Modules:
  0.0 711.2 jit_solution(18404804091022164108)
XLA Ops:
  47.6 9.7 %collective-permute-done.12 = bf16[2,592,128]{2,1,0:T(8,128)(2,1)S(1)} collective-permute-done((bf16[2,592,128]{2,1,0:T(8,128)(2,1)S(1)}, bf16[2,592,128]{2,1,0:T(8,128)(2,1)S(1)}, u32[]{:S(2)}, u32[]{:S(2)}) %collective-permute-start.12) | collective-permute-done | bytes 303136 | tf_op jit(solution)/shard_map/ppermute | solution.py:871
  73.3 11.4 %collective-permute-done.26 = bf16[576,128]{1,0:T(8,128)(2,1)S(1)} collective-permute-done((bf16[576,128]{1,0:T(8,128)(2,1)S(1)}, bf16[576,128]{1,0:T(8,128)(2,1)S(1)}, u32[]{:S(2)}, u32[]{:S(2)}) %collective-permute-start.26) | collective-permute-done | bytes 147488 | tf_op jit(solution)/shard_map/ppermute | solution.py:871
  87.4 8.4 %shard_map.237 = (f32[1024,512]{1,0:T(8,128)}, f32[4,512]{1,0:T(4,128)}, bf16[2304,512]{1,0:T(8,128)(2,1)}) custom-call(s32[2]{0:T(128)} %refs_0_.27, bf16[1024,256]{1,0:T(8,128)(2,1)} %bitcast.258, s32[1]{0:T(128)} %bitcast.1.refs_2_.me_ref.refs_5_.refs_0_, bf16[8,144,128]{2,1,0:T(8,128)(2,1)} %copy-done.17, bf16[8,144,128]{2,1,0:T(8,128)(2,1)} %copy-done.41, ...), custom_call_target="tpu_custom_call" | custom-call | flops 2415919104 | bytes 6553600 | tf_op jit(solution)/shard_map/pallas_call | solution.py:244
  116.2 14.1 %collective-permute-done.31 = bf16[4,288,128]{2,1,0:T(8,128)(2,1)S(1)} collective-permute-done((bf16[4,288,128]{2,1,0:T(8,128)(2,1)S(1)}, bf16[4,288,128]{2,1,0:T(8,128)(2,1)S(1)}, u32[]{:S(2)}, u32[]{:S(2)}) %collective-permute-start.31) | collective-permute-done | bytes 294944 | tf_op jit(solution)/shard_map/ppermute | solution.py:871
  156.6 12.2 %shard_map.239 = (f32[1024,512]{1,0:T(8,128)}, f32[4,512]{1,0:T(4,128)}, bf16[1024,512]{1,0:T(8,128)(2,1)}, bf16[4608,512]{1,0:T(8,128)(2,1)}) custom-call(s32[2]{0:T(128)} %refs_0_.27, f32[1024,512]{1,0:T(8,128)} %get-tuple-element.93.refs_1_.refs_7_.refs_2_, f32[4,512]{1,0:T(4,128)} %add.385.refs_2_.refs_8_.refs_3_, ...), custom_call_target="tpu_custom_call" | custom-call | flops 4831838208 | bytes 8912896 | tf_op jit(solution)/shard_map/pallas_call | solution.py:244
  188.4 12.1 %shard_map.240 = (f32[1024,512]{1,0:T(8,128)}, f32[4,512]{1,0:T(4,128)}, bf16[1024,512]{1,0:T(8,128)(2,1)}, bf16[4608,512]{1,0:T(8,128)(2,1)}) custom-call(s32[2]{0:T(128)} %refs_0_.27, f32[1024,512]{1,0:T(8,128)} %get-tuple-element.101.refs_1_.refs_8_.refs_2_, f32[4,512]{1,0:T(4,128)} %add.393.refs_2_.refs_9_.refs_3_, ...), custom_call_target="tpu_custom_call" | custom-call | flops 4831838208 | bytes 8912896 | tf_op jit(solution)/shard_map/pallas_call | solution.py:244
  223.4 11.3 %shard_map.243 = (f32[1024,512]{1,0:T(8,128)}, f32[4,512]{1,0:T(4,128)}, bf16[4608,512]{1,0:T(8,128)(2,1)}) custom-call(s32[2]{0:T(128)} %refs_0_.27, bf16[1024,512]{1,0:T(8,128)(2,1)} %shard_map.242.refs_1_, s32[1]{0:T(128)} %bitcast.1.refs_2_.me_ref.refs_5_.refs_0_, bf16[32,1728,128]{2,1,0:T(8,128)(2,1)} %bitcast.237), custom_call_target="tpu_custom_call" | custom-call | flops 4831838208 | bytes 8912896 | tf_op jit(solution)/shard_map/pallas_call | solution.py:244
  252.9 12.1 %shard_map.244 = (f32[1024,512]{1,0:T(8,128)}, f32[4,512]{1,0:T(4,128)}, bf16[1024,512]{1,0:T(8,128)(2,1)}, bf16[4608,512]{1,0:T(8,128)(2,1)}) custom-call(s32[2]{0:T(128)} %refs_0_.27, f32[1024,512]{1,0:T(8,128)} %get-tuple-element.114.refs_1_.refs_8_.refs_2_, f32[4,512]{1,0:T(4,128)} %add.403.refs_2_.refs_9_.refs_3_, ...), custom_call_target="tpu_custom_call" | custom-call | flops 4831838208 | bytes 8912896 | tf_op jit(solution)/shard_map/pallas_call | solution.py:244
  276.2 11.0 %shard_map.241 = (f32[1024,1536]{1,0:T(8,128)}, f32[4,1536]{1,0:T(4,128)}, bf16[512,1536]{1,0:T(8,128)(2,1)}) custom-call(s32[2]{0:T(128)} %refs_0_.27, bf16[1024,512]{1,0:T(8,128)(2,1)} %get-tuple-element.111.refs_1_, s32[1]{0:T(128)} %bitcast.1.refs_2_.me_ref.refs_5_.refs_0_, bf16[32,1728,128]{2,1,0:T(8,128)(2,1)} %bitcast.239), custom_call_target="tpu_custom_call" | custom-call | flops 1610612736 | bytes 7864320 | tf_op jit(solution)/shard_map/pallas_call | solution.py:808
  326.0 8.7 %shard_map.248 = (f32[3,1024,256]{2,1,0:T(8,128)}, f32[1024,256]{1,0:T(8,128)}, f32[1024,768]{1,0:T(8,128)}, f32[4,1024]{1,0:T(4,128)}) custom-call(s32[2]{0:T(128)} %refs_0_.27, f32[1024,256]{1,0:T(8,128)} %get-tuple-element.122.bot_ref.refs_2_, f32[4,256]{1,0:T(4,128)} %slice.676.bot_st.refs_3_, f32[1024,768]{1,0:T(8,128)} %get-tuple-element.123.gate_ref.pre_ref, ...), custom_call_target="tpu_custom_call" | custom-call | flops 20971520 | bytes 11534336 | tf_op jit(solution)/shard_map/pallas_call | solution.py:496
  349.5 12.4 %shard_map.250 = (f32[1024,512]{1,0:T(8,128)}, f32[1024,1536]{1,0:T(8,128)}, f32[4,1536]{1,0:T(4,128)}) custom-call(s32[2]{0:T(128)} %refs_0_.27, f32[1024,512]{1,0:T(8,128)} %get-tuple-element.109.top_ref.refs_7_.refs_2_, f32[4,512]{1,0:T(4,128)} %add.398.top_st.refs_8_.refs_3_, f32[1024,1536]{1,0:T(8,128)} %get-tuple-element.113.wide_ref.pre_ref, ...), custom_call_target="tpu_custom_call" | custom-call | flops 47185920 | bytes 20971520 | tf_op jit(solution)/shard_map/pallas_call | solution.py:432
  362.6 10.8 %shard_map.249 = (bf16[3,2,18,32,256]{4,3,2,1,0:T(8,128)(2,1)}, f32[1024,512]{1,0:T(8,128)}, f32[4,512]{1,0:T(4,128)}) custom-call(s32[2]{0:T(128)} %refs_0_.27, f32[1024,256]{1,0:T(8,128)} %get-tuple-element.125.refs_1_, f32[1024,256]{1,0:T(8,128)} %get-tuple-element.122.bot_ref.refs_2_, f32[4,256]{1,0:T(4,128)} %slice.676.bot_st.refs_3_, ...), custom_call_target="tpu_custom_call" | custom-call | flops 2415919104 | bytes 12845056 | tf_op jit(solution)/shard_map/pallas_call | solution.py:632
  397.8 16.2 %shard_map.252 = (bf16[3,2,18,32,512]{4,3,2,1,0:T(8,128)(2,1)}, f32[1024,512]{1,0:T(8,128)}, f32[4,512]{1,0:T(4,128)}) custom-call(s32[2]{0:T(128)} %refs_0_.27, f32[1024,512]{1,0:T(8,128)} %get-tuple-element.128.refs_1_, f32[1024,512]{1,0:T(8,128)} %get-tuple-element.116.refs_1_.refs_7_.refs_2_, f32[4,512]{1,0:T(4,128)} %add.408.refs_2_.refs_8_.refs_3_, ...), custom_call_target="tpu_custom_call" | custom-call | flops 4831838208 | bytes 15204352 | tf_op jit(solution)/shard_map/pallas_call | solution.py:632
  427.0 10.3 %shard_map.254 = (bf16[1024,1536]{1,0:T(8,128)(2,1)}, f32[1024,512]{1,0:T(8,128)}) custom-call(s32[2]{0:T(128)} %refs_0_.27, f32[1024,1536]{1,0:T(8,128)} %get-tuple-element.142.g_ref, f32[1024,1536]{1,0:T(8,128)} %get-tuple-element.113.wide_ref.pre_ref, f32[4,1536]{1,0:T(4,128)} %slice.673.wide_st.st_ref, f32[4,1536]{1,0:T(4,128)} %slice.685.sm_ref, ...), custom_call_target="tpu_custom_call" | custom-call | flops 1610612736 | bytes 17301504 | tf_op jit(solution)/shard_map/pallas_call | solution.py:854
  443.2 9.5 %shard_map.264.refs_3_ = bf16[32,1728,128]{2,1,0:T(8,128)(2,1)} custom-call(s32[1]{0:T(128)} %bitcast.1.refs_2_.me_ref.refs_5_.refs_0_, bf16[1024,512]{1,0:T(8,128)(2,1)} %get-tuple-element.119.refs_1_, bf16[3,2,18,32,512]{4,3,2,1,0:T(8,128)(2,1)} %get-tuple-element.168.refs_2_, ...), custom_call_target="tpu_custom_call", output_to_operand_aliasing={{}: (3, {})} | custom-call | flops 4831838208 | bytes 8912896 | tf_op jit(solution)/shard_map/pallas_call | solution.py:768
  453.3 18.2 %shard_map.253 = (bf16[3,2,18,32,512]{4,3,2,1,0:T(8,128)(2,1)}, f32[1024,512]{1,0:T(8,128)}, f32[4,512]{1,0:T(4,128)}) custom-call(s32[2]{0:T(128)} %refs_0_.27, f32[1024,512]{1,0:T(8,128)} %get-tuple-element.135.refs_1_, f32[1024,512]{1,0:T(8,128)} %get-tuple-element.114.refs_1_.refs_8_.refs_2_, f32[4,512]{1,0:T(4,128)} %add.403.refs_2_.refs_9_.refs_3_, ...), custom_call_target="tpu_custom_call" | custom-call | flops 4831838208 | bytes 15204352 | tf_op jit(solution)/shard_map/pallas_call | solution.py:632
  471.4 9.4 %shard_map.265 = bf16[32,1728,128]{2,1,0:T(8,128)(2,1)} custom-call(s32[1]{0:T(128)} %bitcast.1.refs_2_.me_ref.refs_5_.refs_0_, bf16[1024,512]{1,0:T(8,128)(2,1)} %shard_map.242.refs_1_, bf16[3,2,18,32,512]{4,3,2,1,0:T(8,128)(2,1)} %get-tuple-element.167.refs_2_, bf16[32,1728,128]{2,1,0:T(8,128)(2,1)} %shard_map.264.refs_3_), custom_call_target="tpu_custom_call", output_to_operand_aliasing={{}: (3, {})} | custom-call | flops 4831838208 | bytes 8912896 | tf_op jit(solution)/shard_map/pallas_call | solution.py:768
  498.9 17.0 %shard_map.255 = (bf16[3,2,18,32,512]{4,3,2,1,0:T(8,128)(2,1)}, f32[1024,512]{1,0:T(8,128)}, f32[4,512]{1,0:T(4,128)}) custom-call(s32[2]{0:T(128)} %refs_0_.27, f32[1024,512]{1,0:T(8,128)} %get-tuple-element.139.refs_1_, f32[1024,512]{1,0:T(8,128)} %get-tuple-element.109.top_ref.refs_7_.refs_2_, f32[4,512]{1,0:T(4,128)} %add.398.top_st.refs_8_.refs_3_, ...), custom_call_target="tpu_custom_call" | custom-call | flops 4831838208 | bytes 15204352 | tf_op jit(solution)/shard_map/pallas_call | solution.py:632
  534.1 15.3 %shard_map.256 = (bf16[3,2,18,32,512]{4,3,2,1,0:T(8,128)(2,1)}, f32[1024,512]{1,0:T(8,128)}, f32[4,512]{1,0:T(4,128)}) custom-call(s32[2]{0:T(128)} %refs_0_.27, f32[1024,512]{1,0:T(8,128)} %get-tuple-element.145.refs_1_, f32[1024,512]{1,0:T(8,128)} %get-tuple-element.101.refs_1_.refs_8_.refs_2_, f32[4,512]{1,0:T(4,128)} %add.393.refs_2_.refs_9_.refs_3_, ...), custom_call_target="tpu_custom_call" | custom-call | flops 4831838208 | bytes 15204352 | tf_op jit(solution)/shard_map/pallas_call | solution.py:632
  573.5 9.7 %shard_map.260 = (bf16[8,576,128]{2,1,0:T(8,128)(2,1)}, bf16[8,576,128]{2,1,0:T(8,128)(2,1)}, bf16[2,8,576,128]{3,2,1,0:T(8,128)(2,1)}) custom-call(s32[1]{0:T(128)} %bitcast.1.refs_2_.me_ref.refs_5_.refs_0_, bf16[1024,512]{1,0:T(8,128)(2,1)} %get-tuple-element.111.refs_1_, bf16[3,2,18,32,512]{4,3,2,1,0:T(8,128)(2,1)} %get-tuple-element.161.refs_2_), custom_call_target="tpu_custom_call" | custom-call | flops 4831838208 | bytes 8912896 | tf_op jit(solution)/shard_map/pallas_call | solution.py:768
  584.0 9.1 %shard_map.257 = (bf16[3,2,18,32,512]{4,3,2,1,0:T(8,128)(2,1)}, f32[1024,256]{1,0:T(8,128)}) custom-call(s32[2]{0:T(128)} %refs_0_.27, f32[1024,512]{1,0:T(8,128)} %get-tuple-element.148.refs_1_, f32[1024,512]{1,0:T(8,128)} %get-tuple-element.93.refs_1_.refs_7_.refs_2_, f32[4,512]{1,0:T(4,128)} %add.385.refs_2_.refs_8_.refs_3_, ...), custom_call_target="tpu_custom_call" | custom-call | flops 2415919104 | bytes 12845056 | tf_op jit(solution)/shard_map/pallas_call | solution.py:632
  600.0 9.7 %shard_map.259 = (bf16[8,576,128]{2,1,0:T(8,128)(2,1)}, bf16[8,576,128]{2,1,0:T(8,128)(2,1)}, bf16[2,8,576,128]{3,2,1,0:T(8,128)(2,1)}) custom-call(s32[1]{0:T(128)} %bitcast.1.refs_2_.me_ref.refs_5_.refs_0_, bf16[1024,512]{1,0:T(8,128)(2,1)} %get-tuple-element.156.refs_1_, bf16[3,2,18,32,512]{4,3,2,1,0:T(8,128)(2,1)} %get-tuple-element.157.refs_2_), custom_call_target="tpu_custom_call" | custom-call | flops 4831838208 | bytes 8912896 | tf_op jit(solution)/shard_map/pallas_call | solution.py:768
  640.3 12.7 %collective-permute-done.109 = bf16[2,4,288,128]{3,2,1,0:T(8,128)(2,1)S(1)} collective-permute-done((bf16[2,4,288,128]{3,2,1,0:T(8,128)(2,1)S(1)}, bf16[2,4,288,128]{3,2,1,0:T(8,128)(2,1)S(1)}, u32[]{:S(2)}, u32[]{:S(2)}) %collective-permute-start.109) | collective-permute-done | bytes 589856 | tf_op jit(solution)/shard_map/ppermute | solution.py:871
  655.2 10.4 %collective-permute-done.102 = bf16[2,4,288,128]{3,2,1,0:T(8,128)(2,1)S(1)} collective-permute-done((bf16[2,4,288,128]{3,2,1,0:T(8,128)(2,1)S(1)}, bf16[2,4,288,128]{3,2,1,0:T(8,128)(2,1)S(1)}, u32[]{:S(2)}, u32[]{:S(2)}) %collective-permute-start.102) | collective-permute-done | bytes 589856 | tf_op jit(solution)/shard_map/ppermute | solution.py:871
  (511 shorter events, 414.1 us)
Async XLA Ops:
  7.2 216.2 %all-gather.3.cloned.1.call-start = ((), (), s32[]{:S(2)}) async-start(), calls=%async_computation.2 | async-start | bytes 14598144 | tf_op jit(solution)/shard_map/all_gather | solution.py:1119
  38.5 658.4 %reduce-scatter.2.cloned.1.call-start = ((), (), s32[]{:S(2)}) async-start(), calls=%async_computation.1 | async-start | bytes 14598144 | tf_op jit(solution)/shard_map/reduce_scatter | solution.py:1168
  59.2 25.8 %collective-permute-start.8 = (bf16[8,144,128]{2,1,0:T(8,128)(2,1)S(1)}, bf16[8,144,128]{2,1,0:T(8,128)(2,1)S(1)}, u32[]{:S(2)}, u32[]{:S(2)}) collective-permute-start(bf16[8,144,128]{2,1,0:T(8,128)(2,1)S(1)} %pad_maximum_fusion.5.refs_5_), channel_id=1, source_target_pairs={{0,1},{1,0},{2,3},{3,2},{4,5},{5,4},{6,7},{7,6},{8,9},{9,8},{10,11... | collective-permute-start | bytes 884744 | tf_op jit(solution)/shard_map/ppermute | solution.py:871
  59.2 27.4 %collective-permute-start.7 = (bf16[8,144,128]{2,1,0:T(8,128)(2,1)S(1)}, bf16[8,144,128]{2,1,0:T(8,128)(2,1)S(1)}, u32[]{:S(2)}, u32[]{:S(2)}) collective-permute-start(bf16[8,144,128]{2,1,0:T(8,128)(2,1)S(1)} %collective-permute-done.3.refs_4_), channel_id=1, source_target_pairs={{0,1},{1,0},{2,3},{3,2},{4,5},{5,4},{6,7},{7,6},{8,9},{9,8},{10,11... | collective-permute-start | bytes 884744 | tf_op jit(solution)/shard_map/ppermute | solution.py:871
  61.5 25.1 %collective-permute-start.9 = (bf16[8,144,128]{2,1,0:T(8,128)(2,1)S(1)}, bf16[8,144,128]{2,1,0:T(8,128)(2,1)S(1)}, u32[]{:S(2)}, u32[]{:S(2)}) collective-permute-start(bf16[8,144,128]{2,1,0:T(8,128)(2,1)S(1)} %collective-permute-done.5.refs_6_), channel_id=1, source_target_pairs={{0,1},{1,0},{2,3},{3,2},{4,5},{5,4},{6,7},{7,6},{8,9},{9,8},{10,11... | collective-permute-start | bytes 884744 | tf_op jit(solution)/shard_map/ppermute | solution.py:871
  64.1 20.5 %collective-permute-start.26 = (bf16[576,128]{1,0:T(8,128)(2,1)S(1)}, bf16[576,128]{1,0:T(8,128)(2,1)S(1)}, u32[]{:S(2)}, u32[]{:S(2)}) collective-permute-start(bf16[576,128]{1,0:T(8,128)(2,1)S(1)} %copy-done.24), channel_id=1, source_target_pairs={{0,16},{1,17},{2,18},{3,19},{4,20},{5,21},{6,22},{7,23},{8,24},{9,... | collective-permute-start | bytes 442376 | tf_op jit(solution)/shard_map/ppermute | solution.py:871
  71.7 26.4 %collective-permute-start.14 = (bf16[8,288,128]{2,1,0:T(8,128)(2,1)S(1)}, bf16[8,288,128]{2,1,0:T(8,128)(2,1)S(1)}, u32[]{:S(2)}, u32[]{:S(2)}) collective-permute-start(bf16[8,288,128]{2,1,0:T(8,128)(2,1)S(1)} %constant_dynamic-update-slice_fusion.2.refs_0_.refs_6_), channel_id=1, source_target_pairs={{0,2},{1,3},{2,0},{3,1},{4,6},{5,7},{6,4},{7,5},{8,10},{9,11},{10,... | collective-permute-start | bytes 1769480 | tf_op jit(solution)/shard_map/ppermute | solution.py:871
  106.6 27.6 %collective-permute-start.21 = (bf16[8,288,128]{2,1,0:T(8,128)(2,1)S(1)}, bf16[8,288,128]{2,1,0:T(8,128)(2,1)S(1)}, u32[]{:S(2)}, u32[]{:S(2)}) collective-permute-start(bf16[8,288,128]{2,1,0:T(8,128)(2,1)S(1)} %constant_dynamic-update-slice_fusion.2.refs_0_.refs_6_), channel_id=1, source_target_pairs={{0,1},{1,0},{2,3},{3,2},{4,5},{5,4},{6,7},{7,6},{8,9},{9,8},{10,11... | collective-permute-start | bytes 1769480 | tf_op jit(solution)/shard_map/ppermute | solution.py:871
  106.6 32.8 %collective-permute-start.23 = (bf16[8,304,128]{2,1,0:T(8,128)(2,1)S(1)}, bf16[8,304,128]{2,1,0:T(8,128)(2,1)S(1)}, u32[]{:S(2)}, u32[]{:S(2)}) collective-permute-start(bf16[8,304,128]{2,1,0:T(8,128)(2,1)S(1)} %constant_dynamic-update-slice_fusion.4.refs_2_.refs_8_), channel_id=1, source_target_pairs={{0,1},{1,0},{2,3},{3,2},{4,5},{5,4},{6,7},{7,6},{8,9},{9,8},{10,11... | collective-permute-start | bytes 1867784 | tf_op jit(solution)/shard_map/ppermute | solution.py:871
  107.2 32.8 %collective-permute-start.24 = (bf16[8,304,128]{2,1,0:T(8,128)(2,1)S(1)}, bf16[8,304,128]{2,1,0:T(8,128)(2,1)S(1)}, u32[]{:S(2)}, u32[]{:S(2)}) collective-permute-start(bf16[8,304,128]{2,1,0:T(8,128)(2,1)S(1)} %collective-permute-done.17.refs_3_.refs_9_), channel_id=1, source_target_pairs={{0,1},{1,0},{2,3},{3,2},{4,5},{5,4},{6,7},{7,6},{8,9},{9,8},{10,11... | collective-permute-start | bytes 1867784 | tf_op jit(solution)/shard_map/ppermute | solution.py:871
  110.9 28.6 %collective-permute-start.22 = (bf16[8,288,128]{2,1,0:T(8,128)(2,1)S(1)}, bf16[8,288,128]{2,1,0:T(8,128)(2,1)S(1)}, u32[]{:S(2)}, u32[]{:S(2)}) collective-permute-start(bf16[8,288,128]{2,1,0:T(8,128)(2,1)S(1)} %collective-permute-done.14.refs_1_.refs_7_), channel_id=1, source_target_pairs={{0,1},{1,0},{2,3},{3,2},{4,5},{5,4},{6,7},{7,6},{8,9},{9,8},{10,11... | collective-permute-start | bytes 1769480 | tf_op jit(solution)/shard_map/ppermute | solution.py:871
  136.8 19.1 %collective-permute-start.29 = (bf16[8,288,128]{2,1,0:T(8,128)(2,1)S(1)}, bf16[8,288,128]{2,1,0:T(8,128)(2,1)S(1)}, u32[]{:S(2)}, u32[]{:S(2)}) collective-permute-start(bf16[8,288,128]{2,1,0:T(8,128)(2,1)S(1)} %constant_dynamic-update-slice_fusion.8.refs_6_), channel_id=1, source_target_pairs={{0,2},{1,3},{2,0},{3,1},{4,6},{5,7},{6,4},{7,5},{8,10},{9,11},{10,... | collective-permute-start | bytes 1769480 | tf_op jit(solution)/shard_map/ppermute | solution.py:871
  139.4 47.8 %collective-permute-start.38 = (bf16[8,288,128]{2,1,0:T(8,128)(2,1)S(1)}, bf16[8,288,128]{2,1,0:T(8,128)(2,1)S(1)}, u32[]{:S(2)}, u32[]{:S(2)}) collective-permute-start(bf16[8,288,128]{2,1,0:T(8,128)(2,1)S(1)} %constant_dynamic-update-slice_fusion.10.refs_8_), channel_id=1, source_target_pairs={{0,1},{1,0},{2,3},{3,2},{4,5},{5,4},{6,7},{7,6},{8,9},{9,8},{10,11... | collective-permute-start | bytes 1769480 | tf_op jit(solution)/shard_map/ppermute | solution.py:871
  139.5 47.8 %collective-permute-start.36 = (bf16[8,288,128]{2,1,0:T(8,128)(2,1)S(1)}, bf16[8,288,128]{2,1,0:T(8,128)(2,1)}, u32[]{:S(2)}, u32[]{:S(2)}) collective-permute-start(bf16[8,288,128]{2,1,0:T(8,128)(2,1)S(1)} %constant_dynamic-update-slice_fusion.8.refs_6_), channel_id=1, source_target_pairs={{0,1},{1,0},{2,3},{3,2},{4,5},{5,4},{6,7},{7,6},{8,9},{9,8},{10,11... | collective-permute-start | bytes 1769480 | tf_op jit(solution)/shard_map/ppermute | solution.py:871
  151.0 36.2 %collective-permute-start.39 = (bf16[8,288,128]{2,1,0:T(8,128)(2,1)S(1)}, bf16[8,288,128]{2,1,0:T(8,128)(2,1)S(1)}, u32[]{:S(2)}, u32[]{:S(2)}) collective-permute-start(bf16[8,288,128]{2,1,0:T(8,128)(2,1)S(1)} %collective-permute-done.32.refs_9_), channel_id=1, source_target_pairs={{0,1},{1,0},{2,3},{3,2},{4,5},{5,4},{6,7},{7,6},{8,9},{9,8},{10,11... | collective-permute-start | bytes 1769480 | tf_op jit(solution)/shard_map/ppermute | solution.py:871
  155.9 31.4 %collective-permute-start.37 = (bf16[8,288,128]{2,1,0:T(8,128)(2,1)S(1)}, bf16[8,288,128]{2,1,0:T(8,128)(2,1)S(1)}, u32[]{:S(2)}, u32[]{:S(2)}) collective-permute-start(bf16[8,288,128]{2,1,0:T(8,128)(2,1)S(1)} %collective-permute-done.29.refs_7_), channel_id=1, source_target_pairs={{0,1},{1,0},{2,3},{3,2},{4,5},{5,4},{6,7},{7,6},{8,9},{9,8},{10,11... | collective-permute-start | bytes 1769480 | tf_op jit(solution)/shard_map/ppermute | solution.py:871
  583.3 51.5 %collective-permute-start.106 = (bf16[2,8,576,128]{3,2,1,0:T(8,128)(2,1)}, bf16[2,8,576,128]{3,2,1,0:T(8,128)(2,1)S(1)}, u32[]{:S(2)}, u32[]{:S(2)}) collective-permute-start(bf16[2,8,576,128]{3,2,1,0:T(8,128)(2,1)} %get-tuple-element.163), channel_id=1, source_target_pairs={{0,1},{1,0},{2,3},{3,2},{4,5},{5,4},{6,7},{7,6},{8,9},{9,8},{10,11... | collective-permute-start | bytes 7077896 | tf_op jit(solution)/shard_map/ppermute | solution.py:871
  609.6 27.2 %collective-permute-start.99 = (bf16[2,8,576,128]{3,2,1,0:T(8,128)(2,1)}, bf16[2,8,576,128]{3,2,1,0:T(8,128)(2,1)S(1)}, u32[]{:S(2)}, u32[]{:S(2)}) collective-permute-start(bf16[2,8,576,128]{3,2,1,0:T(8,128)(2,1)} %get-tuple-element.159), channel_id=1, source_target_pairs={{0,1},{1,0},{2,3},{3,2},{4,5},{5,4},{6,7},{7,6},{8,9},{9,8},{10,11... | collective-permute-start | bytes 7077896 | tf_op jit(solution)/shard_map/ppermute | solution.py:871
  632.4 46.5 %collective-permute-start.98 = (bf16[288,128]{1,0:T(8,128)(2,1)S(1)}, bf16[288,128]{1,0:T(8,128)(2,1)S(1)}, u32[]{:S(2)}, u32[]{:S(2)}) collective-permute-start(bf16[288,128]{1,0:T(8,128)(2,1)S(1)} %fusion.39), channel_id=1, source_target_pairs={{0,16},{1,17},{2,18},{3,19},{4,20},{5,21},{6,22},{7,23},{8,24},{9,... | collective-permute-start | bytes 221192 | tf_op jit(solution)/shard_map/ppermute | solution.py:871
  635.1 17.9 %collective-permute-start.109 = (bf16[2,4,288,128]{3,2,1,0:T(8,128)(2,1)S(1)}, bf16[2,4,288,128]{3,2,1,0:T(8,128)(2,1)S(1)}, u32[]{:S(2)}, u32[]{:S(2)}) collective-permute-start(bf16[2,4,288,128]{3,2,1,0:T(8,128)(2,1)S(1)} %pad_maximum_fusion.1), channel_id=1, source_target_pairs={{0,4},{1,5},{2,6},{3,7},{4,0},{5,1},{6,2},{7,3},{8,12},{9,13},{10,... | collective-permute-start | bytes 1769480 | tf_op jit(solution)/shard_map/ppermute | solution.py:871
  636.0 18.3 %collective-permute-start.107 = (bf16[8,288,128]{2,1,0:T(8,128)(2,1)S(1)}, bf16[8,288,128]{2,1,0:T(8,128)(2,1)S(1)}, u32[]{:S(2)}, u32[]{:S(2)}) collective-permute-start(bf16[8,288,128]{2,1,0:T(8,128)(2,1)S(1)} %get-tuple-element.165), channel_id=1, source_target_pairs={{0,2},{1,3},{2,0},{3,1},{4,6},{5,7},{6,4},{7,5},{8,10},{9,11},{10,... | collective-permute-start | bytes 1769480 | tf_op jit(solution)/shard_map/ppermute | solution.py:871
  637.0 28.5 %collective-permute-start.102 = (bf16[2,4,288,128]{3,2,1,0:T(8,128)(2,1)S(1)}, bf16[2,4,288,128]{3,2,1,0:T(8,128)(2,1)S(1)}, u32[]{:S(2)}, u32[]{:S(2)}) collective-permute-start(bf16[2,4,288,128]{3,2,1,0:T(8,128)(2,1)S(1)} %pad_maximum_fusion), channel_id=1, source_target_pairs={{0,4},{1,5},{2,6},{3,7},{4,0},{5,1},{6,2},{7,3},{8,12},{9,13},{10,... | collective-permute-start | bytes 1769480 | tf_op jit(solution)/shard_map/ppermute | solution.py:871
  638.7 28.3 %collective-permute-start.100 = (bf16[8,288,128]{2,1,0:T(8,128)(2,1)S(1)}, bf16[8,288,128]{2,1,0:T(8,128)(2,1)S(1)}, u32[]{:S(2)}, u32[]{:S(2)}) collective-permute-start(bf16[8,288,128]{2,1,0:T(8,128)(2,1)S(1)} %get-tuple-element.223), channel_id=1, source_target_pairs={{0,2},{1,3},{2,0},{3,1},{4,6},{5,7},{6,4},{7,5},{8,10},{9,11},{10,... | collective-permute-start | bytes 1769480 | tf_op jit(solution)/shard_map/ppermute | solution.py:871
  653.2 19.0 %collective-permute-start.110 = (bf16[4,288,128]{2,1,0:T(8,128)(2,1)S(1)}, bf16[4,288,128]{2,1,0:T(8,128)(2,1)S(1)}, u32[]{:S(2)}, u32[]{:S(2)}) collective-permute-start(bf16[4,288,128]{2,1,0:T(8,128)(2,1)S(1)} %get-tuple-element.215), channel_id=1, source_target_pairs={{0,2},{1,3},{2,0},{3,1},{4,6},{5,7},{6,4},{7,5},{8,10},{9,11},{10,... | collective-permute-start | bytes 884744 | tf_op jit(solution)/shard_map/ppermute | solution.py:871
  (140 other events, 1289.9 us)
Sparse Core Ops, SparseCore 0:
  38.6 130.9 all-gather.2
  481.0 171.6 reduce-scatter.1

commit v2 on v1

--- a/solution.py
+++ b/solution.py
@@ -15,7 +15,8 @@
 LANES = 128
 F32 = jnp.float32
 BF16 = jnp.bfloat16
-VMEM_LIMIT = 56 * 1024 * 1024
+COST = 0.1
+VMEM_LIMIT = 20 * 1024 * 1024
 
 
 def params(grid_dims=0):
@@ -25,9 +26,13 @@
     )
 
 
+def cost(flops, size):
+    return pl.CostEstimate(flops=int(flops * COST), bytes_accessed=int(size * COST), transcendentals=0)
+
+
 def whole(shape):
     zeros = (0,) * len(shape)
-    return pl.BlockSpec(shape, lambda *_: zeros)
+    return pl.BlockSpec(shape, lambda *_: zeros, pipeline_mode=pl.Buffered(1))
 
 
 SCALARS = pl.BlockSpec(memory_space=pltpu.SMEM)
@@ -107,9 +112,14 @@
     return jnp.sum(one, 0, keepdims=True), jnp.sum(two, 0, keepdims=True)
 
 
+def in_hbm(x):
+    return pltpu.with_memory_space_constraint(x, pltpu.HBM)
+
+
 class Pieces:
     def __init__(self, member, parts, me, sources):
-        self.member, self.parts, self.me, self.sources = member, parts, me, sources
+        self.member, self.parts, self.me = member, parts, me
+        self.sources = [in_hbm(x) for x in sources]
         self.shape = member.shape
 
 
@@ -237,7 +247,7 @@
         out_specs.append(whole((pix, chans)))
     scratch = [pltpu.VMEM((3, frames, rows + 2, cols, chans), BF16)]
     if pieces:
-        outs.append(sds(kernel.shape, BF16))
+        outs.append(pltpu.HBM(kernel.shape, BF16))
         out_specs.append(ANYWHERE)
         scratch += [pltpu.VMEM(kernel.shape, BF16), pltpu.SemaphoreType.DMA((2,))]
     size = kernel.shape[0] * kernel.shape[1]
@@ -249,7 +259,7 @@
         out_shape=outs,
         scratch_shapes=scratch,
         compiler_params=params(1),
-        cost_estimate=pl.CostEstimate(flops=2 * pix * size, bytes_accessed=size * 2 + pix * 4096, transcendentals=0),
+        cost_estimate=cost(2 * pix * size, size * 2 + pix * 4096),
     )(*args)
 
 
@@ -310,28 +320,26 @@
         out_specs=whole((pix, chans)),
         out_shape=sds((pix, chans), BF16),
         compiler_params=params(),
-        cost_estimate=pl.CostEstimate(flops=pix * chans * 20, bytes_accessed=pix * chans * 6, transcendentals=pix * chans * 2),
+        cost_estimate=cost(pix * chans * 20, pix * chans * 6),
     )(*args)
 
 
-def task_kernel(geom, domain_ref, top_ref, top_st, wide_ref, wide_st, gain_t, bias_t, gain_w, bias_w, task_ref, scr_ref):
+def task_kernel(geom, domain_ref, top_ref, top_st, gain_t, bias_t, *refs):
     frames, rows, cols, counts = geom
     pixels = rows * cols
-    chans = top_ref.shape[-1]
+    masks = [refs[4 * k : 4 * k + 4] for k in range(TASKS)]
+    task_ref, scr_ref = refs[-2:]
     for f in range(frames):
-        for lane in range(0, chans, LANES):
+        for lane in range(0, top_ref.shape[-1], LANES):
             lanes = slice(lane, lane + LANES)
 
-            def table(st, gain, bias, sl):
-                average, inverse = frame_tables(st[:, sl], domain_ref[f], counts)
-                scale = inverse * gain[:, sl]
-                return scale, bias[:, sl] - average * scale
-
-            t_scale, t_shift = table(top_st, gain_t, bias_t, lanes)
-            wide = []
-            for k in range(TASKS):
-                sl = slice(k * chans + lane, k * chans + lane + LANES)
-                wide.append((sl, *table(wide_st, gain_w, bias_w, sl)))
+            def table(st, gain, bias):
+                average, inverse = frame_tables(st[:, lanes], domain_ref[f], counts)
+                scale = inverse * gain[:, lanes]
+                return scale, bias[:, lanes] - average * scale
+
+            t_scale, t_shift = table(top_st, gain_t, bias_t)
+            wide = [table(*mask[1:]) for mask in masks]
 
             def one(i, _):
                 at = [pl.multiple_of(f * pixels + (2 * i + h) * cols, cols) for h in (0, 1)]
@@ -339,11 +347,10 @@
                 weight = softmax_window(top, cols)
                 held = [w * t for w, t in zip(weight, top)]
                 for k in range(TASKS):
-                    sl, scale, shift = wide[k]
+                    scale, shift = wide[k]
                     total = None
                     for h in (0, 1):
-                        mask = sigmoid(wide_ref[pl.ds(at[h], cols), sl] * scale + shift)
-                        term = mask * held[h]
+                        term = sigmoid(masks[k][0][pl.ds(at[h], cols), lanes] * scale + shift) * held[h]
                         total = term if total is None else total + term
                     scr_ref[k] = total
                     even = scr_ref[k, pl.ds(0, cols // 2, stride=2), :]
@@ -354,11 +361,11 @@
             lax.fori_loop(0, rows // 2, one, 0, unroll=2)
 
 
-def task_layer(geom, domain, top, top_st, wide, wide_st, gain_t, bias_t, gain_w, bias_w):
+def task_layer(geom, domain, top, top_st, gain_t, bias_t, masks):
     frames, rows, cols, _ = geom
     pix, chans = top.shape
     task_shape = (frames, rows // 2, TASKS, cols // 2, chans)
-    args = (domain, top, top_st, wide, wide_st, gain_t, bias_t, gain_w, bias_w)
+    args = (domain, top, top_st, gain_t, bias_t, *(x for mask in masks for x in mask))
     return pl.pallas_call(
         functools.partial(task_kernel, geom),
         in_specs=[SCALARS] + [whole(x.shape) for x in args[1:]],
@@ -366,77 +373,61 @@
         out_shape=sds(task_shape, F32),
         scratch_shapes=[pltpu.VMEM((TASKS, cols, LANES), F32)],
         compiler_params=params(),
-        cost_estimate=pl.CostEstimate(flops=pix * chans * 60, bytes_accessed=pix * chans * 28, transcendentals=pix * chans * 5),
+        cost_estimate=cost(pix * chans * 60, pix * chans * 28),
     )(*args)
 
 
-def pool_early_kernel(geom, domain_ref, top_ref, top_st, wide_ref, wide_st, gain_t, bias_t, gain_w, bias_w, cot_ref,
-                      mix_ref, gw_ref, sums_ref, scr_ref):
+def pool_early_kernel(geom, first, domain_ref, top_ref, top_st, gain_t, bias_t, wide_ref, wide_st, gain_w, bias_w, cot_ref, *refs):
     frames, rows, cols, counts = geom
     pixels = rows * cols
-    chans = top_ref.shape[-1]
-    for lane in range(0, chans, LANES):
+    mix_ref, gw_ref, sums_ref, scr_ref = refs[-4:]
+    for lane in range(0, top_ref.shape[-1], LANES):
         lanes = slice(lane, lane + LANES)
         sums = []
         for f in range(frames):
             average, inverse = frame_tables(top_st[:, lanes], domain_ref[f], counts)
             t_scale = inverse * gain_t[:, lanes]
             t_shift = bias_t[:, lanes] - average * t_scale
-            wide = []
-            for k in range(TASKS):
-                sl = slice(k * chans + lane, k * chans + lane + LANES)
-                wide.append((sl, *frame_tables(wide_st[:, sl], domain_ref[f], counts)))
+            w_mean, w_inv = frame_tables(wide_st[:, lanes], domain_ref[f], counts)
 
             def one(i, carry):
                 at = [pl.multiple_of(f * pixels + (2 * i + h) * cols, cols) for h in (0, 1)]
-                top = []
+                top = top_rows(top_ref, at, cols, lanes, t_scale, t_shift)
+                weight = softmax_window(top, cols)
+                cot = spread_cols(scr_ref, cot_ref[f, i, :, lanes].astype(F32))
+                one_sum, two_sum = carry
                 for h in (0, 1):
-                    act = top_ref[pl.ds(at[h], cols), lanes] * t_scale + t_shift
-                    top.append(act * sigmoid(act))
-                weight = softmax_window(top, cols)
-                held = [w * t for w, t in zip(weight, top)]
-                mix = [None, None]
-                new = []
-                for k in range(TASKS):
-                    sl, average, inverse = wide[k]
-                    cot = spread_cols(scr_ref, cot_ref[f, i, k, :, lanes].astype(F32))
-                    one_sum, two_sum = carry[2 * k], carry[2 * k + 1]
-                    for h in (0, 1):
-                        xhat = (wide_ref[pl.ds(at[h], cols), sl] - average) * inverse
-                        mask = sigmoid(xhat * gain_w[:, sl] + bias_w[:, sl])
-                        part = cot * mask
-                        mix[h] = part if mix[h] is None else mix[h] + part
-                        g = part * held[h] * (1.0 - mask)
-                        gw_ref[pl.ds(at[h], cols), sl] = g
-                        one_sum = one_sum + fold(g)
-                        two_sum = two_sum + fold(g * xhat)
-                    new += [one_sum, two_sum]
-                for h in (0, 1):
-                    mix_ref[pl.ds(at[h], cols), lanes] = mix[h]
-                return tuple(new)
+                    xhat = (wide_ref[pl.ds(at[h], cols), lanes] - w_mean) * w_inv
+                    mask = sigmoid(xhat * gain_w[:, lanes] + bias_w[:, lanes])
+                    part = cot * mask
+                    mix = part if first else refs[0][pl.ds(at[h], cols), lanes] + part
+                    mix_ref[pl.ds(at[h], cols), lanes] = mix
+                    g = part * (weight[h] * top[h]) * (1.0 - mask)
+                    gw_ref[pl.ds(at[h], cols), lanes] = g
+                    one_sum = one_sum + fold(g)
+                    two_sum = two_sum + fold(g * xhat)
+                return one_sum, two_sum
 
             zero = jnp.zeros((8, LANES), F32)
-            sums.append(lax.fori_loop(0, rows // 2, one, (zero,) * (2 * TASKS)))
-        for k in range(TASKS):
-            first = [jnp.sum(s[2 * k], 0, keepdims=True) for s in sums]
-            second = [jnp.sum(s[2 * k + 1], 0, keepdims=True) for s in sums]
-            sl = slice(k * chans + lane, k * chans + lane + LANES)
-            sums_ref[:, sl] = by_domain(first, second, domain_ref)
-
-
-def pool_early(geom, domain, top, top_st, wide, wide_st, gain_t, bias_t, gain_w, bias_w, cot):
-    _, _, cols, _ = geom
+            sums.append(lax.fori_loop(0, rows // 2, one, (zero, zero), unroll=2))
+        sums_ref[:, lanes] = by_domain(
+            [jnp.sum(s[0], 0, keepdims=True) for s in sums], [jnp.sum(s[1], 0, keepdims=True) for s in sums], domain_ref
+        )
+
+
+def pool_early(geom, domain, _, top_st, gain_t, bias_t, wide, wide_st, gain_w, bias_w, cot, top, mix=None):
+    cols = geom[2]
     pix, chans = top.shape
-    args = (domain, top, top_st, wide, wide_st, gain_t, bias_t, gain_w, bias_w, cot)
-    outs = [sds((pix, chans), F32), sds((pix, TASKS * chans), F32), sds((4, TASKS * chans), F32)]
+    args = (domain, top, top_st, gain_t, bias_t, wide, wide_st, gain_w, bias_w, cot) + (() if mix is None else (mix,))
+    outs = [sds((pix, chans), F32)] * 2 + [sds((4, chans), F32)]
     return pl.pallas_call(
-        functools.partial(pool_early_kernel, geom),
+        functools.partial(pool_early_kernel, geom, mix is None),
         in_specs=[SCALARS] + [whole(x.shape) for x in args[1:]],
         out_specs=[whole(o.shape) for o in outs],
         out_shape=outs,
         scratch_shapes=[pltpu.VMEM((cols, LANES), F32)],
         compiler_params=params(),
-        cost_estimate=pl.CostEstimate(flops=pix * chans * 90, bytes_accessed=pix * chans * 40, transcendentals=pix * chans * 5),
+        cost_estimate=cost(pix * chans * 40, pix * chans * 20),
     )(*args)
 
 
@@ -499,7 +490,7 @@
         out_specs=[whole(o.shape) for o in outs],
         out_shape=outs,
         compiler_params=params(),
-        cost_estimate=pl.CostEstimate(flops=pix * chans * 80, bytes_accessed=pix * chans * 44, transcendentals=pix * chans * 4),
+        cost_estimate=cost(pix * chans * 80, pix * chans * 44),
     )(*args)
 
 
@@ -619,7 +610,7 @@
     frames, rows, cols, _ = geom
     pix, width = top[0].shape
     chans = kernel.shape[0] // 9
-    args = [domain, *top, kernel]
+    args = [domain, *top, in_hbm(kernel)]
     specs = [SCALARS] + [whole(x.shape) for x in top] + [pl.BlockSpec((3 * chans, width), lambda a: (a, 0))]
     win = (3, frames, rows + 2, cols, width)
     outs = [sds(win, BF16), sds((pix, chans), F32)]
@@ -636,8 +627,71 @@
         out_specs=[whole(o.shape) for o in outs],
         out_shape=outs,
         compiler_params=params(1),
-        cost_estimate=pl.CostEstimate(flops=2 * pix * kernel.size, bytes_accessed=kernel.size * 2 + pix * 10240, transcendentals=0),
+        cost_estimate=cost(2 * pix * kernel.size, kernel.size * 2 + pix * 10240),
     )(*args, *extra)
+
+
+def low_kernel(geom, domain_ref, g_ref, pre_ref, st_ref, sm_ref, gain_ref, win_ref):
+    frames, rows, cols, counts = geom
+    pixels = rows * cols
+    clear_edges(win_ref, rows)
+    for f in range(frames):
+        tables = back_tables(st_ref, sm_ref, gain_ref, domain_ref[f], counts)
+
+        def one_row(r, _):
+            at = pl.multiple_of(f * pixels + r * cols, cols)
+            low = norm_back_rows(g_ref[pl.ds(at, cols), :], pre_ref[pl.ds(at, cols), :], tables)
+            put_windows(win_ref, f, r, low, cols)
+            return 0
+
+        lax.fori_loop(0, rows, one_row, 0, unroll=2)
+
+
+def low_layer(geom, domain, top):
+    frames, rows, cols, _ = geom
+    pix, width = top[0].shape
+    out = sds((3, frames, rows + 2, cols, width), BF16)
+    return pl.pallas_call(
+        functools.partial(low_kernel, geom),
+        grid=(1,),
+        in_specs=[SCALARS] + [whole(x.shape) for x in top],
+        out_specs=whole(out.shape),
+        out_shape=out,
+        compiler_params=params(1),
+        cost_estimate=cost(pix * width * 20, pix * width * 14),
+    )(domain, *top)
+
+
+def input_kernel(geom, win_ref, kernel_ref, out_ref):
+    rows = geom[1]
+    step = pl.program_id(0)
+    chans = kernel_ref.shape[0] // 3
+    source = jnp.concatenate([window(win_ref, 2 - b, 2 - step, rows) for b in range(3)], 1)
+    weight = jnp.concatenate([kernel_ref[b * chans : (b + 1) * chans, :] for b in range(3)], 1)
+    part = lax.dot_general(source, weight, (((1,), (1,)), ((), ())), preferred_element_type=F32)
+
+    @pl.when(step == 0)
+    def _():
+        out_ref[...] = part
+
+    @pl.when(step > 0)
+    def _():
+        out_ref[...] += part
+
+
+def input_layer(geom, win, kernel):
+    frames, rows, cols, _ = geom
+    pix = frames * rows * cols
+    chans, width = kernel.shape[0] // 9, kernel.shape[1]
+    return pl.pallas_call(
+        functools.partial(input_kernel, geom),
+        grid=(3,),
+        in_specs=[whole(win.shape), pl.BlockSpec((3 * chans, width), lambda a: (a, 0))],
+        out_specs=whole((pix, chans)),
+        out_shape=sds((pix, chans), F32),
+        compiler_params=params(1),
+        cost_estimate=cost(2 * pix * kernel.size, kernel.size * 2 + pix * 4096),
+    )(win, in_hbm(kernel))
 
 
 class Member:
@@ -671,7 +725,31 @@
         scratch_shapes=[pltpu.SemaphoreType.DMA],
         grid=(1,),
         compiler_params=params(1),
-        cost_estimate=pl.CostEstimate(flops=0, bytes_accessed=4 * pieces.shape[0] * pieces.shape[1], transcendentals=0),
+        cost_estimate=cost(0, 4 * pieces.shape[0] * pieces.shape[1]),
+    )(pieces.me, *pieces.sources)
+
+
+def affine_kernel(member, parts, me_ref, *refs):
+    out_ref, rows_ref, sem = refs[-3:]
+    fetch(member, parts, me_ref, refs[:-3], rows_ref, sem)
+    arrived(rows_ref, sem)
+    width = out_ref.shape[1] // 32
+    for d in range(32):
+        rows = rows_ref[16 * d : 16 * d + 16].astype(F32)
+        both = jnp.concatenate([rows[:8], rows[8:]], 1)
+        out_ref[:, d * width : (d + 1) * width] = (both[0:2] + both[2:4] + both[4:6])[:, :width]
+
+
+def collect_affine(pieces):
+    return pl.pallas_call(
+        functools.partial(affine_kernel, pieces.member, pieces.parts),
+        in_specs=[SCALARS] + [ANYWHERE] * len(pieces.sources),
+        out_specs=whole((2, 5120)),
+        out_shape=sds((2, 5120), F32),
+        scratch_shapes=[pltpu.VMEM((512, LANES), BF16), pltpu.SemaphoreType.DMA],
+        grid=(1,),
+        compiler_params=params(1),
+        cost_estimate=cost(10000000, 1000000),
     )(pieces.me, *pieces.sources)
 
 
@@ -709,36 +787,21 @@
         out_shape=out,
         scratch_shapes=[pltpu.VMEM((chans, pix), BF16)],
         compiler_params=params(1),
-        cost_estimate=pl.CostEstimate(flops=2 * pix * out.size, bytes_accessed=out.size * 2 + pix * 4096, transcendentals=0),
+        cost_estimate=cost(2 * pix * out.size, out.size * 2 + pix * 4096),
     )(act, low)
 
 
-def weight_blocks_kernel(geom, member, steps, far, aliased, *refs):
+def weight_blocks_kernel(geom, member, steps, held, *refs):
     refs = list(refs)
     me_ref, act_ref, low_ref = (refs.pop(0) for _ in range(3))
-    if aliased:
-        refs.pop(0)
-    outs = [refs.pop(0) for _ in range(3 if far else 1)]
-    scr_ref, tr_ref, sem = refs
+    if held:
+        del refs[:3]
+    near_ref, far_ref, send_ref, scr_ref, tr_ref, sem = refs
     step = pl.program_id(0)
     chans = tr_ref.shape[0]
     for b, part in enumerate(weight_parts(geom, step, act_ref, low_ref, tr_ref)):
         scr_ref[pl.ds(pl.multiple_of(step * 3 * chans, chans) + b * chans, chans), :] = part.astype(BF16)
-
-    def copies(i):
-        if not far:
-            for j in range(4):
-                for at, row, col in member.spots(i, j):
-                    yield scr_ref.at[pl.ds(row, member.vr), pl.ds(col, LANES)], outs[0].at[i * 4 + j, pl.ds(at, member.vr)]
-            return
-        me = me_ref[0]
-        e = i ^ (me >> 2)
-        q = ((e & 1) << 2) | (e & 2) | (e >> 2)
-        for jd in range(4):
-            dst = outs[2].at[jd >> 1, q] if jd & 1 else outs[jd >> 1].at[q]
-            for at, row, col in member.spots(i, (me & 3) ^ jd):
-                yield scr_ref.at[span(row, member.vr), span(col, LANES)], dst.at[pl.ds(at, member.vr)]
-
+    me = me_ref[0]
     share = member.shape[0] // 8
     done = 0
     for s in range(steps):
@@ -747,8 +810,14 @@
         @pl.when(step == s)
         def _(done=done, ready=ready):
             for i in range(done, ready):
-                for src, dst in copies(i):
-                    pltpu.make_async_copy(src, dst, sem).start()
+                e = i ^ (me >> 2)
+                q = ((e & 1) << 2) | (e & 2) | (e >> 2)
+                for jd in range(4):
+                    dst = send_ref.at[jd >> 1, q] if jd & 1 else (near_ref, far_ref)[jd >> 1].at[q]
+                    for at, row, col in member.spots(i, (me & 3) ^ jd):
+                        pltpu.make_async_copy(
+                            scr_ref.at[span(row, member.vr), span(col, LANES)], dst.at[pl.ds(at, member.vr)], sem
+                        ).start()
 
         done = ready
 
@@ -757,26 +826,84 @@
         pltpu.make_async_copy(scr_ref, scr_ref, sem).wait()
 
 
-def weight_blocks(geom, me, act, low, member, rows, far, buffer=None):
+def weight_blocks(geom, me, act, low, member, rows, held=None):
     pix, chans = act.shape
     win = low.ndim == 5
     steps = 3 if win else 1
     shard = (rows, LANES)
-    outs = [sds((8, *shard), BF16)] * 2 + [sds((2, 8, *shard), BF16)] if far else [sds((32, *shard), BF16)]
-    args = [me, act, low] + ([] if buffer is None else [buffer])
+    outs = [pltpu.HBM((8, *shard), BF16)] * 2 + [pltpu.HBM((2, 8, *shard), BF16)]
+    args = [me, act, low] + [in_hbm(x) for x in held or ()]
     size = member.shape[0] * member.shape[1]
-    got = pl.pallas_call(
-        functools.partial(weight_blocks_kernel, geom, member, steps, far, buffer is not None),
+    return pl.pallas_call(
+        functools.partial(weight_blocks_kernel, geom, member, steps, held is not None),
         grid=(steps,),
-        in_specs=[SCALARS, whole(act.shape), whole(low.shape)] + [ANYWHERE] * (buffer is not None),
-        out_specs=[ANYWHERE] * len(outs),
+        in_specs=[SCALARS, whole(act.shape), whole(low.shape)] + [ANYWHERE] * len(held or ()),
+        out_specs=[ANYWHERE] * 3,
         out_shape=outs,
         scratch_shapes=[pltpu.VMEM(member.shape, BF16), pltpu.VMEM((chans, pix), BF16), pltpu.SemaphoreType.DMA],
-        input_output_aliases={} if buffer is None else {3: 0},
+        input_output_aliases={} if held is None else {3: 0, 4: 1, 5: 2},
         compiler_params=params(1),
-        cost_estimate=pl.CostEstimate(flops=2 * pix * size, bytes_accessed=size * 2 + pix * 4096, transcendentals=0),
+        cost_estimate=cost(2 * pix * size, size * 2 + pix * 4096),
     )(*args)
-    return got if far else got[0]
+
+
+def weight_piece_kernel(geom, member, step, held, *refs):
+    rows = geom[1]
+    refs = list(refs)
+    me_ref, act_ref, low_ref = (refs.pop(0) for _ in range(3))
+    if held:
+        del refs[:3]
+    near_ref, far_ref, send_ref = (refs.pop(0) for _ in range(3))
+    if step == 0:
+        tr_ref = refs.pop(0)
+        tr_ref[...] = act_ref[...].astype(F32).T.astype(BF16)
+    else:
+        tr_ref = act_ref
+    scr_ref, sem = refs
+    chans = tr_ref.shape[0]
+    for b in range(3):
+        part = jnp.dot(tr_ref[...], window(low_ref, 2 - b, 2 - step, rows), preferred_element_type=F32)
+        scr_ref[b * chans : (b + 1) * chans, :] = part.astype(BF16)
+    me = me_ref[0]
+    start, stop = 3 * chans * step, 3 * chans * (step + 1)
+    for i in range(8):
+        first, last = max(start, i * member.vr), min(stop, (i + 1) * member.vr)
+        if first >= last:
+            continue
+        e = i ^ (me >> 2)
+        q = ((e & 1) << 2) | (e & 2) | (e >> 2)
+        for jd in range(4):
+            dst = send_ref.at[jd >> 1, q] if jd & 1 else (near_ref, far_ref)[jd >> 1].at[q]
+            col = ((me & 3) ^ jd) * LANES
+            pltpu.make_async_copy(
+                scr_ref.at[pl.ds(first - start, last - first), span(col, LANES)],
+                dst.at[pl.ds(member.at + first - i * member.vr, last - first)],
+                sem,
+            ).start()
+    arrived(scr_ref, sem)
+
+
+def weight_piece(geom, me, act, low, member, rows, step, held=None):
+    chans = member.shape[0] // 9
+    pix, width = low.shape[1] * geom[1] * geom[2], low.shape[-1]
+    shard = (rows, LANES)
+    outs = [pltpu.HBM((8, *shard), BF16)] * 2 + [pltpu.HBM((2, 8, *shard), BF16)]
+    out_specs = [ANYWHERE] * 3
+    if step == 0:
+        outs.append(sds((chans, pix), BF16))
+        out_specs.append(whole((chans, pix)))
+    args = [me, act, low] + [in_hbm(x) for x in held or ()]
+    return pl.pallas_call(
+        functools.partial(weight_piece_kernel, geom, member, step, held is not None),
+        grid=(1,),
+        in_specs=[SCALARS, whole(act.shape), whole(low.shape)] + [ANYWHERE] * len(held or ()),
+        out_specs=out_specs,
+        out_shape=outs,
+        scratch_shapes=[pltpu.VMEM((3 * chans, width), BF16), pltpu.SemaphoreType.DMA],
+        input_output_aliases={} if held is None else {3: 0, 4: 1, 5: 2},
+        compiler_params=params(1),
+        cost_estimate=cost(2 * pix * 3 * chans * width, chans * width * 6),
+    )(*args)
 
 
 def point_kernel(geom, pieces, *refs):
@@ -813,13 +940,14 @@
         scratch_shapes=[pltpu.SemaphoreType.DMA] * pieces,
         grid=(1,),
         compiler_params=params(1),
-        cost_estimate=pl.CostEstimate(flops=2 * pix * chans * width, bytes_accessed=chans * width * 2 + pix * width * 4, transcendentals=0),
+        cost_estimate=cost(2 * pix * chans * width, chans * width * 2 + pix * width * 4),
     )(*args)
 
 
-def point_back_kernel(geom, domain_ref, g_ref, pre_ref, st_ref, sm_ref, gain_ref, mat_ref, low_ref, out_ref):
+def point_back_kernel(geom, added, domain_ref, g_ref, pre_ref, st_ref, sm_ref, gain_ref, mat_ref, *refs):
     frames, rows, cols, counts = geom
     pixels = rows * cols
+    low_ref, out_ref = refs[-2:]
     for f in range(frames):
         tables = back_tables(st_ref, sm_ref, gain_ref, domain_ref[f], counts)
 
@@ -831,39 +959,28 @@
 
         lax.fori_loop(0, rows, one_row, 0, unroll=2)
     part = lax.dot_general(low_ref[...], mat_ref[...], (((1,), (1,)), ((), ())), preferred_element_type=F32)
-
-    @pl.when(pl.program_id(0) == 0)
-    def _():
-        out_ref[...] = part
-
-    @pl.when(pl.program_id(0) > 0)
-    def _():
-        out_ref[...] += part
-
-
-def point_back(geom, domain, g, pre, stats, sums, gain, mat):
+    out_ref[...] = part + refs[0][...] if added else part
+
+
+def point_back(geom, domain, g, pre, stats, sums, gain, mat, added=None):
     pix, width = g.shape
     chans = mat.shape[0]
-    block = min(width, 512)
-    while width % block:
-        block -= 256
-    col = lambda n: (0, n)
-    specs = [SCALARS, pl.BlockSpec((pix, block), col), pl.BlockSpec((pix, block), col)]
-    specs += [pl.BlockSpec((4, block), col)] * 2 + [pl.BlockSpec((1, block), col), pl.BlockSpec((chans, block), col)]
+    args = (domain, g, pre, stats, sums, gain, mat) + (() if added is None else (added,))
     outs = [sds((pix, width), BF16), sds((pix, chans), F32)]
     return pl.pallas_call(
-        functools.partial(point_back_kernel, geom),
-        grid=(width // block,),
-        in_specs=specs,
-        out_specs=[pl.BlockSpec((pix, block), col), whole((pix, chans))],
+        functools.partial(point_back_kernel, geom, added is not None),
+        grid=(1,),
+        in_specs=[SCALARS] + [whole(x.shape) for x in args[1:]],
+        out_specs=[whole(o.shape) for o in outs],
         out_shape=outs,
         compiler_params=params(1),
-        cost_estimate=pl.CostEstimate(flops=2 * pix * mat.size, bytes_accessed=mat.size * 2 + pix * width * 10, transcendentals=0),
-    )(domain, g, pre, stats, sums, gain, mat)
+        cost_estimate=cost(2 * pix * mat.size, mat.size * 2 + pix * width * 10),
+    )(*args)
 
 
 AXES = ("dp", "fsdp")
 CORE, X, Y, Z_NEAR, Z_FAR = range(5)
+ORDER = (CORE, Z_NEAR, Z_FAR, X, Y)
 
 
 def swap(x, bit):
@@ -880,7 +997,7 @@
 
 
 def tied(value, to):
-    return lax.optimization_barrier((value, to))[0]
+    return value if to is None else lax.optimization_barrier((value, to))[0]
 
 
 class Links:
@@ -890,13 +1007,20 @@
     def busy(self, bit, *values):
         self.under_way.setdefault(bit, []).extend(values)
 
-    def total(self, x, after=None):
-        for bit in all_bits():
+    def total(self, x, after=None, order=None, fill=()):
+        bits = order if order and len(all_bits()) == 5 else all_bits()
+        fill = list(fill)
+        for bit in bits:
             for value in self.under_way.pop(bit, ()):
                 x = tied(x, value)
-            x = x + swap(x, bit)
+            got = swap(x, bit)
+            if fill and (bit != CORE or len(bits) != 5):
+                got = tied(got, fill.pop(0)(x))
+            x = x + got
             for start in (after or {}).get(bit, ()):
                 start(x)
+        for work in fill:
+            work(x)
         return x
 
 
@@ -907,37 +1031,39 @@
 class Gather:
     def __init__(self, links, shard):
         self.links, self.shard, self.cut = links, shard, half_rows(shard.shape[0])
+        self.sources = None
 
     def far(self, to=None):
-        self.z = self.shard if to is None else tied(self.shard, to)
-        self.seen = swap(self.z, Z_FAR)
+        self.z = tied(self.shard, to)
+        self.got = swap(self.z, Z_FAR)
 
     def near(self, to=None):
-        z = jnp.stack([self.z, self.seen])
-        z = z if to is None else tied(z, to)
-        self.seen = swap(z, Z_NEAR)
-        z = jnp.concatenate([z, self.seen])
+        self.z = jnp.stack(tied((self.z, self.got), to))
+        self.got = swap(self.z, Z_NEAR)
+
+    def first(self, to=None):
+        z = jnp.concatenate(tied((self.z, self.got), to))
         self.a, self.b = z[:, : self.cut], z[:, self.cut :]
-
-    def first(self, to=None):
-        a, b = (self.a, self.b) if to is None else (tied(self.a, to), tied(self.b, to))
-        self.seen = swap(a, Y), swap(b, X)
-        self.a, self.b = jnp.concatenate([a, self.seen[0]]), jnp.concatenate([b, self.seen[1]])
+        self.got = swap(self.a, Y), swap(self.b, X)
 
     def second(self, to=None):
-        a, b = (self.a, self.b) if to is None else (tied(self.a, to), tied(self.b, to))
-        self.seen = swap(a, X), swap(b, Y)
-        self.held = [a, self.seen[0], b, self.seen[1]]
+        a, b, (got_a, got_b) = tied((self.a, self.b, self.got), to)
+        self.a, self.b = jnp.concatenate([a, got_a]), jnp.concatenate([b, got_b])
+        self.got = swap(self.a, X), swap(self.b, Y)
 
     def busy(self):
-        self.links.busy(X, self.seen[0])
-        self.links.busy(Y, self.seen[1])
+        if isinstance(self.got, tuple):
+            self.links.busy(X, self.got[0])
+            self.links.busy(Y, self.got[1])
+        else:
+            self.links.busy(CORE, self.got)
 
     def finish(self, to=None):
         rows = self.shard.shape[0]
+        self.a, self.b, self.got = tied((self.a, self.b, self.got), to)
         self.sources, self.parts = [], []
         for core in (0, 1):
-            for n, value in enumerate(self.held):
+            for n, value in enumerate((self.a, self.got[0], self.b, self.got[1])):
                 z = [8 * (k >> 1) + 16 * (k & 1) for k in range(4)]
                 if n < 2:
                     masks = [core + 2 * n + 4 * y + m for y in (0, 1) for m in z]
@@ -961,40 +1087,48 @@
 class Scatter:
     def __init__(self, links, blocks):
         self.links = links
-        near, far, send = blocks
-        self.cut = half_rows(near.shape[1])
-        got = swap(send, CORE)
+        self.near_blocks, self.far_blocks, send = blocks
+        self.cut = half_rows(self.near_blocks.shape[1])
+        self.got = swap(send, CORE)
+
+    def first(self, to=None):
         cut = self.cut
-        self.a = [plus(near[:, :cut], got[0, :, :cut]), plus(far[:, :cut], got[1, :, :cut])]
-        self.b = [
+        near, far, got = tied((self.near_blocks, self.far_blocks, self.got), to)
+        self.a, send_a = plus(near[:, :cut], got[0, :, :cut]), plus(far[:, :cut], got[1, :, :cut])
+        self.b, send_b = (
             jnp.stack([plus(near[s, cut:], got[0, s, cut:]), plus(far[s, cut:], got[1, s, cut:])])
             for s in (slice(0, 4), slice(4, 8))
-        ]
-
-    def first(self, to=None):
-        send_a, send_b = self.a[1], self.b[1]
-        if to is not None:
-            send_a, send_b = tied(send_a, to), tied(send_b, to)
-        got_a, got_b = swap(send_a, X), swap(send_b, Y)
-        self.a = [plus(self.a[0][:4], got_a[:4]), plus(self.a[0][4:], got_a[4:])]
-        self.b = [plus(self.b[0][0], got_b[0]), plus(self.b[0][1], got_b[1])]
-
-    def second(self):
-        got_a, got_b = swap(self.a[1], Y), swap(self.b[1], X)
-        self.links.busy(Y, got_a)
-        self.links.busy(X, got_b)
-        self.z = [
-            jnp.concatenate([plus(self.a[0][s], got_a[s]), plus(self.b[0][s], got_b[s])], 1)
-            for s in (slice(0, 2), slice(2, 4))
-        ]
-
-    def along_z(self, to=None):
-        send = self.z[1] if to is None else tied(self.z[1], to)
-        got = swap(send, Z_NEAR)
-        keep, send = plus(self.z[0][0], got[0]), plus(self.z[0][1], got[1])
-        got = swap(send, Z_FAR)
-        self.links.busy(Z_NEAR, got)
-        self.out = keep.astype(F32) + got.astype(F32)
+        )
+        self.got = swap(send_a, X), swap(send_b, Y)
+
+    def second(self, to=None):
+        a, b, (got_a, got_b) = tied((self.a, self.b, self.got), to)
+        self.a, self.b = plus(a[:4], got_a[:4]), plus(b[0], got_b[0])
+        self.got = swap(plus(a[4:], got_a[4:]), Y), swap(plus(b[1], got_b[1]), X)
+
+    def near_sums(self, to=None):
+        a, b, (got_a, got_b) = tied((self.a, self.b, self.got), to)
+        self.z, self.send = (
+            jnp.concatenate([plus(a[s], got_a[s]), plus(b[s], got_b[s])], 1) for s in (slice(0, 2), slice(2, 4))
+        )
+
+    def near(self, to=None):
+        self.got = swap(tied(self.send, to), Z_NEAR)
+
+    def far(self, to=None):
+        z, got = tied((self.z, self.got), to)
+        self.z = plus(z[0], got[0])
+        self.got = swap(plus(z[1], got[1]), Z_FAR)
+
+    def finish(self, to=None):
+        z, got = tied((self.z, self.got), to)
+        self.out = z.astype(F32) + got.astype(F32)
+
+    def busy(self):
+        if isinstance(self.got, tuple):
+            self.links.busy(X, *self.got)
+        else:
+            self.links.busy(CORE, self.got)
 
 
 def rows_of_chip(shard):
@@ -1066,22 +1200,39 @@
         self.geom = geom
         self.mats = {name: gather_matrix(w) for name, w in weights.items()}
         self.affine = gather(jnp.stack([gains, biases])).transpose(1, 0, 2).reshape(2, 1, -1)
-        self.grads = {}
+        self.grads, self.ready = {}, None
 
     def get(self, name):
         return self.mats[name]
 
+    def whole(self, name):
+        return self.mats[name]
+
     def put(self, name, matrix):
         pass
 
+    def layer_done(self, n, local):
+        pass
+
     def during(self, point):
         return {}
 
     def add(self, name, act, low):
-        self.grads[name] = scatter_matrix(weight_layer(self.geom, act, low))
-
-    def step(self, point, value=None):
+        got = weight_layer(self.geom, act, low)
+        self.grads[name] = scatter_matrix(got)
+        return got
+
+    def pieces(self, name, act, low):
+        return [lambda x: self.add(name, act, low)]
+
+    def send(self, n):
         pass
+
+    def after_layer(self, n, local):
+        pass
+
+    def tail(self, blocks, kernels):
+        return [kernel(None) for kernel in kernels]
 
 
 class ThisMesh:
@@ -1090,100 +1241,166 @@
         self.me = number(1)
         sizes = (8, 4)
         full = {n: (w.shape[0] * 8, w.shape[1] * 4) for n, w in weights.items()}
-        at, packed, self.rest = 0, [], {}
-        for name in ("six", "gating", "attend", "five", "four"):
-            split = name in ("six", "gating")
-            member = Member(at, full[name], *sizes, split=split)
-            packed.append(pack(rows_of_chip(weights[name]) if split else weights[name]))
-            self.rest[name] = member
-            at += member.rows
-        self.rest_rows = at
-        self.rest_packed = jnp.concatenate(packed)
-        self.lone = {n: Member(0, full[n], *sizes) for n in ("one", "two", "three")}
-        affine = in_three(jnp.stack([gains, biases])).reshape(-1)
-        affine = jnp.pad(affine, (0, 2048 - affine.shape[0])).reshape(16, LANES)
-        two = self.lone["two"].rows
-        self.g1 = Gather(links, weights["one"])
-        self.g2 = Gather(links, jnp.concatenate([weights["two"], affine]))
-        self.g3 = Gather(links, weights["three"])
-        g1, g2, g3 = self.g1, self.g2, self.g3
+        splits = ("six", "gating")
+        g1 = Gather(links, weights["one"])
         g1.far()
+        packed = {n: pack(rows_of_chip(tied(w, g1.got)) if n in splits else w) for n, w in weights.items()}
+        gains, biases = tied((gains, biases), g1.got)
+        affine = in_three(jnp.stack([gains, biases])).reshape(6, -1)
+        affine = jnp.pad(affine, ((0, 2), (0, 2 * LANES - affine.shape[1])))
+        affine = jnp.concatenate([affine[:, :LANES], affine[:, LANES:]])
+        groups = (("one",), ("two",), ("three",), ("four",), ("five",), ("six", "gating", "attend"))
+        self.g, self.members, self.group = [], {}, {}
+        for names in groups:
+            at = 0
+            for name in names:
+                self.members[name] = Member(at, full[name], *sizes, split=name in splits)
+                at += self.members[name].rows
+            if names == ("one",):
+                group = g1
+            else:
+                group = Gather(links, jnp.concatenate([packed[n] for n in names] + [affine] * (names == ("two",))))
+            self.g.append(group)
+            self.group.update((n, group) for n in names)
+        g2 = self.g[1]
         g1.near()
-        g2.far(g1.seen)
+        g2.far(g1.got)
         g1.first()
-        g2.near(g1.seen)
+        g2.near(g1.got)
         g1.second()
         g1.finish()
-        g3.far(g2.seen)
-        g2.first(g1.seen)
-        self.shards = lax.all_gather(tied(self.rest_packed, g1.seen), AXES)
-        g3.near(g2.seen)
-        g2.second()
-        g2.busy()
-        self.mats = {"one": g1.pieces(self.lone["one"])}
-        self.grads, self.buffer, self.pending = {}, None, {}
+        self.g[2].far(g2.got)
+        g2.first(g1.got)
+        self.ready = self.g[5].shard
+        self.mats = {}
+        self.grads, self.blocks, self.sums = {}, {}, {}
+        self.homes, self.rows = {}, {}
+        for names in (("six", "gating"), ("five",), ("four",), ("three", "attend"), ("two",), ("one",)):
+            at = 0
+            for name in names:
+                self.homes[name] = Member(at, full[name], *sizes, split=name in splits)
+                at += self.homes[name].rows
+            self.rows.update((name, at) for name in names)
+
+    def layer_done(self, n, local):
+        if n < 6:
+            self.g[n].second((local, self.g[n + 1].got) if n < 5 else local)
+            self.g[n].busy()
 
     def get(self, name):
         if name in self.mats:
             return self.mats[name]
+        group = self.group[name]
+        self.mats[name] = group.pieces(self.members[name])
         if name == "two":
-            self.g2.finish()
-            rows = self.lone["two"].rows
-            self.mats[name] = self.g2.pieces(self.lone["two"])
-            flat = collect(self.g2.pieces(FlatMember(rows, 16)))
-            parts = flat.reshape(32, 2048)[:, :960].astype(F32).reshape(32, 3, 2, 160)
-            self.affine = (parts[:, 0] + parts[:, 1] + parts[:, 2]).transpose(1, 0, 2).reshape(2, 1, -1)
-        elif name == "three":
-            self.g3.finish()
-            self.mats[name] = self.g3.pieces(self.lone["three"])
-        else:
-            self.mats[name] = Pieces(self.rest[name], [(0, self.rest_rows, None)], self.me, [self.shards])
+            self.affine = collect_affine(group.pieces(FlatMember(self.members["two"].rows, 16)))[:, None]
+        return self.mats[name]
+
+    def whole(self, name):
+        self.mats[name] = collect(self.get(name))
         return self.mats[name]
 
     def put(self, name, matrix):
         self.mats[name] = matrix
 
     def during(self, point):
-        if point == 1:
-
-            def start(x):
-                self.g3.first(x)
-                self.g3.second()
-                self.g3.busy()
-
-            return {Y: [start]}
-        if point == 12 and "three" in self.pending:
-
-            def start(x):
-                self.pending["three"].first(x)
-                self.pending["three"].second()
-
-            return {Y: [start]}
-        return {}
+        if point <= 5:
+
+            def x_done(x):
+                self.g[point].finish(x)
+
+            if point == 5:
+                return {X: [x_done]}
+            group = self.g[point + 1]
+
+            def z_done(x):
+                group.near(x)
+
+            def y_done(x):
+                group.first(x)
+                if point < 4:
+                    self.g[point + 2].far(x)
+
+            return {Z_FAR: [z_done], X: [x_done], Y: [y_done]}
+        n = 14 - point
+
+        def z_done(x):
+            self.sums[n + 2].near(x)
+
+        def y_done(x):
+            self.sums[n + 1].second(x)
+            if n < 5:
+                self.sums[n + 2].far(x)
+
+        return {Y: [y_done], Z_FAR: [z_done] if n < 5 else []}
 
     def add(self, name, act, low):
-        if name in self.rest:
-            self.buffer = weight_blocks(self.geom, self.me, act, low, self.rest[name], self.rest_rows, False, self.buffer)
-            if name == "four":
-                out = lax.psum_scatter(self.buffer, AXES, tiled=False)
-                for n, m in self.rest.items():
-                    value = unpack(out[m.at : m.at + m.rows], m.blocks)
-                    self.grads[n] = (columns_of_core(value) if m.split else value).astype(F32)
-        else:
-            m = self.lone[name]
-            blocks = weight_blocks(self.geom, self.me, act, low, m, m.rows, True)
-            self.pending[name] = Scatter(self.links, blocks)
-
-    def step(self, point, value=None):
-        if point == "last":
-            for name in ("two", "one"):
-                s = self.pending[name]
-                s.first()
-                s.second()
-            for name in ("three", "two", "one"):
-                s = self.pending[name]
-                s.along_z()
-                self.grads[name] = s.out
+        n = NUMBER[name]
+        self.blocks[n] = weight_blocks(
+            self.geom, self.me, act, low, self.homes[name], self.rows[name], self.blocks.get(n)
+        )
+        return self.blocks[n][0]
+
+    def pieces(self, name, act, low):
+        def piece(step):
+            def work(x):
+                n = NUMBER[name]
+                if step == 0:
+                    *self.blocks[n], self.turned = weight_piece(
+                        self.geom, self.me, tied(act, x), low, self.homes[name], self.rows[name], 0
+                    )
+                else:
+                    self.blocks[n] = weight_piece(
+                        self.geom, self.me, tied(self.turned, x), low, self.homes[name], self.rows[name], step, self.blocks[n]
+                    )
+                return self.blocks[n][0]
+
+            return work
+
+        return [piece(step) for step in range(3)]
+
+    def send(self, n):
+        self.sums[n] = Scatter(self.links, self.blocks[n])
+
+    def after_layer(self, n, local):
+        if n < 4:
+            self.sums[n + 3].finish(local)
+            local = (local, self.sums[n + 3].out)
+        if n < 5:
+            self.sums[n + 2].near_sums(local)
+            local = self.sums[n + 2].send
+        self.sums[n + 1].first(local)
+        self.sums[n + 1].busy()
+
+    def tail(self, blocks, kernels):
+        self.send(1)
+        one, two, three, four = (self.sums[n] for n in (1, 2, 3, 4))
+        four.finish(blocks)
+        two.first((blocks, four.out))
+        three.near_sums(two.b)
+        three.near(two.b)
+        outs = [kernels[0]((two.b, three.z))]
+        one.first(outs[0])
+        three.far(one.b)
+        outs.append(kernels[1]((one.b, three.z)))
+        two.second(outs[1])
+        one.second(two.b)
+        three.finish(two.b)
+        two.near_sums((one.b, three.out))
+        two.near()
+        one.near_sums(two.z)
+        one.near()
+        two.far(one.z)
+        one.far(two.z)
+        two.finish(one.z)
+        one.finish()
+        for name, m in self.homes.items():
+            out = unpack(self.sums[NUMBER[name]].out[m.at : m.at + m.rows], m.blocks)
+            self.grads[name] = columns_of_core(out) if m.split else out
+        return outs
+
+
+NUMBER = dict(one=1, two=2, three=3, attend=3, four=4, five=5, six=6, gating=6)
 
 
 class FlatMember:
@@ -1237,8 +1454,9 @@
         w.put(name, got[-1])
         return got[:2]
 
-    pre_1, local = forward("one", source)
-    st_1 = links.total(local, w.during(1))
+    pre_1, local = forward("one", tied(source, w.ready))
+    w.layer_done(1, local)
+    st_1 = links.total(local, w.during(1), ORDER)
     w.get("two")
     widths = (C_MID, C_MID, C_MID, TASKS * C_MID, C_MID, C_MID, C_DEC, TASKS * C_DEC)
     gain, bias, at = [], [], 0
@@ -1247,68 +1465,154 @@
         bias.append(w.affine[1, :, at : at + width])
         at += width
     pre_2, local, act_1 = forward("two", pre_1, (st_1, gain[0], bias[0]))
-    st_2 = links.total(local)
+    w.layer_done(2, local)
+    st_2 = links.total(local, w.during(2), ORDER)
     pre_3, local, act_2 = forward("three", pre_2, (st_2, gain[1], bias[1]))
-    st_3 = links.total(local)
+    w.layer_done(3, local)
+    st_3 = links.total(local, w.during(3), ORDER)
     unpooled = pool_layer(geom, domain, pre_3, st_3, gain[2], bias[2])
     pre_4, local = forward("four", unpooled)
-    st_4 = links.total(local)
+    w.layer_done(4, local)
+    st_4 = links.total(local, w.during(4), ORDER)
     pre_5, local, act_4 = forward("five", pre_4, (st_4, gain[4], bias[4]))
-    st_5 = links.total(local)
+    w.layer_done(5, local)
+    st_5 = links.total(local, w.during(5), ORDER)
     pre_g, local_g = point("gating", act_4)
-    pre_a, local_a = point("attend", act_2)
     pre_6, local, act_5 = forward("six", pre_5, (st_5, gain[5], bias[5]))
-    both = links.total(jnp.concatenate([local, local_g, local_a], 1))
-    st_6, st_g, st_a = both[:, :C_DEC], both[:, C_DEC : 4 * C_DEC], both[:, 4 * C_DEC :]
+    attend = w.whole("attend")
+    wide = []
+
+    def attend_part(k):
+        def work(x):
+            wide.append(point_layer(geom, domain, tied(act_2, x), attend[:, k * C_MID : (k + 1) * C_MID]))
+            return wide[-1][0]
+
+        return work
+
+    both = links.total(jnp.concatenate([local, local_g], 1), None, ORDER, [attend_part(k) for k in range(TASKS)])
+    st_6, st_g = both[:, :C_DEC], both[:, C_DEC:]
+    pre_a = [p for p, _ in wide]
     task_maps, g_6, g_g, local = head_layer(
         geom, domain, pre_6, st_6, pre_g, st_g, gain[6], bias[6], gain[7], bias[7], dec_cot
     )
-    both = links.total(local)
-    sm_6, sm_g = both[:, :C_DEC], both[:, C_DEC:]
-    pool_args = (geom, domain, pre_3, st_3, pre_a, st_a, gain[2], bias[2], gain[3], bias[3])
-    mix, g_a, sums_a = pool_early(*pool_args, enc_cot)
-    task_features = task_layer(*pool_args)
+    out_maps = []
+
+    def place_maps(x):
+        out_maps.append(tied(task_maps, x).transpose(1, 0, 2).reshape(frames, rows, cols, TASKS, C_DEC))
+        return out_maps[0]
+
+    both = links.total(jnp.concatenate([local] + [s for _, s in wide], 1), None, ORDER, [place_maps])
+    sm_6, sm_g, st_a = both[:, :C_DEC], both[:, C_DEC : 4 * C_DEC], both[:, 4 * C_DEC :]
+    st_a = [st_a[:, k * C_MID : (k + 1) * C_MID] for k in range(TASKS)]
+    pool_args = (geom, domain, pre_3, st_3, gain[2], bias[2])
+    masks = [(pre_a[k], st_a[k], gain[3][:, k * C_MID : (k + 1) * C_MID], bias[3][:, k * C_MID : (k + 1) * C_MID]) for k in range(TASKS)]
 
     win_6, g_5, local = backward_layer(
         geom, domain, (g_6, pre_6, st_6, sm_6, gain[6]), w.get("six"), lower=(pre_5, st_5, gain[5], bias[5])
     )
-    both = links.total(jnp.concatenate([local, sums_a], 1))
-    sm_5, sm_a = both[:, :C_MID], both[:, C_MID:]
-    w.add("six", act_5, win_6)
-    low_g, add_4 = point_back(geom, domain, g_g, pre_g, st_g, sm_g, gain[7], w.get("gating"))
-    w.add("gating", act_4, low_g)
+    early, gate_back = [], []
+
+    def early_part(k):
+        def work(x):
+            early.append(pool_early(*pool_args, *masks[k], enc_cot[:, :, k], tied(pre_3, x), early[-1][0] if early else None))
+            return early[-1][0]
+
+        return work
+
+    def gate_part(x):
+        gate_back.extend(point_back(geom, domain, tied(g_g, x), pre_g, st_g, sm_g, gain[7], w.get("gating")))
+        return gate_back[0]
+
+    sm_5 = links.total(
+        local, None, ORDER, [lambda x: w.add("six", act_5, tied(win_6, x)), gate_part, early_part(0), early_part(1)]
+    )
+    early_part(2)(sm_5)
+    mix = early[-1][0]
+    low_g, add_4 = gate_back
+    blocks = w.add("gating", act_4, low_g)
+    w.send(6)
     win_5, g_4, local = backward_layer(
-        geom, domain, (g_5, pre_5, st_5, sm_5, gain[5]), w.get("five"), added=add_4, lower=(pre_4, st_4, gain[4], bias[4])
+        geom,
+        domain,
+        (tied(g_5, blocks), pre_5, st_5, sm_5, gain[5]),
+        w.get("five"),
+        added=add_4,
+        lower=(pre_4, st_4, gain[4], bias[4]),
     )
-    sm_4 = links.total(local)
-    low_a, add_2 = point_back(geom, domain, g_a, pre_a, st_a, sm_a, gain[3], w.get("attend"))
-    w.add("attend", act_2, low_a)
-    w.add("five", act_4, win_5)
+    w.after_layer(5, local)
+    both = links.total(
+        jnp.concatenate([local] + [e[2] for e in early], 1), w.during(9), ORDER, w.pieces("five", act_4, win_5)
+    )
+    w.send(5)
+    sm_4 = both[:, :C_MID]
+    sm_a = [both[:, (k + 1) * C_MID : (k + 2) * C_MID] for k in range(TASKS)]
     win_4, g_3, local = backward_layer(
-        geom, domain, (g_4, pre_4, st_4, sm_4, gain[4]), w.get("four"), lower=(pre_3, st_3, gain[2], bias[2]), mix=mix
+        geom,
+        domain,
+        (g_4, pre_4, st_4, sm_4, gain[4]),
+        w.get("four"),
+        lower=(pre_3, st_3, gain[2], bias[2]),
+        mix=mix,
     )
-    sm_3 = links.total(local)
-    w.add("four", unpooled, win_4)
+    w.after_layer(4, local)
+    backs = []
+
+    def attend_back(k):
+        def work(x):
+            backs.append(
+                point_back(
+                    geom, domain, tied(early[k][1], x), pre_a[k], st_a[k], sm_a[k], masks[k][2],
+                    attend[:, k * C_MID : (k + 1) * C_MID], backs[-1][1] if backs else None,
+                )
+            )
+            return backs[-1][1]
+
+        return work
+
+    sm_3 = links.total(local, w.during(10), ORDER, w.pieces("four", unpooled, win_4) + [attend_back(0)])
+    w.send(4)
+    attend_back(1)(sm_3)
+    attend_back(2)(backs[-1][1])
+    low_a = jnp.concatenate([low for low, _ in backs], 1)
     win_3, g_2, local = backward_layer(
-        geom, domain, (g_3, pre_3, st_3, sm_3, gain[2]), w.get("three"), added=add_2, lower=(pre_2, st_2, gain[1], bias[1])
+        geom,
+        domain,
+        (g_3, pre_3, st_3, sm_3, gain[2]),
+        w.get("three"),
+        added=backs[-1][1],
+        lower=(pre_2, st_2, gain[1], bias[1]),
     )
-    sm_2 = links.total(local)
-    w.add("three", act_2, win_3)
+    w.after_layer(3, local)
+    sm_2 = links.total(
+        local, w.during(11), ORDER, w.pieces("three", act_2, win_3) + [lambda x: w.add("attend", act_2, tied(low_a, x))]
+    )
+    w.send(3)
     win_2, g_1, local = backward_layer(
-        geom, domain, (g_2, pre_2, st_2, sm_2, gain[1]), w.get("two"), lower=(pre_1, st_1, gain[0], bias[0])
+        geom,
+        domain,
+        (g_2, pre_2, st_2, sm_2, gain[1]),
+        w.get("two"),
+        lower=(pre_1, st_1, gain[0], bias[0]),
     )
-    sm_1 = links.total(local, w.during(12))
-    w.add("two", act_1, win_2)
-    win_1, frames_grad = backward_layer(geom, domain, (g_1, pre_1, st_1, sm_1, gain[0]), w.get("one"))
-    w.add("one", source, win_1)
-    w.step("last")
-
-    sums = jnp.concatenate([sm_1, sm_2, sm_3, sm_a, sm_4, sm_5, sm_6, sm_g], 1)
+    w.after_layer(2, local)
+    sm_1 = links.total(local, w.during(12), ORDER, w.pieces("two", act_1, win_2))
+    w.send(2)
+    win_1 = low_layer(geom, domain, (g_1, pre_1, st_1, sm_1, gain[0]))
+    blocks = w.add("one", source, win_1)
+    frames_grad, task_features = w.tail(
+        blocks,
+        (
+            lambda to: input_layer(geom, tied(win_1, to), w.get("one")),
+            lambda to: task_layer(geom, domain, tied(pre_3, to), *pool_args[3:], masks),
+        ),
+    )
+
+    sums = jnp.concatenate([sm_1, sm_2, sm_3, *sm_a, sm_4, sm_5, sm_6, sm_g], 1)
     shard = gains.shape[0]
     mine = lax.dynamic_slice_in_dim(sums, lax.axis_index(AXES) * shard, shard, 1)
     return (
         task_features.transpose(0, 1, 3, 2, 4),
-        task_maps.transpose(1, 0, 2).reshape(frames, rows, cols, TASKS, C_DEC),
+        out_maps[0],
         frames_grad.reshape(frames, rows, cols, C_IN),
         *(w.grads[n] for n in ("one", "two", "three", "attend", "four", "five", "six", "gating")),
         mine[2] + mine[3],

time: 716 us -> 584 us (0.82)
  waiting for transfers between devices: 241 us -> 162 us
  Pallas kernels: 281 us -> 204 us
  starting transfers between devices: 127 us -> 148 us
  between operations: 15.6 us -> 3.88 us
    ppermute x115 -> x166, waiting for transfers between devices: 241 us -> 162 us  [swap(): return lax.ppermute(x, AXES, [(i, i ^ 1 << bit) for i in range(n)])]
    pallas_call x8 -> x4, Pallas kernels: 59.8 us -> 13.7 us  [weight_blocks(): pl.pallas_call(functools.partial(weight_blocks_kernel, geom, member, step...]
    pallas_call x3 -> x22, Pallas kernels: 29.8 us -> 61.6 us  [the longest x12 35.4 us: weight_piece(): pl.pallas_call(functools.partial(weight_piece_kernel, geom, member, step,...]
    pallas_call x6 -> x5, Pallas kernels: 86.5 us -> 55 us  [backward_layer(): pl.pallas_call(functools.partial(backward_kernel, geom, added is not None...]
    ppermute x115 -> x166, starting transfers between devices: 127 us -> 148 us  [swap(): return lax.ppermute(x, AXES, [(i, i ^ 1 << bit) for i in range(n)])]
    pallas_call x6, Pallas kernels: 64.3 us -> 49.5 us  [forward_layer(): pl.pallas_call(functools.partial(forward_kernel, geom, norm is not None,...]
    unnamed x119 -> x247, local copies, waits for them, and re-layouts: 10.8 us -> 20.8 us
    add x62 -> x65, other arithmetic: 12.9 us -> 3.34 us  [the longest x6 2.99 us: finish(): self.out = z.astype(F32) + got.astype(F32)]
  transfers between devices with their start and end apart: 117 -> 166, of which waited for: 74 -> 71; matrix products, arithmetic and copies ran while one was open for 4% -> 6% of each run, Pallas kernels for 26% -> 29%
where the time goes in v2:
time: 584 us; the launch traced here: 573 us
  Pallas kernels  204 us (35%)
  waiting for transfers between devices  162 us (28%)
  starting transfers between devices  148 us (25%)
  other arithmetic  30.9 us (5%)
  local copies, waits for them, and re-layouts  24.4 us (4%)
    ppermute x166, waiting for transfers between devices, swap(): return lax.ppermute(x, AXES, [(i, i ^ 1 << bit) for i in range(n)])  162 us
    ppermute x166, starting transfers between devices, swap(): return lax.ppermute(x, AXES, [(i, i ^ 1 << bit) for i in range(n)])  148 us
    pallas_call x5, Pallas kernels, backward_layer(): pl.pallas_call(functools.partial(backward_kernel, geom, added is not None...  55 us
    pallas_call x6, Pallas kernels, forward_layer(): pl.pallas_call(functools.partial(forward_kernel, geom, norm is not None,...  49.5 us
    pallas_call x12, Pallas kernels, weight_piece(): pl.pallas_call(functools.partial(weight_piece_kernel, geom, member, step,...  35.4 us
    unnamed x247, local copies, waits for them, and re-layouts  20.8 us
    pallas_call x4, Pallas kernels, weight_blocks(): pl.pallas_call(functools.partial(weight_blocks_kernel, geom, member, step...  13.7 us
  transfers between devices with their start and end apart: 166, of which 71 were waited for; matrix products, arithmetic and copies ran while one was open for 6% of the time, Pallas kernels for 29%

profile of v2, /device:TPU:0, one launch (start us, length us, event | category | flops | bytes accessed | tf_op | source)
XLA Modules:
  0.0 572.6 jit_solution(3070827349093063481)
XLA Ops:
  4.8 4.1 collective-permute-done
  25.0 4.2 collective-permute-done.15
  31.6 6.5 %collective-permute-done.16 = bf16[2,592,128]{2,1,0:T(8,128)(2,1)S(1)} collective-permute-done((bf16[2,592,128]{2,1,0:T(8,128)(2,1)S(1)}, bf16[2,592,128]{2,1,0:T(8,128)(2,1)S(1)}, u32[]{:S(2)}, u32[]{:S(2)}) %collective-permute-start.16) | collective-permute-done | bytes 303136 | tf_op jit(solution)/shard_map/ppermute | solution.py:988
  40.4 6.1 %shard_map.237 = (f32[1024,512]{1,0:T(8,128)S(1)}, f32[4,512]{1,0:T(4,128)S(1)}, bf16[2304,512]{1,0:T(8,128)(2,1)}) custom-call(s32[2]{0:T(128)S(1)} %copy-done.22, bf16[1024,256]{1,0:T(8,128)(2,1)S(1)} %bitcast.275, s32[1]{0:T(128)} %bitcast.1.refs_2_.me_ref.refs_5_.refs_0_, bf16[8,144,128]{2,1,0:T(8,128)(2,1)} %copy-done.60, ...), custom_call_target="tpu_custom_call" | custom-call | flops 241591904 | bytes 655360 | tf_op jit(solution)/shard_map/pallas_call | solution.py:254
  77.2 9.4 %shard_map.239 = (f32[1024,512]{1,0:T(8,128)S(1)}, f32[4,512]{1,0:T(4,128)S(1)}, bf16[1024,512]{1,0:T(8,128)(2,1)S(1)}, bf16[4608,512]{1,0:T(8,128)(2,1)}) custom-call(s32[2]{0:T(128)S(1)} %copy-done.22, f32[1024,512]{1,0:T(8,128)S(1)} %get-tuple-element.365.refs_1_.refs_7_.pre_ref, f32[4,512]{1,0:T(4,128)S(1)} %add.549.refs_2_.refs_8_.st_ref, ...), custom_call_target="tpu_custom_call" | custom-call | flops 483183808 | bytes 891289 | tf_op jit(solution)/shard_map/pallas_call | solution.py:254
  114.8 9.3 %shard_map.240 = (f32[1024,512]{1,0:T(8,128)S(1)}, f32[4,512]{1,0:T(4,128)S(1)}, bf16[1024,512]{1,0:T(8,128)(2,1)S(1)}, bf16[4608,512]{1,0:T(8,128)(2,1)}) custom-call(s32[2]{0:T(128)S(1)} %copy-done.22, f32[1024,512]{1,0:T(8,128)S(1)} %get-tuple-element.385.refs_1_.refs_8_.refs_2_, f32[4,512]{1,0:T(4,128)S(1)} %add.554.refs_2_.refs_9_.refs_3_, ...), custom_call_target="tpu_custom_call" | custom-call | flops 483183808 | bytes 891289 | tf_op jit(solution)/shard_map/pallas_call | solution.py:254
  153.9 9.6 %shard_map.242 = (f32[1024,512]{1,0:T(8,128)S(1)}, f32[4,512]{1,0:T(4,128)S(1)}, bf16[4608,512]{1,0:T(8,128)(2,1)}) custom-call(s32[2]{0:T(128)S(1)} %copy-done.22, bf16[1024,512]{1,0:T(8,128)(2,1)S(1)} %shard_map.241.refs_1_, s32[1]{0:T(128)} %bitcast.1.refs_2_.me_ref.refs_5_.refs_0_, bf16[8,288,128]{2,1,0:T(8,128)(2,1)} %copy-done.56, ...), custom_call_target="tpu_custom_call" | custom-call | flops 483183808 | bytes 891289 | tf_op jit(solution)/shard_map/pallas_call | solution.py:254
  189.6 9.3 %shard_map.243 = (f32[1024,512]{1,0:T(8,128)S(1)}, f32[4,512]{1,0:T(4,128)S(1)}, bf16[1024,512]{1,0:T(8,128)(2,1)S(1)}, bf16[4608,512]{1,0:T(8,128)(2,1)}) custom-call(s32[2]{0:T(128)S(1)} %copy-done.22, f32[1024,512]{1,0:T(8,128)S(1)} %get-tuple-element.419.refs_1_.refs_8_.refs_2_, f32[4,512]{1,0:T(4,128)S(1)} %add.564.refs_2_.refs_9_.refs_3_, ...), custom_call_target="tpu_custom_call" | custom-call | flops 483183808 | bytes 891289 | tf_op jit(solution)/shard_map/pallas_call | solution.py:254
  224.2 5.8 %shard_map.244 = (f32[1024,256]{1,0:T(8,128)S(1)}, f32[4,256]{1,0:T(4,128)S(1)}, bf16[1024,512]{1,0:T(8,128)(2,1)S(1)}, bf16[4608,256]{1,0:T(8,128)(2,1)}) custom-call(s32[2]{0:T(128)S(1)} %copy-done.22, f32[1024,512]{1,0:T(8,128)S(1)} %get-tuple-element.436.refs_1_.refs_7_.refs_2_, f32[4,512]{1,0:T(4,128)S(1)} %add.569.refs_2_.refs_8_.refs_3_, ...), custom_call_target="tpu_custom_call" | custom-call | flops 241591904 | bytes 655360 | tf_op jit(solution)/shard_map/pallas_call | solution.py:254
  230.0 4.1 shard_map.245
  276.1 8.1 %shard_map.251 = (bf16[3,2,18,32,256]{4,3,2,1,0:T(8,128)(2,1)S(1)}, f32[1024,512]{1,0:T(8,128)S(1)}, f32[4,512]{1,0:T(4,128)S(1)}) custom-call(s32[2]{0:T(128)S(1)} %copy-done.22, f32[1024,256]{1,0:T(8,128)S(1)} %get-tuple-element.467.refs_1_, f32[1024,256]{1,0:T(8,128)S(1)} %get-tuple-element.452.bot_ref.refs_2_, f32[4,256]{1,0:T(4,128)S(1)} %slice.1145.bot_st.refs_3_, ...), custom_call_target="tpu_custom_call" | custom-call | flops 241591904 | bytes 1284505 | tf_op jit(solution)/shard_map/pallas_call | solution.py:623
  285.9 4.4 shard_map.252
  311.7 11.2 %shard_map.257 = (bf16[3,2,18,32,512]{4,3,2,1,0:T(8,128)(2,1)S(1)}, f32[1024,512]{1,0:T(8,128)S(1)}, f32[4,512]{1,0:T(4,128)S(1)}) custom-call(s32[2]{0:T(128)S(1)} %copy-done.22, f32[1024,512]{1,0:T(8,128)S(1)} %get-tuple-element.490.refs_1_, f32[1024,512]{1,0:T(8,128)S(1)} %get-tuple-element.436.refs_1_.refs_7_.refs_2_, ...), custom_call_target="tpu_custom_call" | custom-call | flops 483183808 | bytes 1520435 | tf_op jit(solution)/shard_map/pallas_call | solution.py:623
  349.7 13.6 %shard_map.262 = (bf16[3,2,18,32,512]{4,3,2,1,0:T(8,128)(2,1)S(1)}, f32[1024,512]{1,0:T(8,128)S(1)}, f32[4,512]{1,0:T(4,128)S(1)}) custom-call(s32[2]{0:T(128)S(1)} %copy-done.22, f32[1024,512]{1,0:T(8,128)S(1)} %get-tuple-element.500.refs_1_, f32[1024,512]{1,0:T(8,128)S(1)} %get-tuple-element.419.refs_1_.refs_8_.refs_2_, ...), custom_call_target="tpu_custom_call" | custom-call | flops 483183808 | bytes 1520435 | tf_op jit(solution)/shard_map/pallas_call | solution.py:623
  398.9 10.9 %shard_map.269 = (bf16[3,2,18,32,512]{4,3,2,1,0:T(8,128)(2,1)S(1)}, f32[1024,512]{1,0:T(8,128)S(1)}, f32[4,512]{1,0:T(4,128)S(1)}) custom-call(s32[2]{0:T(128)S(1)} %copy-done.22, f32[1024,512]{1,0:T(8,128)S(1)} %get-tuple-element.530.refs_1_, f32[1024,512]{1,0:T(8,128)S(1)} %get-tuple-element.686.top_ref.refs_7_.refs_2_, ...), custom_call_target="tpu_custom_call" | custom-call | flops 483183808 | bytes 1520435 | tf_op jit(solution)/shard_map/pallas_call | solution.py:623
  435.0 4.1 copy.61
  444.0 4.7 collective-permute-done.138
  452.6 11.2 %shard_map.274 = (bf16[3,2,18,32,512]{4,3,2,1,0:T(8,128)(2,1)S(1)}, f32[1024,512]{1,0:T(8,128)S(1)}, f32[4,512]{1,0:T(4,128)S(1)}) custom-call(s32[2]{0:T(128)S(1)} %copy-done.22, f32[1024,512]{1,0:T(8,128)S(1)} %copy-done.18, f32[1024,512]{1,0:T(8,128)S(1)} %copy-done.9, f32[4,512]{1,0:T(4,128)S(1)} %add.554.refs_2_.refs_9_.refs_3_, ...), custom_call_target="tpu_custom_call" | custom-call | flops 483183808 | bytes 1520435 | tf_op jit(solution)/shard_map/pallas_call | solution.py:623
  510.8 4.2 shard_map.279
  521.0 5.6 shard_map.280
  532.3 5.3 shard_map.281
  537.8 4.2 collective-permute-done.159
  547.4 4.8 collective-permute-done.157
  555.1 5.1 collective-permute-done.161
  (805 shorter events, 403.0 us)
Async XLA Ops:
  47.9 19.2 %collective-permute-start.22 = (bf16[8,304,128]{2,1,0:T(8,128)(2,1)S(1)}, bf16[8,304,128]{2,1,0:T(8,128)(2,1)S(1)}, u32[]{:S(2)}, u32[]{:S(2)}) collective-permute-start(bf16[8,304,128]{2,1,0:T(8,128)(2,1)S(1)} %constant_dynamic-update-slice_fusion.11.refs_2_.refs_8_), channel_id=1, source_target_pairs={{0,4},{1,5},{2,6},{3,7},{4,0},{5,1},{6,2},{7,3},{8,12},{9,13},{10,... | collective-permute-start | bytes 1867784 | tf_op jit(solution)/shard_map/ppermute | solution.py:988
  88.1 17.3 %collective-permute-start.37 = (bf16[8,288,128]{2,1,0:T(8,128)(2,1)S(1)}, bf16[8,288,128]{2,1,0:T(8,128)(2,1)S(1)}, u32[]{:S(2)}, u32[]{:S(2)}) collective-permute-start(bf16[8,288,128]{2,1,0:T(8,128)(2,1)S(1)} %constant_dynamic-update-slice_fusion.17.refs_8_), channel_id=1, source_target_pairs={{0,4},{1,5},{2,6},{3,7},{4,0},{5,1},{6,2},{7,3},{8,12},{9,13},{10,... | collective-permute-start | bytes 1769480 | tf_op jit(solution)/shard_map/ppermute | solution.py:988
  125.9 17.0 %collective-permute-start.52 = (bf16[8,288,128]{2,1,0:T(8,128)(2,1)S(1)}, bf16[8,288,128]{2,1,0:T(8,128)(2,1)S(1)}, u32[]{:S(2)}, u32[]{:S(2)}) collective-permute-start(bf16[8,288,128]{2,1,0:T(8,128)(2,1)S(1)} %constant_dynamic-update-slice_fusion.23.refs_5_), channel_id=1, source_target_pairs={{0,4},{1,5},{2,6},{3,7},{4,0},{5,1},{6,2},{7,3},{8,12},{9,13},{10,... | collective-permute-start | bytes 1769480 | tf_op jit(solution)/shard_map/ppermute | solution.py:988
  146.8 16.6 %collective-permute-start.62 = (bf16[4,288,128]{2,1,0:T(8,128)(2,1)S(1)}, bf16[4,288,128]{2,1,0:T(8,128)(2,1)S(1)}, u32[]{:S(2)}, u32[]{:S(2)}) collective-permute-start(bf16[4,288,128]{2,1,0:T(8,128)(2,1)S(1)} %get-tuple-element.426), channel_id=1, source_target_pairs={{0,4},{1,5},{2,6},{3,7},{4,0},{5,1},{6,2},{7,3},{8,12},{9,13},{10,... | collective-permute-start | bytes 884744 | tf_op jit(solution)/shard_map/ppermute | solution.py:988
  148.3 15.2 %collective-permute-start.63 = (bf16[4,288,128]{2,1,0:T(8,128)(2,1)S(1)}, bf16[4,288,128]{2,1,0:T(8,128)(2,1)S(1)}, u32[]{:S(2)}, u32[]{:S(2)}) collective-permute-start(bf16[4,288,128]{2,1,0:T(8,128)(2,1)S(1)} %get-tuple-element.429), channel_id=1, source_target_pairs={{0,2},{1,3},{2,0},{3,1},{4,6},{5,7},{6,4},{7,5},{8,10},{9,11},{10,... | collective-permute-start | bytes 884744 | tf_op jit(solution)/shard_map/ppermute | solution.py:988
  165.1 17.1 %collective-permute-start.67 = (bf16[8,288,128]{2,1,0:T(8,128)(2,1)S(1)}, bf16[8,288,128]{2,1,0:T(8,128)(2,1)S(1)}, u32[]{:S(2)}, u32[]{:S(2)}) collective-permute-start(bf16[8,288,128]{2,1,0:T(8,128)(2,1)S(1)} %constant_dynamic-update-slice_fusion.29.refs_8_), channel_id=1, source_target_pairs={{0,4},{1,5},{2,6},{3,7},{4,0},{5,1},{6,2},{7,3},{8,12},{9,13},{10,... | collective-permute-start | bytes 1769480 | tf_op jit(solution)/shard_map/ppermute | solution.py:988
  199.0 15.2 %collective-permute-start.79 = (bf16[8,288,128]{2,1,0:T(8,128)(2,1)S(1)}, bf16[8,288,128]{2,1,0:T(8,128)(2,1)S(1)}, u32[]{:S(2)}, u32[]{:S(2)}) collective-permute-start(bf16[8,288,128]{2,1,0:T(8,128)(2,1)S(1)} %constant_dynamic-update-slice_fusion.33.refs_6_.refs_3_.refs_0_), channel_id=1, source_target_pairs={{0,2},{1,3},{2,0},{3,1},{4,6},{5,7},{6,4},{7,5},{8,10},{9,11},{10,... | collective-permute-start | bytes 1769480 | tf_op jit(solution)/shard_map/ppermute | solution.py:988
  200.6 17.3 %collective-permute-start.81 = (bf16[8,288,128]{2,1,0:T(8,128)(2,1)S(1)}, bf16[8,288,128]{2,1,0:T(8,128)(2,1)S(1)}, u32[]{:S(2)}, u32[]{:S(2)}) collective-permute-start(bf16[8,288,128]{2,1,0:T(8,128)(2,1)S(1)} %constant_dynamic-update-slice_fusion.35.refs_8_.refs_5_.refs_2_), channel_id=1, source_target_pairs={{0,4},{1,5},{2,6},{3,7},{4,0},{5,1},{6,2},{7,3},{8,12},{9,13},{10,... | collective-permute-start | bytes 1769480 | tf_op jit(solution)/shard_map/ppermute | solution.py:988
  295.0 27.9 %collective-permute-start.105 = (bf16[2,8,384,128]{3,2,1,0:T(8,128)(2,1)}, bf16[2,8,384,128]{3,2,1,0:T(8,128)(2,1)S(1)}, u32[]{:S(2)}, u32[]{:S(2)}) collective-permute-start(bf16[2,8,384,128]{3,2,1,0:T(8,128)(2,1)} %get-tuple-element.517), channel_id=1, source_target_pairs={{0,1},{1,0},{2,3},{3,2},{4,5},{5,4},{6,7},{7,6},{8,9},{9,8},{10,11... | collective-permute-start | bytes 4718600 | tf_op jit(solution)/shard_map/ppermute | solution.py:988
  339.4 24.1 %collective-permute-start.113 = (bf16[2,8,576,128]{3,2,1,0:T(8,128)(2,1)}, bf16[2,8,576,128]{3,2,1,0:T(8,128)(2,1)S(1)}, u32[]{:S(2)}, u32[]{:S(2)}) collective-permute-start(bf16[2,8,576,128]{3,2,1,0:T(8,128)(2,1)} %get-tuple-element.543), channel_id=1, source_target_pairs={{0,1},{1,0},{2,3},{3,2},{4,5},{5,4},{6,7},{7,6},{8,9},{9,8},{10,11... | collective-permute-start | bytes 7077896 | tf_op jit(solution)/shard_map/ppermute | solution.py:988
  347.6 15.8 %collective-permute-start.115 = (bf16[4,192,128]{2,1,0:T(8,128)(2,1)S(1)}, bf16[4,192,128]{2,1,0:T(8,128)(2,1)S(1)}, u32[]{:S(2)}, u32[]{:S(2)}) collective-permute-start(bf16[4,192,128]{2,1,0:T(8,128)(2,1)S(1)} %get-tuple-element.801), channel_id=1, source_target_pairs={{0,2},{1,3},{2,0},{3,1},{4,6},{5,7},{6,4},{7,5},{8,10},{9,11},{10,... | collective-permute-start | bytes 589832 | tf_op jit(solution)/shard_map/ppermute | solution.py:988
  382.2 29.9 %collective-permute-start.123 = (bf16[2,8,576,128]{3,2,1,0:T(8,128)(2,1)}, bf16[2,8,576,128]{3,2,1,0:T(8,128)(2,1)S(1)}, u32[]{:S(2)}, u32[]{:S(2)}) collective-permute-start(bf16[2,8,576,128]{3,2,1,0:T(8,128)(2,1)} %get-tuple-element.586), channel_id=1, source_target_pairs={{0,1},{1,0},{2,3},{3,2},{4,5},{5,4},{6,7},{7,6},{8,9},{9,8},{10,11... | collective-permute-start | bytes 7077896 | tf_op jit(solution)/shard_map/ppermute | solution.py:988
  390.7 19.2 %collective-permute-start.127 = (bf16[384,128]{1,0:T(8,128)(2,1)S(1)}, bf16[384,128]{1,0:T(8,128)(2,1)S(1)}, u32[]{:S(2)}, u32[]{:S(2)}) collective-permute-start(bf16[384,128]{1,0:T(8,128)(2,1)S(1)} %get-tuple-element.841), channel_id=1, source_target_pairs={{0,16},{1,17},{2,18},{3,19},{4,20},{5,21},{6,22},{7,23},{8,24},{9,... | collective-permute-start | bytes 294920 | tf_op jit(solution)/shard_map/ppermute | solution.py:988
  392.6 17.4 %collective-permute-start.125 = (bf16[4,288,128]{2,1,0:T(8,128)(2,1)S(1)}, bf16[4,288,128]{2,1,0:T(8,128)(2,1)S(1)}, u32[]{:S(2)}, u32[]{:S(2)}) collective-permute-start(bf16[4,288,128]{2,1,0:T(8,128)(2,1)S(1)} %get-tuple-element.791), channel_id=1, source_target_pairs={{0,2},{1,3},{2,0},{3,1},{4,6},{5,7},{6,4},{7,5},{8,10},{9,11},{10,... | collective-permute-start | bytes 884744 | tf_op jit(solution)/shard_map/ppermute | solution.py:988
  393.5 16.5 %collective-permute-start.124 = (bf16[4,288,128]{2,1,0:T(8,128)(2,1)S(1)}, bf16[4,288,128]{2,1,0:T(8,128)(2,1)S(1)}, u32[]{:S(2)}, u32[]{:S(2)}) collective-permute-start(bf16[4,288,128]{2,1,0:T(8,128)(2,1)S(1)} %get-tuple-element.793), channel_id=1, source_target_pairs={{0,4},{1,5},{2,6},{3,7},{4,0},{5,1},{6,2},{7,3},{8,12},{9,13},{10,... | collective-permute-start | bytes 884744 | tf_op jit(solution)/shard_map/ppermute | solution.py:988
  434.8 31.9 %collective-permute-start.135 = (bf16[2,8,768,128]{3,2,1,0:T(8,128)(2,1)}, bf16[2,8,768,128]{3,2,1,0:T(8,128)(2,1)}, u32[]{:S(2)}, u32[]{:S(2)}) collective-permute-start(bf16[2,8,768,128]{3,2,1,0:T(8,128)(2,1)} %get-tuple-element.633), channel_id=1, source_target_pairs={{0,1},{1,0},{2,3},{3,2},{4,5},{5,4},{6,7},{7,6},{8,9},{9,8},{10,11... | collective-permute-start | bytes 9437192 | tf_op jit(solution)/shard_map/ppermute | solution.py:988
  448.7 15.1 %collective-permute-start.139 = (bf16[576,128]{1,0:T(8,128)(2,1)S(1)}, bf16[576,128]{1,0:T(8,128)(2,1)S(1)}, u32[]{:S(2)}, u32[]{:S(2)}) collective-permute-start(bf16[576,128]{1,0:T(8,128)(2,1)S(1)} %get-tuple-element.824), channel_id=1, source_target_pairs={{0,16},{1,17},{2,18},{3,19},{4,20},{5,21},{6,22},{7,23},{8,24},{9,... | collective-permute-start | bytes 442376 | tf_op jit(solution)/shard_map/ppermute | solution.py:988
  452.5 22.7 %collective-permute-start.165 = (f32[32,192]{1,0:T(8,128)S(1)}, f32[32,192]{1,0:T(8,128)S(1)}, u32[]{:S(2)}, u32[]{:S(2)}) collective-permute-start(f32[32,192]{1,0:T(8,128)S(1)} %fusion.84), channel_id=1, source_target_pairs={{0,1},{1,0},{2,3},{3,2},{4,5},{5,4},{6,7},{7,6},{8,9},{9,8},{10,11... | collective-permute-start | bytes 73736 | tf_op jit(solution)/shard_map/ppermute | solution.py:988
  473.1 20.5 %collective-permute-start.141 = (bf16[2,4,384,128]{3,2,1,0:T(8,128)(2,1)}, bf16[2,4,384,128]{3,2,1,0:T(8,128)(2,1)}, u32[]{:S(2)}, u32[]{:S(2)}) collective-permute-start(bf16[2,4,384,128]{3,2,1,0:T(8,128)(2,1)} %pad_maximum_fusion.1), channel_id=1, source_target_pairs={{0,4},{1,5},{2,6},{3,7},{4,0},{5,1},{6,2},{7,3},{8,12},{9,13},{10,... | collective-permute-start | bytes 2359304 | tf_op jit(solution)/shard_map/ppermute | solution.py:988
  473.9 19.8 %collective-permute-start.140 = (bf16[8,384,128]{2,1,0:T(8,128)(2,1)}, bf16[8,384,128]{2,1,0:T(8,128)(2,1)}, u32[]{:S(2)}, u32[]{:S(2)}) collective-permute-start(bf16[8,384,128]{2,1,0:T(8,128)(2,1)} %get-tuple-element.747), channel_id=1, source_target_pairs={{0,2},{1,3},{2,0},{3,1},{4,6},{5,7},{6,4},{7,5},{8,10},{9,11},{10,... | collective-permute-start | bytes 2359304 | tf_op jit(solution)/shard_map/ppermute | solution.py:988
  498.9 17.6 %collective-permute-start.145 = (bf16[2,8,576,128]{3,2,1,0:T(8,128)(2,1)}, bf16[2,8,576,128]{3,2,1,0:T(8,128)(2,1)S(1)}, u32[]{:S(2)}, u32[]{:S(2)}) collective-permute-start(bf16[2,8,576,128]{3,2,1,0:T(8,128)(2,1)} %get-tuple-element.661), channel_id=1, source_target_pairs={{0,1},{1,0},{2,3},{3,2},{4,5},{5,4},{6,7},{7,6},{8,9},{9,8},{10,11... | collective-permute-start | bytes 7077896 | tf_op jit(solution)/shard_map/ppermute | solution.py:988
  516.9 20.7 %collective-permute-start.154 = (bf16[2,4,288,128]{3,2,1,0:T(8,128)(2,1)S(1)}, bf16[2,4,288,128]{3,2,1,0:T(8,128)(2,1)S(1)}, u32[]{:S(2)}, u32[]{:S(2)}) collective-permute-start(bf16[2,4,288,128]{3,2,1,0:T(8,128)(2,1)S(1)} %pad_maximum_fusion.8), channel_id=1, source_target_pairs={{0,4},{1,5},{2,6},{3,7},{4,0},{5,1},{6,2},{7,3},{8,12},{9,13},{10,... | collective-permute-start | bytes 1769480 | tf_op jit(solution)/shard_map/ppermute | solution.py:988
  518.1 19.5 %collective-permute-start.153 = (bf16[8,288,128]{2,1,0:T(8,128)(2,1)S(1)}, bf16[8,288,128]{2,1,0:T(8,128)(2,1)S(1)}, u32[]{:S(2)}, u32[]{:S(2)}) collective-permute-start(bf16[8,288,128]{2,1,0:T(8,128)(2,1)S(1)} %get-tuple-element.750), channel_id=1, source_target_pairs={{0,2},{1,3},{2,0},{3,1},{4,6},{5,7},{6,4},{7,5},{8,10},{9,11},{10,... | collective-permute-start | bytes 1769480 | tf_op jit(solution)/shard_map/ppermute | solution.py:988
  526.8 16.2 %collective-permute-start.152 = (bf16[2,4,144,128]{3,2,1,0:T(8,128)(2,1)S(1)}, bf16[2,4,144,128]{3,2,1,0:T(8,128)(2,1)S(1)}, u32[]{:S(2)}, u32[]{:S(2)}) collective-permute-start(bf16[2,4,144,128]{3,2,1,0:T(8,128)(2,1)S(1)} %pad_maximum_fusion.26), channel_id=1, source_target_pairs={{0,4},{1,5},{2,6},{3,7},{4,0},{5,1},{6,2},{7,3},{8,12},{9,13},{10,... | collective-permute-start | bytes 884744 | tf_op jit(solution)/shard_map/ppermute | solution.py:988
  (248 other events, 2617.3 us)

commit v3 on v2

--- a/solution.py
+++ b/solution.py
@@ -16,7 +16,7 @@
 F32 = jnp.float32
 BF16 = jnp.bfloat16
 COST = 0.1
-VMEM_LIMIT = 20 * 1024 * 1024
+VMEM_LIMIT = 12 * 1024 * 1024
 
 
 def params(grid_dims=0):
@@ -164,61 +164,44 @@
     act_ref = refs.pop(0) if normed else None
     if pieces:
         matrix_ref = refs.pop(0)
-    win_ref = refs.pop(0)
+    win_ref, held_ref, sem = refs
+
     if pieces:
-        held_ref, sem = refs.pop(0), refs.pop(0)
-    step = pl.program_id(0)
-    chans = win_ref.shape[-1]
-
-    @pl.when(step == 0)
-    def _():
-        if pieces:
-            fetch(*pieces, me_ref, sources, held_ref, sem.at[0])
-        clear_edges(win_ref, rows)
-        for f in range(frames):
+        fetch(*pieces, me_ref, sources, held_ref, sem.at[0])
+    else:
+        pltpu.make_async_copy(kernel_ref, held_ref, sem.at[0]).start()
+    clear_edges(win_ref, rows)
+    for f in range(frames):
+        if normed:
+            average, inverse = frame_tables(stats_ref[...], domain_ref[f], counts)
+            scale = inverse * gain_ref[...]
+            shift = bias_ref[...] - average * scale
+
+        def one_row(r, _):
+            at = pl.multiple_of(f * pixels + r * cols, cols)
+            value = source_ref[pl.ds(at, cols), :].astype(F32)
             if normed:
-                average, inverse = frame_tables(stats_ref[...], domain_ref[f], counts)
-                scale = inverse * gain_ref[...]
-                shift = bias_ref[...] - average * scale
-
-            def one_row(r, _):
-                at = pl.multiple_of(f * pixels + r * cols, cols)
-                value = source_ref[pl.ds(at, cols), :].astype(F32)
-                if normed:
-                    act = value * scale + shift
-                    value = act * sigmoid(act)
-                    act_ref[pl.ds(at, cols), :] = value.astype(BF16)
-                put_windows(win_ref, f, r, value, cols)
-                return 0
-
-            lax.fori_loop(0, rows, one_row, 0, unroll=2)
-        if pieces:
-            arrived(held_ref, sem.at[0])
-            pltpu.make_async_copy(held_ref, matrix_ref, sem.at[1]).start()
-
-    source = jnp.concatenate([window(win_ref, b, step, rows) for b in range(3)], 1)
+                act = value * scale + shift
+                value = act * sigmoid(act)
+                act_ref[pl.ds(at, cols), :] = value.astype(BF16)
+            put_windows(win_ref, f, r, value, cols)
+            return 0
+
+        lax.fori_loop(0, rows, one_row, 0, unroll=2)
+    arrived(held_ref, sem.at[0])
     if pieces:
-        matrix = held_ref[pl.ds(pl.multiple_of(step * 3 * chans, 3 * chans), 3 * chans), :]
-    else:
-        matrix = kernel_ref[...]
-    part = jnp.dot(source, matrix, preferred_element_type=F32)
-
-    @pl.when(step == 0)
-    def _():
-        out_ref[...] = part
-
-    @pl.when(step > 0)
-    def _():
-        out_ref[...] += part
-
-    @pl.when(step == 2)
-    def _():
-        for lane in range(0, out_ref.shape[-1], 256):
-            lanes = slice(lane, lane + 256)
-            pairs = [column_sums(out_ref, f, pixels, lanes) for f in range(frames)]
-            sums_ref[:, lanes] = by_domain([p[0] for p in pairs], [p[1] for p in pairs], domain_ref)
-        if pieces:
-            pltpu.make_async_copy(held_ref, matrix_ref, sem.at[1]).wait()
+        pltpu.make_async_copy(held_ref, matrix_ref, sem.at[1]).start()
+    source = jnp.concatenate([window(win_ref, b, a, rows) for a in range(3) for b in range(3)], 1)
+    out = jnp.dot(source, held_ref[...], preferred_element_type=F32)
+    out_ref[...] = out
+    parts = [out[f * pixels : (f + 1) * pixels] for f in range(frames)]
+    sums_ref[...] = by_domain(
+        [jnp.sum(fold(p), 0, keepdims=True) for p in parts],
+        [jnp.sum(fold(p * p), 0, keepdims=True) for p in parts],
+        domain_ref,
+    )
+    if pieces:
+        pltpu.make_async_copy(held_ref, matrix_ref, sem.at[1]).wait()
 
 
 ANYWHERE = pl.BlockSpec(memory_space=pl.ANY)
@@ -237,8 +220,8 @@
         args += [kernel.me, *kernel.sources]
         specs += [SCALARS] + [ANYWHERE] * len(kernel.sources)
     else:
-        args.append(kernel)
-        specs.append(pl.BlockSpec((3 * chans, width), lambda a: (a, 0)))
+        args.append(in_hbm(kernel))
+        specs.append(ANYWHERE)
     outs, out_specs = [sds((pix, width), F32)], [whole((pix, width))]
     outs.append(sds((4, width), F32))
     out_specs.append(whole((4, width)))
@@ -246,14 +229,14 @@
         outs.append(sds((pix, chans), BF16))
         out_specs.append(whole((pix, chans)))
     scratch = [pltpu.VMEM((3, frames, rows + 2, cols, chans), BF16)]
+    scratch += [pltpu.VMEM(kernel.shape, BF16), pltpu.SemaphoreType.DMA((2,))]
     if pieces:
         outs.append(pltpu.HBM(kernel.shape, BF16))
         out_specs.append(ANYWHERE)
-        scratch += [pltpu.VMEM(kernel.shape, BF16), pltpu.SemaphoreType.DMA((2,))]
     size = kernel.shape[0] * kernel.shape[1]
     return pl.pallas_call(
         functools.partial(forward_kernel, geom, norm is not None, (kernel.member, kernel.parts) if pieces else None),
-        grid=(3,),
+        grid=(1,),
         in_specs=specs,
         out_specs=out_specs,
         out_shape=outs,
@@ -514,118 +497,98 @@
     g_ref, pre_ref, st_ref, sm_ref, gain_ref = (refs.pop(0) for _ in range(5))
     kernel_ref = refs.pop(0)
     add_ref = refs.pop(0) if added else None
-    if epilogue in ("silu", "pool"):
-        lpre_ref, lst_ref, lgain_ref, lbias_ref = (refs.pop(0) for _ in range(4))
+    lpre_ref, lst_ref, lgain_ref, lbias_ref = (refs.pop(0) for _ in range(4))
     if epilogue == "pool":
         mix_ref = refs.pop(0)
-    win_ref = refs.pop(0)
-    out_ref = refs.pop(0)
-    if epilogue != "none":
-        sums_ref = refs.pop(0)
-    step = pl.program_id(0)
-    chans = kernel_ref.shape[0] // 3
-
-    @pl.when(step == 0)
-    def _():
-        clear_edges(win_ref, rows)
+    win_ref, out_ref, sums_ref, held_ref, sem = refs
+    chans = kernel_ref.shape[0] // 9
+
+    load = pltpu.make_async_copy(kernel_ref, held_ref, sem)
+    load.start()
+    clear_edges(win_ref, rows)
+    for f in range(frames):
+        tables = back_tables(st_ref, sm_ref, gain_ref, domain_ref[f], counts)
+
+        def one_row(r, _):
+            at = pl.multiple_of(f * pixels + r * cols, cols)
+            low = norm_back_rows(g_ref[pl.ds(at, cols), :], pre_ref[pl.ds(at, cols), :], tables)
+            put_windows(win_ref, f, r, low, cols)
+            return 0
+
+        lax.fori_loop(0, rows, one_row, 0, unroll=2)
+    load.wait()
+    source = jnp.concatenate([window(win_ref, 2 - b, 2 - a, rows) for a in range(3) for b in range(3)], 1)
+    weight = jnp.concatenate([held_ref[k * chans : (k + 1) * chans, :] for k in range(9)], 1)
+    out = lax.dot_general(source, weight, (((1,), (1,)), ((), ())), preferred_element_type=F32)
+    out_ref[...] = out + add_ref[...] if added else out
+
+    for lane in range(0, chans, LANES):
+        lanes = slice(lane, lane + LANES)
+        sums = []
         for f in range(frames):
-            tables = back_tables(st_ref, sm_ref, gain_ref, domain_ref[f], counts)
-
-            def one_row(r, _):
+            mean, inv = frame_tables(lst_ref[:, lanes], domain_ref[f], counts)
+
+            def slope(at):
+                xhat = (lpre_ref[pl.ds(at, cols), lanes] - mean) * inv
+                act = xhat * lgain_ref[:, lanes] + lbias_ref[:, lanes]
+                s = sigmoid(act)
+                return xhat, act * s, s * (1.0 + act * (1.0 - s))
+
+            def finish(at, g, xhat, carry):
+                out_ref[pl.ds(at, cols), lanes] = g
+                return carry[0] + fold(g), carry[1] + fold(g * xhat)
+
+            def one_row(r, carry):
                 at = pl.multiple_of(f * pixels + r * cols, cols)
-                low = norm_back_rows(g_ref[pl.ds(at, cols), :], pre_ref[pl.ds(at, cols), :], tables)
-                put_windows(win_ref, f, r, low, cols)
-                return 0
-
-            lax.fori_loop(0, rows, one_row, 0, unroll=2)
-
-    source = jnp.concatenate([window(win_ref, 2 - b, 2 - step, rows) for b in range(3)], 1)
-    weight = jnp.concatenate([kernel_ref[b * chans : (b + 1) * chans, :] for b in range(3)], 1)
-    nt = (((1,), (1,)), ((), ()))
-    part = lax.dot_general(source, weight, nt, preferred_element_type=F32)
-
-    @pl.when(step == 0)
-    def _():
-        out_ref[...] = part + add_ref[...] if added else part
-
-    @pl.when(step > 0)
-    def _():
-        out_ref[...] += part
-
-    if epilogue == "none":
-        return
-
-    @pl.when(step == 2)
-    def _():
-        for lane in range(0, chans, LANES):
-            lanes = slice(lane, lane + LANES)
-            sums = []
-            for f in range(frames):
-                mean, inv = frame_tables(lst_ref[:, lanes], domain_ref[f], counts)
-
-                def slope(at):
-                    xhat = (lpre_ref[pl.ds(at, cols), lanes] - mean) * inv
-                    act = xhat * lgain_ref[:, lanes] + lbias_ref[:, lanes]
-                    s = sigmoid(act)
-                    return xhat, act * s, s * (1.0 + act * (1.0 - s))
-
-                def finish(at, g, xhat, carry):
-                    out_ref[pl.ds(at, cols), lanes] = g
-                    return carry[0] + fold(g), carry[1] + fold(g * xhat)
-
-                def one_row(r, carry):
-                    at = pl.multiple_of(f * pixels + r * cols, cols)
-                    xhat, _, steep = slope(at)
-                    return finish(at, out_ref[pl.ds(at, cols), lanes] * steep, xhat, carry)
-
-                def one_pair(i, carry):
-                    at = [pl.multiple_of(f * pixels + (2 * i + h) * cols, cols) for h in (0, 1)]
-                    xhat, top, steep = zip(*(slope(a) for a in at))
-                    weight = softmax_window(top, cols)
-                    up = [out_ref[pl.ds(a, cols), lanes] for a in at]
-                    mix = [mix_ref[pl.ds(a, cols), lanes] for a in at]
-                    pooled = pair_sum(weight[0] * top[0] + weight[1] * top[1], cols)
-                    d_pool = pair_sum(weight[0] * up[0] + weight[1] * up[1], cols)
-                    flow = [m + d_pool for m in mix]
-                    d_w = [u * pooled + fl * t for u, fl, t in zip(up, flow, top)]
-                    centre = pair_sum(weight[0] * d_w[0] + weight[1] * d_w[1], cols)
-                    for h in (0, 1):
-                        d_top = weight[h] * (flow[h] + d_w[h] - centre)
-                        carry = finish(at[h], d_top * steep[h], xhat[h], carry)
-                    return carry
-
-                zero = jnp.zeros((8, LANES), F32)
-                if epilogue == "silu":
-                    sums.append(lax.fori_loop(0, rows, one_row, (zero, zero), unroll=2))
-                else:
-                    sums.append(lax.fori_loop(0, rows // 2, one_pair, (zero, zero)))
-            sums_ref[:, lanes] = by_domain(
-                [jnp.sum(s[0], 0, keepdims=True) for s in sums],
-                [jnp.sum(s[1], 0, keepdims=True) for s in sums],
-                domain_ref,
-            )
-
-
-def backward_layer(geom, domain, top, kernel, added=None, lower=None, mix=None):
+                xhat, _, steep = slope(at)
+                return finish(at, out_ref[pl.ds(at, cols), lanes] * steep, xhat, carry)
+
+            def one_pair(i, carry):
+                at = [pl.multiple_of(f * pixels + (2 * i + h) * cols, cols) for h in (0, 1)]
+                xhat, top, steep = zip(*(slope(a) for a in at))
+                weight = softmax_window(top, cols)
+                up = [out_ref[pl.ds(a, cols), lanes] for a in at]
+                mix = [mix_ref[pl.ds(a, cols), lanes] for a in at]
+                pooled = pair_sum(weight[0] * top[0] + weight[1] * top[1], cols)
+                d_pool = pair_sum(weight[0] * up[0] + weight[1] * up[1], cols)
+                flow = [m + d_pool for m in mix]
+                d_w = [u * pooled + fl * t for u, fl, t in zip(up, flow, top)]
+                centre = pair_sum(weight[0] * d_w[0] + weight[1] * d_w[1], cols)
+                for h in (0, 1):
+                    d_top = weight[h] * (flow[h] + d_w[h] - centre)
+                    carry = finish(at[h], d_top * steep[h], xhat[h], carry)
+                return carry
+
+            zero = jnp.zeros((8, LANES), F32)
+            if epilogue == "silu":
+                sums.append(lax.fori_loop(0, rows, one_row, (zero, zero), unroll=2))
+            else:
+                sums.append(lax.fori_loop(0, rows // 2, one_pair, (zero, zero)))
+        sums_ref[:, lanes] = by_domain(
+            [jnp.sum(s[0], 0, keepdims=True) for s in sums],
+            [jnp.sum(s[1], 0, keepdims=True) for s in sums],
+            domain_ref,
+        )
+
+
+def backward_layer(geom, domain, top, kernel, lower, added=None, mix=None):
     frames, rows, cols, _ = geom
     pix, width = top[0].shape
     chans = kernel.shape[0] // 9
     args = [domain, *top, in_hbm(kernel)]
-    specs = [SCALARS] + [whole(x.shape) for x in top] + [pl.BlockSpec((3 * chans, width), lambda a: (a, 0))]
+    specs = [SCALARS] + [whole(x.shape) for x in top] + [ANYWHERE]
     win = (3, frames, rows + 2, cols, width)
     outs = [sds(win, BF16), sds((pix, chans), F32)]
-    extra = [] if added is None else [added]
-    epilogue = "none"
-    if lower is not None:
-        epilogue = "silu" if mix is None else "pool"
-        extra += list(lower) + ([] if mix is None else [mix])
-        outs.append(sds((4, chans), F32))
+    extra = ([] if added is None else [added]) + list(lower) + ([] if mix is None else [mix])
+    epilogue = "silu" if mix is None else "pool"
+    outs.append(sds((4, chans), F32))
     return pl.pallas_call(
         functools.partial(backward_kernel, geom, added is not None, epilogue),
-        grid=(3,),
+        grid=(1,),
         in_specs=specs + [whole(x.shape) for x in extra],
         out_specs=[whole(o.shape) for o in outs],
         out_shape=outs,
+        scratch_shapes=[pltpu.VMEM(kernel.shape, BF16), pltpu.SemaphoreType.DMA],
         compiler_params=params(1),
         cost_estimate=cost(2 * pix * kernel.size, kernel.size * 2 + pix * 10240),
     )(*args, *extra)
@@ -978,6 +941,34 @@
     )(*args)
 
 
+def share_kernel(widths, me_ref, *refs):
+    *sums, gain_ref, bias_ref, flat_ref = refs
+    at = 0
+    for ref, width in zip(sums, widths):
+        flat_ref[0:1, at : at + width] = ref[2:3, :] + ref[3:4, :]
+        flat_ref[1:2, at : at + width] = ref[0:1, :] + ref[1:2, :]
+        at += width
+    share = gain_ref.shape[1]
+    mine = pltpu.roll(flat_ref[...], at - me_ref[0] * share, 1)
+    gain_ref[...] = mine[0:1, :share]
+    bias_ref[...] = mine[1:2, :share]
+
+
+def share_of(me, sums, share):
+    widths = [x.shape[1] for x in sums]
+    got = pl.pallas_call(
+        functools.partial(share_kernel, widths),
+        grid=(1,),
+        in_specs=[SCALARS] + [whole(x.shape) for x in sums],
+        out_specs=[whole((1, share))] * 2,
+        out_shape=[sds((1, share), F32)] * 2,
+        scratch_shapes=[pltpu.VMEM((8, sum(widths)), F32)],
+        compiler_params=params(1),
+        cost_estimate=cost(0, 100000),
+    )(me, *(in_hbm(x) for x in sums))
+    return [x[0] for x in got]
+
+
 AXES = ("dp", "fsdp")
 CORE, X, Y, Z_NEAR, Z_FAR = range(5)
 ORDER = (CORE, Z_NEAR, Z_FAR, X, Y)
@@ -1018,7 +1009,7 @@
                 got = tied(got, fill.pop(0)(x))
             x = x + got
             for start in (after or {}).get(bit, ()):
-                start(x)
+                x = tied(x, start(x))
         for work in fill:
             work(x)
         return x
@@ -1084,51 +1075,112 @@
     return (a.astype(F32) + b.astype(F32)).astype(BF16)
 
 
+def add_kernel(jobs, *refs):
+    refs = list(refs)
+    count = sum(n for _, n, _ in jobs)
+    ins, outs = refs[:count], refs[count:]
+    for work, n_in, n_out in jobs:
+        work(*ins[:n_in], *outs[:n_out])
+        del ins[:n_in], outs[:n_out]
+
+
+def add_all(*jobs):
+    ins = [x for _, job, _ in jobs for x in job]
+    outs = [x for _, _, job in jobs for x in job]
+    got = pl.pallas_call(
+        functools.partial(add_kernel, [(work, len(i), len(o)) for work, i, o in jobs]),
+        grid=(1,),
+        in_specs=[whole(x.shape) for x in ins],
+        out_specs=[whole(x.shape) for x in outs],
+        out_shape=outs,
+        compiler_params=params(1),
+        cost_estimate=cost(0, sum(x.size * 2 for x in ins + outs)),
+    )(*ins)
+    result = []
+    for _, _, job in jobs:
+        result.append(got[: len(job)])
+        got = got[len(job) :]
+    return result
+
+
+def first_work(cut, near, far, got, a, send_a, b, send_b):
+    a[...] = plus(near[:, :cut], got[0, :, :cut])
+    send_a[...] = plus(far[:, :cut], got[1, :, :cut])
+    for half, out in enumerate((b, send_b)):
+        s = slice(4 * half, 4 * half + 4)
+        out[0] = plus(near[s, cut:], got[0, s, cut:])
+        out[1] = plus(far[s, cut:], got[1, s, cut:])
+
+
+def second_work(a, b, got_a, got_b, a_out, send_a, b_out, send_b):
+    a_out[...] = plus(a[:4], got_a[:4])
+    send_a[...] = plus(a[4:], got_a[4:])
+    b_out[...] = plus(b[0], got_b[0])
+    send_b[...] = plus(b[1], got_b[1])
+
+
+def near_work(cut, a, b, got_a, got_b, z, send):
+    for half, out in enumerate((z, send)):
+        s = slice(2 * half, 2 * half + 2)
+        out[:, :cut] = plus(a[s], got_a[s])
+        out[:, cut:] = plus(b[s], got_b[s])
+
+
+def far_work(z, got, z_out, send):
+    z_out[...] = plus(z[0], got[0])
+    send[...] = plus(z[1], got[1])
+
+
+def finish_work(z, got, out):
+    out[...] = z[...].astype(F32) + got[...].astype(F32)
+
+
 class Scatter:
     def __init__(self, links, blocks):
-        self.links = links
-        self.near_blocks, self.far_blocks, send = blocks
-        self.cut = half_rows(self.near_blocks.shape[1])
-        self.got = swap(send, CORE)
-
-    def first(self, to=None):
-        cut = self.cut
-        near, far, got = tied((self.near_blocks, self.far_blocks, self.got), to)
-        self.a, send_a = plus(near[:, :cut], got[0, :, :cut]), plus(far[:, :cut], got[1, :, :cut])
-        self.b, send_b = (
-            jnp.stack([plus(near[s, cut:], got[0, s, cut:]), plus(far[s, cut:], got[1, s, cut:])])
-            for s in (slice(0, 4), slice(4, 8))
-        )
+        self.links, self.blocks = links, blocks
+        self.rows = blocks[0].shape[1]
+        self.cut = half_rows(self.rows)
+        self.got = swap(blocks[2], CORE)
+
+    def shape(self, *dims):
+        return sds((*dims, LANES), BF16)
+
+    def first_job(self):
+        c, r = self.cut, self.rows - self.cut
+        outs = [self.shape(8, c)] * 2 + [self.shape(2, 4, r)] * 2
+        return functools.partial(first_work, c), [*self.blocks[:2], self.got], outs
+
+    def first(self, a, send_a, b, send_b):
+        self.a, self.b = a, b
         self.got = swap(send_a, X), swap(send_b, Y)
 
-    def second(self, to=None):
-        a, b, (got_a, got_b) = tied((self.a, self.b, self.got), to)
-        self.a, self.b = plus(a[:4], got_a[:4]), plus(b[0], got_b[0])
-        self.got = swap(plus(a[4:], got_a[4:]), Y), swap(plus(b[1], got_b[1]), X)
-
-    def near_sums(self, to=None):
-        a, b, (got_a, got_b) = tied((self.a, self.b, self.got), to)
-        self.z, self.send = (
-            jnp.concatenate([plus(a[s], got_a[s]), plus(b[s], got_b[s])], 1) for s in (slice(0, 2), slice(2, 4))
-        )
+    def second_job(self):
+        c, r = self.cut, self.rows - self.cut
+        return second_work, [self.a, self.b, *self.got], [self.shape(4, c)] * 2 + [self.shape(4, r)] * 2
+
+    def second(self, a, send_a, b, send_b):
+        self.a, self.b = a, b
+        self.got = swap(send_a, Y), swap(send_b, X)
+
+    def near_job(self):
+        return functools.partial(near_work, self.cut), [self.a, self.b, *self.got], [self.shape(2, self.rows)] * 2
 
     def near(self, to=None):
         self.got = swap(tied(self.send, to), Z_NEAR)
 
-    def far(self, to=None):
-        z, got = tied((self.z, self.got), to)
-        self.z = plus(z[0], got[0])
-        self.got = swap(plus(z[1], got[1]), Z_FAR)
-
-    def finish(self, to=None):
-        z, got = tied((self.z, self.got), to)
-        self.out = z.astype(F32) + got.astype(F32)
-
-    def busy(self):
-        if isinstance(self.got, tuple):
-            self.links.busy(X, *self.got)
-        else:
-            self.links.busy(CORE, self.got)
+    def far_job(self):
+        return far_work, [self.z, self.got], [self.shape(self.rows)] * 2
+
+    def far(self, z, send):
+        self.z = z
+        self.got = swap(send, Z_FAR)
+
+    def finish_job(self):
+        return finish_work, [self.z, self.got], [sds((self.rows, LANES), F32)]
+
+
+def add_after(to, *jobs):
+    return add_all(*((work, tied(ins, to), outs) for work, ins, outs in jobs))
 
 
 def rows_of_chip(shard):
@@ -1225,11 +1277,14 @@
     def pieces(self, name, act, low):
         return [lambda x: self.add(name, act, low)]
 
-    def send(self, n):
+    def send(self, n, to=None):
         pass
 
     def after_layer(self, n, local):
         pass
+
+    def now(self):
+        return None
 
     def tail(self, blocks, kernels):
         return [kernel(None) for kernel in kernels]
@@ -1275,7 +1330,7 @@
         self.mats = {}
         self.grads, self.blocks, self.sums = {}, {}, {}
         self.homes, self.rows = {}, {}
-        for names in (("six", "gating"), ("five",), ("four",), ("three", "attend"), ("two",), ("one",)):
+        for names in (("six", "gating"), ("five",), ("four", "attend"), ("three",), ("two",), ("one",)):
             at = 0
             for name in names:
                 self.homes[name] = Member(at, full[name], *sizes, split=name in splits)
@@ -1327,12 +1382,25 @@
         def z_done(x):
             self.sums[n + 2].near(x)
 
+        def x_done(x):
+            (got,) = add_after(x, self.sums[n + 2].far_job())
+            if n == 2:
+                self.late = got
+            else:
+                self.sums[n + 2].far(*got)
+            return got[0]
+
         def y_done(x):
-            self.sums[n + 1].second(x)
-            if n < 5:
-                self.sums[n + 2].far(x)
-
-        return {Y: [y_done], Z_FAR: [z_done] if n < 5 else []}
+            jobs = [self.sums[n + 1].second_job()]
+            if n == 2:
+                self.send(2)
+                jobs.append(self.sums[2].first_job())
+            got = add_after(x, *jobs)
+            self.sums[n + 1].second(*got[0])
+            if n == 2:
+                self.sums[2].first(*got[1])
+
+        return {Z_FAR: [z_done], X: [x_done], Y: [y_done]} if n < 5 else {Y: [y_done]}
 
     def add(self, name, act, low):
         n = NUMBER[name]
@@ -1359,48 +1427,64 @@
 
         return [piece(step) for step in range(3)]
 
-    def send(self, n):
-        self.sums[n] = Scatter(self.links, self.blocks[n])
+    def send(self, n, to=None):
+        near, far, away = self.blocks[n]
+        self.sums[n] = Scatter(self.links, (near, far, tied(away, to)))
 
     def after_layer(self, n, local):
+        jobs = [self.sums[n + 1].first_job()]
+        if n < 5:
+            jobs.append(self.sums[n + 2].near_job())
         if n < 4:
-            self.sums[n + 3].finish(local)
-            local = (local, self.sums[n + 3].out)
+            jobs.append(self.sums[n + 3].finish_job())
+        got = add_after(local, *jobs)
+        self.sums[n + 1].first(*got[0])
+        self.links.busy(X, *self.sums[n + 1].got)
         if n < 5:
-            self.sums[n + 2].near_sums(local)
-            local = self.sums[n + 2].send
-        self.sums[n + 1].first(local)
-        self.sums[n + 1].busy()
+            s = self.sums[n + 2]
+            s.z, s.send = got[1]
+        if n < 4:
+            (self.sums[n + 3].out,) = got[2]
+
+    def now(self):
+        return self.sums[3].a
 
     def tail(self, blocks, kernels):
-        self.send(1)
-        one, two, three, four = (self.sums[n] for n in (1, 2, 3, 4))
-        four.finish(blocks)
-        two.first((blocks, four.out))
-        three.near_sums(two.b)
-        three.near(two.b)
-        outs = [kernels[0]((two.b, three.z))]
-        one.first(outs[0])
-        three.far(one.b)
-        outs.append(kernels[1]((one.b, three.z)))
-        two.second(outs[1])
-        one.second(two.b)
-        three.finish(two.b)
-        two.near_sums((one.b, three.out))
+        two, three, four = (self.sums[n] for n in (2, 3, 4))
+        outs = [kernels[0](blocks)]
+        got = add_after(outs[0], two.second_job(), three.near_job())
+        two.second(*got[0])
+        three.z, three.send = got[1]
+        three.near()
+        self.send(1, got[0][0])
+        one = self.sums[1]
+        got = add_after(got[0][0], one.first_job(), two.near_job(), three.far_job())
+        one.first(*got[0])
+        two.z, two.send = got[1]
         two.near()
-        one.near_sums(two.z)
+        three.far(*got[2])
+        outs.append(kernels[1](got[0][0]))
+        (got,) = add_after(got[0][0], one.second_job())
+        one.second(*got)
+        (got,) = add_after(got[0], two.far_job())
+        two.far(*got)
+        got = add_after(got[0], one.near_job(), three.finish_job())
+        one.z, one.send = got[0]
         one.near()
-        two.far(one.z)
-        one.far(two.z)
-        two.finish(one.z)
-        one.finish()
+        (three.out,) = got[1]
+        four.far(*tied(tuple(self.late), one.z))
+        got = add_after(one.z, one.far_job(), two.finish_job())
+        one.far(*got[0])
+        (two.out,) = got[1]
+        ((four.out,),) = add_after(got[0][0], four.finish_job())
+        ((one.out,),) = add_after(four.out, one.finish_job())
         for name, m in self.homes.items():
             out = unpack(self.sums[NUMBER[name]].out[m.at : m.at + m.rows], m.blocks)
             self.grads[name] = columns_of_core(out) if m.split else out
         return outs
 
 
-NUMBER = dict(one=1, two=2, three=3, attend=3, four=4, five=5, six=6, gating=6)
+NUMBER = dict(one=1, two=2, three=3, attend=4, four=4, five=5, six=6, gating=6)
 
 
 class FlatMember:
@@ -1495,13 +1579,7 @@
     task_maps, g_6, g_g, local = head_layer(
         geom, domain, pre_6, st_6, pre_g, st_g, gain[6], bias[6], gain[7], bias[7], dec_cot
     )
-    out_maps = []
-
-    def place_maps(x):
-        out_maps.append(tied(task_maps, x).transpose(1, 0, 2).reshape(frames, rows, cols, TASKS, C_DEC))
-        return out_maps[0]
-
-    both = links.total(jnp.concatenate([local] + [s for _, s in wide], 1), None, ORDER, [place_maps])
+    both = links.total(jnp.concatenate([local] + [s for _, s in wide], 1), None, ORDER)
     sm_6, sm_g, st_a = both[:, :C_DEC], both[:, C_DEC : 4 * C_DEC], both[:, 4 * C_DEC :]
     st_a = [st_a[:, k * C_MID : (k + 1) * C_MID] for k in range(TASKS)]
     pool_args = (geom, domain, pre_3, st_3, gain[2], bias[2])
@@ -1530,7 +1608,7 @@
     mix = early[-1][0]
     low_g, add_4 = gate_back
     blocks = w.add("gating", act_4, low_g)
-    w.send(6)
+    w.send(6, sm_5)
     win_5, g_4, local = backward_layer(
         geom,
         domain,
@@ -1543,7 +1621,7 @@
     both = links.total(
         jnp.concatenate([local] + [e[2] for e in early], 1), w.during(9), ORDER, w.pieces("five", act_4, win_5)
     )
-    w.send(5)
+    w.send(5, both)
     sm_4 = both[:, :C_MID]
     sm_a = [both[:, (k + 1) * C_MID : (k + 2) * C_MID] for k in range(TASKS)]
     win_4, g_3, local = backward_layer(
@@ -1570,23 +1648,28 @@
         return work
 
     sm_3 = links.total(local, w.during(10), ORDER, w.pieces("four", unpooled, win_4) + [attend_back(0)])
-    w.send(4)
     attend_back(1)(sm_3)
     attend_back(2)(backs[-1][1])
     low_a = jnp.concatenate([low for low, _ in backs], 1)
+    blocks = w.add("attend", act_2, low_a)
+    w.send(4)
     win_3, g_2, local = backward_layer(
         geom,
         domain,
-        (g_3, pre_3, st_3, sm_3, gain[2]),
+        (tied(g_3, blocks), pre_3, st_3, sm_3, gain[2]),
         w.get("three"),
         added=backs[-1][1],
         lower=(pre_2, st_2, gain[1], bias[1]),
     )
     w.after_layer(3, local)
-    sm_2 = links.total(
-        local, w.during(11), ORDER, w.pieces("three", act_2, win_3) + [lambda x: w.add("attend", act_2, tied(low_a, x))]
-    )
-    w.send(3)
+    tasks = []
+
+    def task_part(x):
+        tasks.append(task_layer(geom, domain, tied(pre_3, x), *pool_args[3:], masks))
+        return tasks[0]
+
+    sm_2 = links.total(local, w.during(11), ORDER, w.pieces("three", act_2, win_3) + [task_part])
+    w.send(3, sm_2)
     win_2, g_1, local = backward_layer(
         geom,
         domain,
@@ -1596,27 +1679,23 @@
     )
     w.after_layer(2, local)
     sm_1 = links.total(local, w.during(12), ORDER, w.pieces("two", act_1, win_2))
-    w.send(2)
-    win_1 = low_layer(geom, domain, (g_1, pre_1, st_1, sm_1, gain[0]))
+    win_1 = low_layer(geom, domain, (tied(g_1, w.now()), pre_1, st_1, sm_1, gain[0]))
     blocks = w.add("one", source, win_1)
-    frames_grad, task_features = w.tail(
+    frames_grad, task_maps = w.tail(
         blocks,
         (
             lambda to: input_layer(geom, tied(win_1, to), w.get("one")),
-            lambda to: task_layer(geom, domain, tied(pre_3, to), *pool_args[3:], masks),
+            lambda to: tied(task_maps, to).transpose(1, 0, 2).reshape(frames, rows, cols, TASKS, C_DEC),
         ),
     )
-
-    sums = jnp.concatenate([sm_1, sm_2, sm_3, *sm_a, sm_4, sm_5, sm_6, sm_g], 1)
-    shard = gains.shape[0]
-    mine = lax.dynamic_slice_in_dim(sums, lax.axis_index(AXES) * shard, shard, 1)
+    gains_grad, biases_grad = share_of(number(1), [sm_1, sm_2, sm_3, *sm_a, sm_4, sm_5, sm_6, sm_g], gains.shape[0])
     return (
-        task_features.transpose(0, 1, 3, 2, 4),
-        out_maps[0],
+        tasks[0].transpose(0, 1, 3, 2, 4),
+        task_maps,
         frames_grad.reshape(frames, rows, cols, C_IN),
         *(w.grads[n] for n in ("one", "two", "three", "attend", "four", "five", "six", "gating")),
-        mine[2] + mine[3],
-        mine[0] + mine[1],
+        gains_grad,
+        biases_grad,
     )
 
 

time: 584 us -> 559 us (0.957); the launches traced: 573 us -> 555 us
  other arithmetic: 30.9 us -> 8.35 us
  starting transfers between devices: 148 us -> 158 us
  local copies, waits for them, and re-layouts: 24.4 us -> 17.6 us
    pallas_call x0 -> x20, Pallas kernels: none -> 12.3 us  [the longest x19 10.7 us: add_all(): pl.pallas_call(functools.partial(add_kernel, [(work, len(i), len(o)) for...]
    convert_element_type x36 -> x0, other arithmetic: 11.7 us -> none  [plus(): return (a.astype(F32) + b.astype(F32)).astype(BF16)]
    ppermute x166, starting transfers between devices: 148 us -> 158 us  [swap(): return lax.ppermute(x, AXES, [(i, i ^ 1 << bit) for i in range(n)])]
    pallas_call x6, Pallas kernels: 49.5 us -> 41.9 us  [forward_layer(): pl.pallas_call(functools.partial(forward_kernel, geom, norm is not None,...]
    another operation x19 -> x1, other arithmetic: 6.83 us -> 0.71 us  [the longest x18 6.12 us: first(): jnp.stack([plus(near[s, cut:], got[0, s, cut:]), plus(far[s, cut:], got[1...]
    unnamed x247 -> x204, local copies, waits for them, and re-layouts: 20.8 us -> 14.7 us
  transfers between devices with their start and end apart: 166 -> 166, of which waited for: 71 -> 71; matrix products, arithmetic and copies ran while one was open for 6% -> 2% of each run, Pallas kernels for 29% -> 31%
where the time goes in v3:
time: 559 us; the launch traced here: 555 us
  Pallas kernels  205 us (37%)
  waiting for transfers between devices  163 us (29%)
  starting transfers between devices  158 us (28%)
  local copies, waits for them, and re-layouts  17.6 us (3%)
  other arithmetic  8.35 us (1%)
    ppermute x166, waiting for transfers between devices, swap(): return lax.ppermute(x, AXES, [(i, i ^ 1 << bit) for i in range(n)])  163 us
    ppermute x166, starting transfers between devices, swap(): return lax.ppermute(x, AXES, [(i, i ^ 1 << bit) for i in range(n)])  158 us
    pallas_call x5, Pallas kernels, backward_layer(): pl.pallas_call(functools.partial(backward_kernel, geom, added is not None...  51.8 us
    pallas_call x6, Pallas kernels, forward_layer(): pl.pallas_call(functools.partial(forward_kernel, geom, norm is not None,...  41.9 us
    pallas_call x12, Pallas kernels, weight_piece(): pl.pallas_call(functools.partial(weight_piece_kernel, geom, member, step,...  35.3 us
    unnamed x204, local copies, waits for them, and re-layouts  14.7 us
    pallas_call x4, Pallas kernels, weight_blocks(): pl.pallas_call(functools.partial(weight_blocks_kernel, geom, member, step...  13.7 us
    pallas_call x4, Pallas kernels, point_layer(): pl.pallas_call(functools.partial(point_kernel, geom, (mat.member, mat.par...  11.4 us
  transfers between devices with their start and end apart: 166, of which 71 were waited for; matrix products, arithmetic and copies ran while one was open for 2% of the time, Pallas kernels for 31%

profile of v3, /device:TPU:0, one launch (start us, length us, event | category | flops | bytes accessed | tf_op | source)
XLA Modules:
  0.0 555.5 jit_solution(9824696903733660146)
XLA Ops:
  33.7 6.6 %collective-permute-done.16 = bf16[2,592,128]{2,1,0:T(8,128)(2,1)S(1)} collective-permute-done((bf16[2,592,128]{2,1,0:T(8,128)(2,1)S(1)}, bf16[2,592,128]{2,1,0:T(8,128)(2,1)S(1)}, u32[]{:S(2)}, u32[]{:S(2)}) %collective-permute-start.16) | collective-permute-done | bytes 303136 | tf_op jit(solution)/shard_map/ppermute | solution.py:979
  44.8 4.8 shard_map.237
  79.2 8.1 %shard_map.239 = (f32[1024,512]{1,0:T(8,128)S(1)}, f32[4,512]{1,0:T(4,128)S(1)}, bf16[1024,512]{1,0:T(8,128)(2,1)S(1)}, bf16[4608,512]{1,0:T(8,128)(2,1)}) custom-call(s32[2]{0:T(128)S(1)} %copy-done.15, f32[1024,512]{1,0:T(8,128)S(1)} %get-tuple-element.453.refs_1_.refs_7_.pre_ref, f32[4,512]{1,0:T(4,128)S(1)} %add.204.refs_2_.refs_8_.st_ref, ...), custom_call_target="tpu_custom_call" | custom-call | flops 483183808 | bytes 891289 | tf_op jit(solution)/shard_map/pallas_call | solution.py:237
  95.9 4.4 collective-permute-done.30
  114.6 8.0 %shard_map.240 = (f32[1024,512]{1,0:T(8,128)S(1)}, f32[4,512]{1,0:T(4,128)S(1)}, bf16[1024,512]{1,0:T(8,128)(2,1)S(1)}, bf16[4608,512]{1,0:T(8,128)(2,1)}) custom-call(s32[2]{0:T(128)S(1)} %copy-done.15, f32[1024,512]{1,0:T(8,128)S(1)} %get-tuple-element.473.refs_1_.refs_8_.refs_2_, f32[4,512]{1,0:T(4,128)S(1)} %add.209.refs_2_.refs_9_.refs_3_, ...), custom_call_target="tpu_custom_call" | custom-call | flops 483183808 | bytes 891289 | tf_op jit(solution)/shard_map/pallas_call | solution.py:237
  153.6 8.0 %shard_map.242 = (f32[1024,512]{1,0:T(8,128)S(1)}, f32[4,512]{1,0:T(4,128)S(1)}, bf16[4608,512]{1,0:T(8,128)(2,1)}) custom-call(s32[2]{0:T(128)S(1)} %copy-done.15, bf16[1024,512]{1,0:T(8,128)(2,1)S(1)} %shard_map.241.refs_1_, s32[1]{0:T(128)} %bitcast.1.refs_2_.me_ref.refs_5_.refs_0_, bf16[8,288,128]{2,1,0:T(8,128)(2,1)} %copy-done.53, ...), custom_call_target="tpu_custom_call" | custom-call | flops 483183808 | bytes 891289 | tf_op jit(solution)/shard_map/pallas_call | solution.py:237
  170.3 4.1 collective-permute-done.60
  187.8 8.0 %shard_map.243 = (f32[1024,512]{1,0:T(8,128)S(1)}, f32[4,512]{1,0:T(4,128)S(1)}, bf16[1024,512]{1,0:T(8,128)(2,1)S(1)}, bf16[4608,512]{1,0:T(8,128)(2,1)}) custom-call(s32[2]{0:T(128)S(1)} %copy-done.15, f32[1024,512]{1,0:T(8,128)S(1)} %get-tuple-element.507.refs_1_.refs_8_.refs_2_, f32[4,512]{1,0:T(4,128)S(1)} %add.219.refs_2_.refs_9_.refs_3_, ...), custom_call_target="tpu_custom_call" | custom-call | flops 483183808 | bytes 891289 | tf_op jit(solution)/shard_map/pallas_call | solution.py:237
  221.2 4.9 shard_map.244
  259.7 4.5 collective-permute-done.94
  272.4 7.1 %shard_map.251 = (bf16[3,2,18,32,256]{4,3,2,1,0:T(8,128)(2,1)S(1)}, f32[1024,512]{1,0:T(8,128)S(1)}, f32[4,512]{1,0:T(4,128)S(1)}) custom-call(s32[2]{0:T(128)S(1)} %copy-done.15, f32[1024,256]{1,0:T(8,128)S(1)} %get-tuple-element.555.refs_1_, f32[1024,256]{1,0:T(8,128)S(1)} %get-tuple-element.540.bot_ref.refs_2_, f32[4,256]{1,0:T(4,128)S(1)} %slice.353.bot_st.refs_3_, ...), custom_call_target="tpu_custom_call" | custom-call | flops 241591904 | bytes 1284505 | tf_op jit(solution)/shard_map/pallas_call | solution.py:585
  281.3 4.4 shard_map.252
  304.5 10.3 %shard_map.257 = (bf16[3,2,18,32,512]{4,3,2,1,0:T(8,128)(2,1)S(1)}, f32[1024,512]{1,0:T(8,128)S(1)}, f32[4,512]{1,0:T(4,128)S(1)}) custom-call(s32[2]{0:T(128)S(1)} %copy-done.15, f32[1024,512]{1,0:T(8,128)S(1)} %get-tuple-element.575.refs_1_, f32[1024,512]{1,0:T(8,128)S(1)} %get-tuple-element.524.refs_1_.refs_7_.refs_2_, ...), custom_call_target="tpu_custom_call" | custom-call | flops 483183808 | bytes 1520435 | tf_op jit(solution)/shard_map/pallas_call | solution.py:585
  338.9 12.9 %shard_map.263 = (bf16[3,2,18,32,512]{4,3,2,1,0:T(8,128)(2,1)S(1)}, f32[1024,512]{1,0:T(8,128)S(1)}, f32[4,512]{1,0:T(4,128)S(1)}) custom-call(s32[2]{0:T(128)S(1)} %copy-done.15, f32[1024,512]{1,0:T(8,128)S(1)} %get-tuple-element.585.refs_1_, f32[1024,512]{1,0:T(8,128)S(1)} %get-tuple-element.507.refs_1_.refs_8_.refs_2_, ...), custom_call_target="tpu_custom_call" | custom-call | flops 483183808 | bytes 1520435 | tf_op jit(solution)/shard_map/pallas_call | solution.py:585
  387.0 10.9 %shard_map.274 = (bf16[3,2,18,32,512]{4,3,2,1,0:T(8,128)(2,1)S(1)}, f32[1024,512]{1,0:T(8,128)S(1)}, f32[4,512]{1,0:T(4,128)S(1)}) custom-call(s32[2]{0:T(128)S(1)} %copy-done.15, f32[1024,512]{1,0:T(8,128)S(1)} %get-tuple-element.681.refs_1_, f32[1024,512]{1,0:T(8,128)S(1)} %get-tuple-element.733.top_ref.refs_7_.refs_2_, ...), custom_call_target="tpu_custom_call" | custom-call | flops 483183808 | bytes 1520435 | tf_op jit(solution)/shard_map/pallas_call | solution.py:585
  412.0 6.0 %collective-permute-done.128.refs_2_ = bf16[8,384,128]{2,1,0:T(8,128)(2,1)S(1)} collective-permute-done((bf16[8,384,128]{2,1,0:T(8,128)(2,1)S(1)}, bf16[8,384,128]{2,1,0:T(8,128)(2,1)S(1)}, u32[]{:S(2)}, u32[]{:S(2)}) %collective-permute-start.128) | collective-permute-done | bytes 786464 | tf_op jit(solution)/shard_map/ppermute | solution.py:979
  423.7 5.3 shard_map.281
  433.6 10.5 %shard_map.282 = (bf16[3,2,18,32,512]{4,3,2,1,0:T(8,128)(2,1)S(1)}, f32[1024,512]{1,0:T(8,128)S(1)}, f32[4,512]{1,0:T(4,128)S(1)}) custom-call(s32[2]{0:T(128)S(1)} %copy-done.15, f32[1024,512]{1,0:T(8,128)S(1)} %get-tuple-element.735.refs_1_, f32[1024,512]{1,0:T(8,128)S(1)} %get-tuple-element.473.refs_1_.refs_8_.refs_2_, ...), custom_call_target="tpu_custom_call" | custom-call | flops 483183808 | bytes 1520435 | tf_op jit(solution)/shard_map/pallas_call | solution.py:585
  468.9 6.9 %collective-permute-done.143.refs_1_ = bf16[2,768,128]{2,1,0:T(8,128)(2,1)S(1)} collective-permute-done((bf16[2,768,128]{2,1,0:T(8,128)(2,1)S(1)}, bf16[2,768,128]{2,1,0:T(8,128)(2,1)S(1)}, u32[]{:S(2)}, u32[]{:S(2)}) %collective-permute-start.143) | collective-permute-done | bytes 393248 | tf_op jit(solution)/shard_map/ppermute | solution.py:979
  489.2 4.2 shard_map.291
  493.4 5.4 shard_map.292
  498.9 5.5 collective-permute-done.148.refs_6_
  507.9 6.4 %collective-permute-done.151.refs_5_ = bf16[4,288,128]{2,1,0:T(8,128)(2,1)S(1)} collective-permute-done((bf16[4,288,128]{2,1,0:T(8,128)(2,1)S(1)}, bf16[4,288,128]{2,1,0:T(8,128)(2,1)S(1)}, u32[]{:S(2)}, u32[]{:S(2)}) %collective-permute-start.151) | collective-permute-done | bytes 294944 | tf_op jit(solution)/shard_map/ppermute | solution.py:979
  528.1 5.8 %collective-permute-done.158.refs_1_ = bf16[2,576,128]{2,1,0:T(8,128)(2,1)S(1)} collective-permute-done((bf16[2,576,128]{2,1,0:T(8,128)(2,1)S(1)}, bf16[2,576,128]{2,1,0:T(8,128)(2,1)S(1)}, u32[]{:S(2)}, u32[]{:S(2)}) %collective-permute-start.158) | collective-permute-done | bytes 294944 | tf_op jit(solution)/shard_map/ppermute | solution.py:979
  (708 shorter events, 388.9 us)
Async XLA Ops:
  49.8 18.5 %collective-permute-start.22 = (bf16[8,304,128]{2,1,0:T(8,128)(2,1)S(1)}, bf16[8,304,128]{2,1,0:T(8,128)(2,1)S(1)}, u32[]{:S(2)}, u32[]{:S(2)}) collective-permute-start(bf16[8,304,128]{2,1,0:T(8,128)(2,1)S(1)} %constant_dynamic-update-slice_fusion.11.refs_2_.refs_8_), channel_id=1, source_target_pairs={{0,4},{1,5},{2,6},{3,7},{4,0},{5,1},{6,2},{7,3},{8,12},{9,13},{10,... | collective-permute-start | bytes 1867784 | tf_op jit(solution)/shard_map/ppermute | solution.py:979
  87.5 15.2 %collective-permute-start.35 = (bf16[8,288,128]{2,1,0:T(8,128)(2,1)S(1)}, bf16[8,288,128]{2,1,0:T(8,128)(2,1)S(1)}, u32[]{:S(2)}, u32[]{:S(2)}) collective-permute-start(bf16[8,288,128]{2,1,0:T(8,128)(2,1)S(1)} %constant_dynamic-update-slice_fusion.15.refs_6_), channel_id=1, source_target_pairs={{0,2},{1,3},{2,0},{3,1},{4,6},{5,7},{6,4},{7,5},{8,10},{9,11},{10,... | collective-permute-start | bytes 1769480 | tf_op jit(solution)/shard_map/ppermute | solution.py:979
  88.4 17.9 %collective-permute-start.37 = (bf16[8,288,128]{2,1,0:T(8,128)(2,1)S(1)}, bf16[8,288,128]{2,1,0:T(8,128)(2,1)S(1)}, u32[]{:S(2)}, u32[]{:S(2)}) collective-permute-start(bf16[8,288,128]{2,1,0:T(8,128)(2,1)S(1)} %constant_dynamic-update-slice_fusion.17.refs_8_), channel_id=1, source_target_pairs={{0,4},{1,5},{2,6},{3,7},{4,0},{5,1},{6,2},{7,3},{8,12},{9,13},{10,... | collective-permute-start | bytes 1769480 | tf_op jit(solution)/shard_map/ppermute | solution.py:979
  122.8 14.9 %collective-permute-start.50 = (bf16[8,288,128]{2,1,0:T(8,128)(2,1)S(1)}, bf16[8,288,128]{2,1,0:T(8,128)(2,1)S(1)}, u32[]{:S(2)}, u32[]{:S(2)}) collective-permute-start(bf16[8,288,128]{2,1,0:T(8,128)(2,1)S(1)} %constant_dynamic-update-slice_fusion.21.refs_3_), channel_id=1, source_target_pairs={{0,2},{1,3},{2,0},{3,1},{4,6},{5,7},{6,4},{7,5},{8,10},{9,11},{10,... | collective-permute-start | bytes 1769480 | tf_op jit(solution)/shard_map/ppermute | solution.py:979
  124.5 16.9 %collective-permute-start.52 = (bf16[8,288,128]{2,1,0:T(8,128)(2,1)S(1)}, bf16[8,288,128]{2,1,0:T(8,128)(2,1)S(1)}, u32[]{:S(2)}, u32[]{:S(2)}) collective-permute-start(bf16[8,288,128]{2,1,0:T(8,128)(2,1)S(1)} %constant_dynamic-update-slice_fusion.23.refs_5_), channel_id=1, source_target_pairs={{0,4},{1,5},{2,6},{3,7},{4,0},{5,1},{6,2},{7,3},{8,12},{9,13},{10,... | collective-permute-start | bytes 1769480 | tf_op jit(solution)/shard_map/ppermute | solution.py:979
  145.3 16.4 %collective-permute-start.63 = (bf16[4,288,128]{2,1,0:T(8,128)(2,1)S(1)}, bf16[4,288,128]{2,1,0:T(8,128)(2,1)S(1)}, u32[]{:S(2)}, u32[]{:S(2)}) collective-permute-start(bf16[4,288,128]{2,1,0:T(8,128)(2,1)S(1)} %get-tuple-element.517), channel_id=1, source_target_pairs={{0,2},{1,3},{2,0},{3,1},{4,6},{5,7},{6,4},{7,5},{8,10},{9,11},{10,... | collective-permute-start | bytes 884744 | tf_op jit(solution)/shard_map/ppermute | solution.py:979
  161.8 15.0 %collective-permute-start.65 = (bf16[8,288,128]{2,1,0:T(8,128)(2,1)S(1)}, bf16[8,288,128]{2,1,0:T(8,128)(2,1)S(1)}, u32[]{:S(2)}, u32[]{:S(2)}) collective-permute-start(bf16[8,288,128]{2,1,0:T(8,128)(2,1)S(1)} %constant_dynamic-update-slice_fusion.27.refs_6_), channel_id=1, source_target_pairs={{0,2},{1,3},{2,0},{3,1},{4,6},{5,7},{6,4},{7,5},{8,10},{9,11},{10,... | collective-permute-start | bytes 1769480 | tf_op jit(solution)/shard_map/ppermute | solution.py:979
  163.3 17.2 %collective-permute-start.67 = (bf16[8,288,128]{2,1,0:T(8,128)(2,1)S(1)}, bf16[8,288,128]{2,1,0:T(8,128)(2,1)S(1)}, u32[]{:S(2)}, u32[]{:S(2)}) collective-permute-start(bf16[8,288,128]{2,1,0:T(8,128)(2,1)S(1)} %constant_dynamic-update-slice_fusion.29.refs_8_), channel_id=1, source_target_pairs={{0,4},{1,5},{2,6},{3,7},{4,0},{5,1},{6,2},{7,3},{8,12},{9,13},{10,... | collective-permute-start | bytes 1769480 | tf_op jit(solution)/shard_map/ppermute | solution.py:979
  196.0 15.2 %collective-permute-start.79 = (bf16[8,288,128]{2,1,0:T(8,128)(2,1)S(1)}, bf16[8,288,128]{2,1,0:T(8,128)(2,1)S(1)}, u32[]{:S(2)}, u32[]{:S(2)}) collective-permute-start(bf16[8,288,128]{2,1,0:T(8,128)(2,1)S(1)} %constant_dynamic-update-slice_fusion.33.refs_6_.refs_3_.refs_0_), channel_id=1, source_target_pairs={{0,2},{1,3},{2,0},{3,1},{4,6},{5,7},{6,4},{7,5},{8,10},{9,11},{10,... | collective-permute-start | bytes 1769480 | tf_op jit(solution)/shard_map/ppermute | solution.py:979
  197.3 17.6 %collective-permute-start.81 = (bf16[8,288,128]{2,1,0:T(8,128)(2,1)S(1)}, bf16[8,288,128]{2,1,0:T(8,128)(2,1)S(1)}, u32[]{:S(2)}, u32[]{:S(2)}) collective-permute-start(bf16[8,288,128]{2,1,0:T(8,128)(2,1)S(1)} %constant_dynamic-update-slice_fusion.35.refs_8_.refs_5_.refs_2_), channel_id=1, source_target_pairs={{0,4},{1,5},{2,6},{3,7},{4,0},{5,1},{6,2},{7,3},{8,12},{9,13},{10,... | collective-permute-start | bytes 1769480 | tf_op jit(solution)/shard_map/ppermute | solution.py:979
  336.5 15.3 %collective-permute-start.113 = (bf16[2,8,576,128]{3,2,1,0:T(8,128)(2,1)}, bf16[2,8,576,128]{3,2,1,0:T(8,128)(2,1)S(1)}, u32[]{:S(2)}, u32[]{:S(2)}) collective-permute-start(bf16[2,8,576,128]{3,2,1,0:T(8,128)(2,1)} %get-tuple-element.633), channel_id=1, source_target_pairs={{0,1},{1,0},{2,3},{3,2},{4,5},{5,4},{6,7},{7,6},{8,9},{9,8},{10,11... | collective-permute-start | bytes 7077896 | tf_op jit(solution)/shard_map/ppermute | solution.py:979
  336.8 15.0 %collective-permute-start.114 = (bf16[4,192,128]{2,1,0:T(8,128)(2,1)S(1)}, bf16[4,192,128]{2,1,0:T(8,128)(2,1)S(1)}, u32[]{:S(2)}, u32[]{:S(2)}) collective-permute-start(bf16[4,192,128]{2,1,0:T(8,128)(2,1)S(1)} %get-tuple-element.645), channel_id=1, source_target_pairs={{0,4},{1,5},{2,6},{3,7},{4,0},{5,1},{6,2},{7,3},{8,12},{9,13},{10,... | collective-permute-start | bytes 589832 | tf_op jit(solution)/shard_map/ppermute | solution.py:979
  352.5 15.2 %collective-permute-start.116 = (bf16[8,288,128]{2,1,0:T(8,128)(2,1)S(1)}, bf16[8,288,128]{2,1,0:T(8,128)(2,1)S(1)}, u32[]{:S(2)}, u32[]{:S(2)}) collective-permute-start(bf16[8,288,128]{2,1,0:T(8,128)(2,1)S(1)} %get-tuple-element.651), channel_id=1, source_target_pairs={{0,2},{1,3},{2,0},{3,1},{4,6},{5,7},{6,4},{7,5},{8,10},{9,11},{10,... | collective-permute-start | bytes 1769480 | tf_op jit(solution)/shard_map/ppermute | solution.py:979
  353.5 14.9 %collective-permute-start.117 = (bf16[2,4,288,128]{3,2,1,0:T(8,128)(2,1)S(1)}, bf16[2,4,288,128]{3,2,1,0:T(8,128)(2,1)S(1)}, u32[]{:S(2)}, u32[]{:S(2)}) collective-permute-start(bf16[2,4,288,128]{3,2,1,0:T(8,128)(2,1)S(1)} %get-tuple-element.653), channel_id=1, source_target_pairs={{0,4},{1,5},{2,6},{3,7},{4,0},{5,1},{6,2},{7,3},{8,12},{9,13},{10,... | collective-permute-start | bytes 1769480 | tf_op jit(solution)/shard_map/ppermute | solution.py:979
  398.8 19.2 %collective-permute-start.128 = (bf16[8,384,128]{2,1,0:T(8,128)(2,1)S(1)}, bf16[8,384,128]{2,1,0:T(8,128)(2,1)S(1)}, u32[]{:S(2)}, u32[]{:S(2)}) collective-permute-start(bf16[8,384,128]{2,1,0:T(8,128)(2,1)S(1)} %get-tuple-element.717), channel_id=1, source_target_pairs={{0,2},{1,3},{2,0},{3,1},{4,6},{5,7},{6,4},{7,5},{8,10},{9,11},{10,... | collective-permute-start | bytes 2359304 | tf_op jit(solution)/shard_map/ppermute | solution.py:979
  399.8 18.8 %collective-permute-start.129 = (bf16[2,4,384,128]{3,2,1,0:T(8,128)(2,1)S(1)}, bf16[2,4,384,128]{3,2,1,0:T(8,128)(2,1)S(1)}, u32[]{:S(2)}, u32[]{:S(2)}) collective-permute-start(bf16[2,4,384,128]{3,2,1,0:T(8,128)(2,1)S(1)} %get-tuple-element.719), channel_id=1, source_target_pairs={{0,4},{1,5},{2,6},{3,7},{4,0},{5,1},{6,2},{7,3},{8,12},{9,13},{10,... | collective-permute-start | bytes 2359304 | tf_op jit(solution)/shard_map/ppermute | solution.py:979
  429.1 15.1 %collective-permute-start.133 = (bf16[2,8,576,128]{3,2,1,0:T(8,128)(2,1)S(1)}, bf16[2,8,576,128]{3,2,1,0:T(8,128)(2,1)S(1)}, u32[]{:S(2)}, u32[]{:S(2)}) collective-permute-start(bf16[2,8,576,128]{3,2,1,0:T(8,128)(2,1)S(1)} %copy-done.30), channel_id=1, source_target_pairs={{0,1},{1,0},{2,3},{3,2},{4,5},{5,4},{6,7},{7,6},{8,9},{9,8},{10,11... | collective-permute-start | bytes 7077896 | tf_op jit(solution)/shard_map/ppermute | solution.py:979
  464.2 16.0 %collective-permute-start.145 = (bf16[2,8,576,128]{3,2,1,0:T(8,128)(2,1)}, bf16[2,8,576,128]{3,2,1,0:T(8,128)(2,1)S(1)}, u32[]{:S(2)}, u32[]{:S(2)}) collective-permute-start(bf16[2,8,576,128]{3,2,1,0:T(8,128)(2,1)} %get-tuple-element.797), channel_id=1, source_target_pairs={{0,1},{1,0},{2,3},{3,2},{4,5},{5,4},{6,7},{7,6},{8,9},{9,8},{10,11... | collective-permute-start | bytes 7077896 | tf_op jit(solution)/shard_map/ppermute | solution.py:979
  483.5 20.8 %collective-permute-start.146 = (bf16[8,288,128]{2,1,0:T(8,128)(2,1)S(1)}, bf16[8,288,128]{2,1,0:T(8,128)(2,1)S(1)}, u32[]{:S(2)}, u32[]{:S(2)}) collective-permute-start(bf16[8,288,128]{2,1,0:T(8,128)(2,1)S(1)} %get-tuple-element.808), channel_id=1, source_target_pairs={{0,2},{1,3},{2,0},{3,1},{4,6},{5,7},{6,4},{7,5},{8,10},{9,11},{10,... | collective-permute-start | bytes 1769480 | tf_op jit(solution)/shard_map/ppermute | solution.py:979
  484.6 19.8 %collective-permute-start.147 = (bf16[2,4,288,128]{3,2,1,0:T(8,128)(2,1)S(1)}, bf16[2,4,288,128]{3,2,1,0:T(8,128)(2,1)S(1)}, u32[]{:S(2)}, u32[]{:S(2)}) collective-permute-start(bf16[2,4,288,128]{3,2,1,0:T(8,128)(2,1)S(1)} %get-tuple-element.809), channel_id=1, source_target_pairs={{0,4},{1,5},{2,6},{3,7},{4,0},{5,1},{6,2},{7,3},{8,12},{9,13},{10,... | collective-permute-start | bytes 1769480 | tf_op jit(solution)/shard_map/ppermute | solution.py:979
  485.5 18.8 %collective-permute-start.148 = (bf16[4,288,128]{2,1,0:T(8,128)(2,1)S(1)}, bf16[4,288,128]{2,1,0:T(8,128)(2,1)S(1)}, u32[]{:S(2)}, u32[]{:S(2)}) collective-permute-start(bf16[4,288,128]{2,1,0:T(8,128)(2,1)S(1)} %get-tuple-element.817), channel_id=1, source_target_pairs={{0,4},{1,5},{2,6},{3,7},{4,0},{5,1},{6,2},{7,3},{8,12},{9,13},{10,... | collective-permute-start | bytes 884744 | tf_op jit(solution)/shard_map/ppermute | solution.py:979
  486.6 17.8 %collective-permute-start.149 = (bf16[4,288,128]{2,1,0:T(8,128)(2,1)S(1)}, bf16[4,288,128]{2,1,0:T(8,128)(2,1)S(1)}, u32[]{:S(2)}, u32[]{:S(2)}) collective-permute-start(bf16[4,288,128]{2,1,0:T(8,128)(2,1)S(1)} %get-tuple-element.818), channel_id=1, source_target_pairs={{0,2},{1,3},{2,0},{3,1},{4,6},{5,7},{6,4},{7,5},{8,10},{9,11},{10,... | collective-permute-start | bytes 884744 | tf_op jit(solution)/shard_map/ppermute | solution.py:979
  518.6 19.7 %collective-permute-start.164 = (f32[288,64]{1,0:T(8,128)S(1)}, f32[288,64]{1,0:T(8,128)S(1)}, u32[]{:S(2)}, u32[]{:S(2)}) collective-permute-start(f32[288,64]{1,0:T(8,128)S(1)} %slice_select_fusion.1), channel_id=1, source_target_pairs={{0,1},{1,0},{2,3},{3,2},{4,5},{5,4},{6,7},{7,6},{8,9},{9,8},{10,11... | collective-permute-start | bytes 221192 | tf_op jit(solution)/shard_map/ppermute | solution.py:979
  519.1 15.4 %collective-permute-start.159 = (bf16[576,128]{1,0:T(8,128)(2,1)S(1)}, bf16[576,128]{1,0:T(8,128)(2,1)S(1)}, u32[]{:S(2)}, u32[]{:S(2)}) collective-permute-start(bf16[576,128]{1,0:T(8,128)(2,1)S(1)} %get-tuple-element.862), channel_id=1, source_target_pairs={{0,16},{1,17},{2,18},{3,19},{4,20},{5,21},{6,22},{7,23},{8,24},{9,... | collective-permute-start | bytes 442376 | tf_op jit(solution)/shard_map/ppermute | solution.py:979
  (229 other events, 1909.1 us)

commit v4 on v3

--- a/solution.py
+++ b/solution.py
@@ -79,6 +79,15 @@
     return jnp.sum(x.reshape(-1, 8, x.shape[-1]), 0)
 
 
+def value_sums(parts, domain_ref, others=None):
+    others = parts if others is None else others
+    return by_domain(
+        [jnp.sum(fold(p), 0, keepdims=True) for p in parts],
+        [jnp.sum(fold(p * o), 0, keepdims=True) for p, o in zip(parts, others)],
+        domain_ref,
+    )
+
+
 def put_windows(win_ref, f, row, value, cols):
     col = lax.broadcasted_iota(jnp.int32, value.shape, 0)
     left = jnp.where(col == 0, 0.0, pltpu.roll(value, 1, 0))
@@ -119,7 +128,7 @@
 class Pieces:
     def __init__(self, member, parts, me, sources):
         self.member, self.parts, self.me = member, parts, me
-        self.sources = [in_hbm(x) for x in sources]
+        self.sources = list(sources)
         self.shape = member.shape
 
 
@@ -272,26 +281,37 @@
     return top
 
 
+def row_pairs(x, cols):
+    x = x.reshape(-1, 2, cols, x.shape[-1])
+    return x[:, 0], x[:, 1]
+
+
+def pair_sums(x):
+    cols = x.shape[1]
+    even = lax.broadcasted_iota(jnp.int32, x.shape, 1) % 2 == 0
+    return x + jnp.where(even, pltpu.roll(x, cols - 1, 1), pltpu.roll(x, 1, 1))
+
+
+def window_weights(top):
+    exps = [jnp.exp(t) for t in top]
+    share = 1.0 / pair_sums(exps[0] + exps[1])
+    return [e * share for e in exps]
+
+
 def pool_kernel(geom, domain_ref, top_ref, top_st, gain_t, bias_t, un_ref):
     frames, rows, cols, counts = geom
     pixels = rows * cols
     for f in range(frames):
+        at = slice(f * pixels, (f + 1) * pixels)
         for lane in range(0, top_ref.shape[-1], LANES):
             lanes = slice(lane, lane + LANES)
             average, inverse = frame_tables(top_st[:, lanes], domain_ref[f], counts)
             scale = inverse * gain_t[:, lanes]
-            shift = bias_t[:, lanes] - average * scale
-
-            def one(i, _):
-                at = [pl.multiple_of(f * pixels + (2 * i + h) * cols, cols) for h in (0, 1)]
-                top = top_rows(top_ref, at, cols, lanes, scale, shift)
-                weight = softmax_window(top, cols)
-                pooled = pair_sum(weight[0] * top[0] + weight[1] * top[1], cols)
-                for h in (0, 1):
-                    un_ref[pl.ds(at[h], cols), lanes] = (weight[h] * pooled).astype(BF16)
-                return 0
-
-            lax.fori_loop(0, rows // 2, one, 0, unroll=2)
+            act = top_ref[at, lanes] * scale + (bias_t[:, lanes] - average * scale)
+            top = row_pairs(act * sigmoid(act), cols)
+            weight = window_weights(top)
+            pooled = pair_sums(weight[0] * top[0] + weight[1] * top[1])
+            un_ref[at, lanes] = jnp.stack([w * pooled for w in weight], 1).reshape(pixels, LANES).astype(BF16)
 
 
 def pool_layer(geom, domain, top, top_st, gain_t, bias_t):
@@ -421,45 +441,34 @@
     chans = bot_ref.shape[-1]
     for lane in range(0, chans, LANES):
         lanes = slice(lane, lane + LANES)
-        sums = []
+        grads, hats = ([[] for _ in range(TASKS + 1)] for _ in range(2))
         for f in range(frames):
-            b_mean, b_inv = frame_tables(bot_st[:, lanes], domain_ref[f], counts)
-            gate = []
+            at = slice(f * pixels, (f + 1) * pixels)
+            mean, inv = frame_tables(bot_st[:, lanes], domain_ref[f], counts)
+            b_hat = (bot_ref[at, lanes] - mean) * inv
+            act = b_hat * gain_b[:, lanes] + bias_b[:, lanes]
+            s = sigmoid(act)
+            bottom = act * s
+            back = None
             for k in range(TASKS):
                 sl = slice(k * chans + lane, k * chans + lane + LANES)
-                gate.append((sl, *frame_tables(gate_st[:, sl], domain_ref[f], counts)))
-
-            def one(r, carry):
-                at = pl.multiple_of(f * pixels + r * cols, cols)
-                b_hat = (bot_ref[pl.ds(at, cols), lanes] - b_mean) * b_inv
-                act = b_hat * gain_b[:, lanes] + bias_b[:, lanes]
-                s = sigmoid(act)
-                bottom = act * s
-                back = None
-                new = []
-                for k in range(TASKS):
-                    sl, mean, inv = gate[k]
-                    xhat = (gate_ref[pl.ds(at, cols), sl] - mean) * inv
-                    value = sigmoid(xhat * gain_g[:, sl] + bias_g[:, sl])
-                    maps_ref[k, pl.ds(at, cols), lanes] = value * bottom
-                    cot = cot_ref[k, pl.ds(at, cols), lanes].astype(F32)
-                    part = cot * value
-                    back = part if back is None else back + part
-                    g = part * bottom * (1.0 - value)
-                    gg_ref[pl.ds(at, cols), sl] = g
-                    new += [carry[2 * k] + fold(g), carry[2 * k + 1] + fold(g * xhat)]
-                g = back * (s * (1.0 + act * (1.0 - s)))
-                gb_ref[pl.ds(at, cols), lanes] = g
-                new += [carry[-2] + fold(g), carry[-1] + fold(g * b_hat)]
-                return tuple(new)
-
-            zero = jnp.zeros((8, LANES), F32)
-            sums.append(lax.fori_loop(0, rows, one, (zero,) * (2 * TASKS + 2), unroll=2))
+                mean, inv = frame_tables(gate_st[:, sl], domain_ref[f], counts)
+                xhat = (gate_ref[at, sl] - mean) * inv
+                value = sigmoid(xhat * gain_g[:, sl] + bias_g[:, sl])
+                maps_ref[k, at, lanes] = value * bottom
+                part = cot_ref[k, at, lanes].astype(F32) * value
+                back = part if back is None else back + part
+                g = part * bottom * (1.0 - value)
+                gg_ref[at, sl] = g
+                grads[k].append(g)
+                hats[k].append(xhat)
+            g = back * (s * (1.0 + act * (1.0 - s)))
+            gb_ref[at, lanes] = g
+            grads[-1].append(g)
+            hats[-1].append(b_hat)
         for k in range(TASKS + 1):
-            first = [jnp.sum(s[2 * k], 0, keepdims=True) for s in sums]
-            second = [jnp.sum(s[2 * k + 1], 0, keepdims=True) for s in sums]
-            at = chans + k * chans + lane if k < TASKS else lane
-            sums_ref[:, at : at + LANES] = by_domain(first, second, domain_ref)
+            to = chans + k * chans + lane if k < TASKS else lane
+            sums_ref[:, to : to + LANES] = value_sums(grads[k], domain_ref, hats[k])
 
 
 def head_layer(geom, domain, bot, bot_st, gate, gate_st, gain_b, bias_b, gain_g, bias_g, cot):
@@ -520,62 +529,52 @@
     source = jnp.concatenate([window(win_ref, 2 - b, 2 - a, rows) for a in range(3) for b in range(3)], 1)
     weight = jnp.concatenate([held_ref[k * chans : (k + 1) * chans, :] for k in range(9)], 1)
     out = lax.dot_general(source, weight, (((1,), (1,)), ((), ())), preferred_element_type=F32)
-    out_ref[...] = out + add_ref[...] if added else out
-
+    if added:
+        out = out + add_ref[...]
+    if epilogue == "silu":
+        first, second = [], []
+        for f in range(frames):
+            at = slice(f * pixels, (f + 1) * pixels)
+            mean, inv = frame_tables(lst_ref[...], domain_ref[f], counts)
+            xhat = (lpre_ref[at] - mean) * inv
+            act = xhat * lgain_ref[...] + lbias_ref[...]
+            s = sigmoid(act)
+            g = out[at] * (s * (1.0 + act * (1.0 - s)))
+            out_ref[at] = g
+            first.append(jnp.sum(fold(g), 0, keepdims=True))
+            second.append(jnp.sum(fold(g * xhat), 0, keepdims=True))
+        sums_ref[...] = by_domain(first, second, domain_ref)
+        return
     for lane in range(0, chans, LANES):
         lanes = slice(lane, lane + LANES)
-        sums = []
+        first, second = [], []
         for f in range(frames):
+            at = slice(f * pixels, (f + 1) * pixels)
             mean, inv = frame_tables(lst_ref[:, lanes], domain_ref[f], counts)
-
-            def slope(at):
-                xhat = (lpre_ref[pl.ds(at, cols), lanes] - mean) * inv
-                act = xhat * lgain_ref[:, lanes] + lbias_ref[:, lanes]
-                s = sigmoid(act)
-                return xhat, act * s, s * (1.0 + act * (1.0 - s))
-
-            def finish(at, g, xhat, carry):
-                out_ref[pl.ds(at, cols), lanes] = g
-                return carry[0] + fold(g), carry[1] + fold(g * xhat)
-
-            def one_row(r, carry):
-                at = pl.multiple_of(f * pixels + r * cols, cols)
-                xhat, _, steep = slope(at)
-                return finish(at, out_ref[pl.ds(at, cols), lanes] * steep, xhat, carry)
-
-            def one_pair(i, carry):
-                at = [pl.multiple_of(f * pixels + (2 * i + h) * cols, cols) for h in (0, 1)]
-                xhat, top, steep = zip(*(slope(a) for a in at))
-                weight = softmax_window(top, cols)
-                up = [out_ref[pl.ds(a, cols), lanes] for a in at]
-                mix = [mix_ref[pl.ds(a, cols), lanes] for a in at]
-                pooled = pair_sum(weight[0] * top[0] + weight[1] * top[1], cols)
-                d_pool = pair_sum(weight[0] * up[0] + weight[1] * up[1], cols)
-                flow = [m + d_pool for m in mix]
-                d_w = [u * pooled + fl * t for u, fl, t in zip(up, flow, top)]
-                centre = pair_sum(weight[0] * d_w[0] + weight[1] * d_w[1], cols)
-                for h in (0, 1):
-                    d_top = weight[h] * (flow[h] + d_w[h] - centre)
-                    carry = finish(at[h], d_top * steep[h], xhat[h], carry)
-                return carry
-
-            zero = jnp.zeros((8, LANES), F32)
-            if epilogue == "silu":
-                sums.append(lax.fori_loop(0, rows, one_row, (zero, zero), unroll=2))
-            else:
-                sums.append(lax.fori_loop(0, rows // 2, one_pair, (zero, zero)))
-        sums_ref[:, lanes] = by_domain(
-            [jnp.sum(s[0], 0, keepdims=True) for s in sums],
-            [jnp.sum(s[1], 0, keepdims=True) for s in sums],
-            domain_ref,
-        )
+            xhat = (lpre_ref[at, lanes] - mean) * inv
+            act = xhat * lgain_ref[:, lanes] + lbias_ref[:, lanes]
+            s = sigmoid(act)
+            steep = s * (1.0 + act * (1.0 - s))
+            top, up, mix = (row_pairs(x, cols) for x in (act * s, out[at, lanes], mix_ref[at, lanes]))
+            weight = window_weights(top)
+            pooled = pair_sums(weight[0] * top[0] + weight[1] * top[1])
+            d_pool = pair_sums(weight[0] * up[0] + weight[1] * up[1])
+            flow = [m + d_pool for m in mix]
+            d_w = [u * pooled + fl * t for u, fl, t in zip(up, flow, top)]
+            centre = pair_sums(weight[0] * d_w[0] + weight[1] * d_w[1])
+            d_top = jnp.stack([w * (fl + d - centre) for w, fl, d in zip(weight, flow, d_w)], 1)
+            g = d_top.reshape(pixels, LANES) * steep
+            out_ref[at, lanes] = g
+            first.append(jnp.sum(fold(g), 0, keepdims=True))
+            second.append(jnp.sum(fold(g * xhat), 0, keepdims=True))
+        sums_ref[:, lanes] = by_domain(first, second, domain_ref)
 
 
 def backward_layer(geom, domain, top, kernel, lower, added=None, mix=None):
     frames, rows, cols, _ = geom
     pix, width = top[0].shape
     chans = kernel.shape[0] // 9
-    args = [domain, *top, in_hbm(kernel)]
+    args = [domain, *top, kernel]
     specs = [SCALARS] + [whole(x.shape) for x in top] + [ANYWHERE]
     win = (3, frames, rows + 2, cols, width)
     outs = [sds(win, BF16), sds((pix, chans), F32)]
@@ -794,8 +793,8 @@
     win = low.ndim == 5
     steps = 3 if win else 1
     shard = (rows, LANES)
-    outs = [pltpu.HBM((8, *shard), BF16)] * 2 + [pltpu.HBM((2, 8, *shard), BF16)]
-    args = [me, act, low] + [in_hbm(x) for x in held or ()]
+    outs = [sds((8, *shard), BF16)] * 2 + [sds((2, 8, *shard), BF16)]
+    args = [me, act, low] + list(held or ())
     size = member.shape[0] * member.shape[1]
     return pl.pallas_call(
         functools.partial(weight_blocks_kernel, geom, member, steps, held is not None),
@@ -850,12 +849,12 @@
     chans = member.shape[0] // 9
     pix, width = low.shape[1] * geom[1] * geom[2], low.shape[-1]
     shard = (rows, LANES)
-    outs = [pltpu.HBM((8, *shard), BF16)] * 2 + [pltpu.HBM((2, 8, *shard), BF16)]
+    outs = [sds((8, *shard), BF16)] * 2 + [sds((2, 8, *shard), BF16)]
     out_specs = [ANYWHERE] * 3
     if step == 0:
         outs.append(sds((chans, pix), BF16))
         out_specs.append(whole((chans, pix)))
-    args = [me, act, low] + [in_hbm(x) for x in held or ()]
+    args = [me, act, low] + list(held or ())
     return pl.pallas_call(
         functools.partial(weight_piece_kernel, geom, member, step, held is not None),
         grid=(1,),
@@ -882,9 +881,9 @@
         matrix_ref, out_ref, sums_ref = refs
     for lane in range(0, out_ref.shape[-1], 256):
         lanes = slice(lane, lane + 256)
-        out_ref[:, lanes] = jnp.dot(act_ref[...], matrix_ref[:, lanes], preferred_element_type=F32)
-        pairs = [column_sums(out_ref, f, pixels, lanes) for f in range(frames)]
-        sums_ref[:, lanes] = by_domain([p[0] for p in pairs], [p[1] for p in pairs], domain_ref)
+        out = jnp.dot(act_ref[...], matrix_ref[:, lanes], preferred_element_type=F32)
+        out_ref[:, lanes] = out
+        sums_ref[:, lanes] = value_sums([out[f * pixels : (f + 1) * pixels] for f in range(frames)], domain_ref)
 
 
 def point_layer(geom, domain, act, mat):
@@ -1384,21 +1383,17 @@
 
         def x_done(x):
             (got,) = add_after(x, self.sums[n + 2].far_job())
-            if n == 2:
-                self.late = got
-            else:
-                self.sums[n + 2].far(*got)
+            self.sums[n + 2].far(*got)
             return got[0]
 
         def y_done(x):
-            jobs = [self.sums[n + 1].second_job()]
             if n == 2:
                 self.send(2)
-                jobs.append(self.sums[2].first_job())
-            got = add_after(x, *jobs)
-            self.sums[n + 1].second(*got[0])
-            if n == 2:
-                self.sums[2].first(*got[1])
+                (got,) = add_after(x, self.sums[2].first_job())
+                self.sums[2].first(*got)
+            else:
+                (got,) = add_after(x, self.sums[n + 1].second_job())
+                self.sums[n + 1].second(*got)
 
         return {Z_FAR: [z_done], X: [x_done], Y: [y_done]} if n < 5 else {Y: [y_done]}
 
@@ -1452,32 +1447,32 @@
     def tail(self, blocks, kernels):
         two, three, four = (self.sums[n] for n in (2, 3, 4))
         outs = [kernels[0](blocks)]
-        got = add_after(outs[0], two.second_job(), three.near_job())
+        got = add_after(outs[0], two.second_job(), three.second_job(), four.finish_job())
         two.second(*got[0])
+        three.second(*got[1])
+        (four.out,) = got[2]
+        ((two.z, two.send),) = add_after(got[0][0], two.near_job())
+        two.near()
+        self.send(1, two.send)
+        one = self.sums[1]
+        (got,) = add_after(two.z, one.first_job())
+        one.first(*got)
+        outs.append(kernels[1](got[0]))
+        got = add_after(got[0], two.far_job(), three.near_job())
+        two.far(*got[0])
         three.z, three.send = got[1]
         three.near()
-        self.send(1, got[0][0])
-        one = self.sums[1]
-        got = add_after(got[0][0], one.first_job(), two.near_job(), three.far_job())
-        one.first(*got[0])
-        two.z, two.send = got[1]
-        two.near()
-        three.far(*got[2])
-        outs.append(kernels[1](got[0][0]))
         (got,) = add_after(got[0][0], one.second_job())
         one.second(*got)
-        (got,) = add_after(got[0], two.far_job())
-        two.far(*got)
-        got = add_after(got[0], one.near_job(), three.finish_job())
+        got = add_after(got[0], one.near_job(), two.finish_job(), three.far_job())
         one.z, one.send = got[0]
+        (two.out,) = got[1]
         one.near()
-        (three.out,) = got[1]
-        four.far(*tied(tuple(self.late), one.z))
-        got = add_after(one.z, one.far_job(), two.finish_job())
-        one.far(*got[0])
-        (two.out,) = got[1]
-        ((four.out,),) = add_after(got[0][0], four.finish_job())
-        ((one.out,),) = add_after(four.out, one.finish_job())
+        three.far(*got[2])
+        (got,) = add_after(one.z, one.far_job())
+        one.far(*got)
+        ((three.out,),) = add_after(got[0], three.finish_job())
+        ((one.out,),) = add_after(three.out, one.finish_job())
         for name, m in self.homes.items():
             out = unpack(self.sums[NUMBER[name]].out[m.at : m.at + m.rows], m.blocks)
             self.grads[name] = columns_of_core(out) if m.split else out

time: 559 us -> 531 us (0.950); the launches traced: 555 us -> 522 us
  Pallas kernels: 205 us -> 171 us
  waiting for transfers between devices: 163 us -> 173 us
    pallas_call x5, Pallas kernels: 51.8 us -> 38.9 us  [backward_layer(): pl.pallas_call(functools.partial(backward_kernel, geom, added is not None...]
    ppermute x166, waiting for transfers between devices: 163 us -> 173 us  [swap(): return lax.ppermute(x, AXES, [(i, i ^ 1 << bit) for i in range(n)])]
    pallas_call x12, Pallas kernels: 35.3 us -> 26.1 us  [weight_piece(): pl.pallas_call(functools.partial(weight_piece_kernel, geom, member, step,...]
    unnamed x204 -> x130, local copies, waits for them, and re-layouts: 14.7 us -> 10.2 us
  transfers between devices with their start and end apart: 166 -> 166, of which waited for: 71 -> 86; matrix products, arithmetic and copies ran while one was open for 2% -> 2% of each run, Pallas kernels for 31% -> 27%
where the time goes in v4:
time: 531 us; the launch traced here: 522 us
  waiting for transfers between devices  173 us (33%)
  Pallas kernels  171 us (32%)
  starting transfers between devices  153 us (29%)
  local copies, waits for them, and re-layouts  13.1 us (2%)
  other arithmetic  8.34 us (2%)
    ppermute x166, waiting for transfers between devices, swap(): return lax.ppermute(x, AXES, [(i, i ^ 1 << bit) for i in range(n)])  173 us
    ppermute x166, starting transfers between devices, swap(): return lax.ppermute(x, AXES, [(i, i ^ 1 << bit) for i in range(n)])  153 us
    pallas_call x6, Pallas kernels, forward_layer(): pl.pallas_call(functools.partial(forward_kernel, geom, norm is not None,...  39.4 us
    pallas_call x5, Pallas kernels, backward_layer(): pl.pallas_call(functools.partial(backward_kernel, geom, added is not None...  38.9 us
    pallas_call x12, Pallas kernels, weight_piece(): pl.pallas_call(functools.partial(weight_piece_kernel, geom, member, step,...  26.1 us
    pallas_call x4, Pallas kernels, weight_blocks(): pl.pallas_call(functools.partial(weight_blocks_kernel, geom, member, step...  11.7 us
    pallas_call x20, Pallas kernels, add_all(): pl.pallas_call(functools.partial(add_kernel, [(work, len(i), len(o)) for...  10.9 us
  transfers between devices with their start and end apart: 166, of which 86 were waited for; matrix products, arithmetic and copies ran while one was open for 2% of the time, Pallas kernels for 27%

profile of v4, /device:TPU:0, one launch (start us, length us, event | category | flops | bytes accessed | tf_op | source)
XLA Modules:
  0.0 521.8 jit_solution(15376188806602625288)
XLA Ops:
  4.7 4.1 collective-permute-done
  33.7 6.6 %collective-permute-done.16 = bf16[2,592,128]{2,1,0:T(8,128)(2,1)S(1)} collective-permute-done((bf16[2,592,128]{2,1,0:T(8,128)(2,1)S(1)}, bf16[2,592,128]{2,1,0:T(8,128)(2,1)S(1)}, u32[]{:S(2)}, u32[]{:S(2)}) %collective-permute-start.16) | collective-permute-done | bytes 303136 | tf_op jit(solution)/shard_map/ppermute | solution.py:978
  44.0 4.2 shard_map.237
  76.9 7.6 %shard_map.239 = (f32[1024,512]{1,0:T(8,128)S(1)}, f32[4,512]{1,0:T(4,128)S(1)}, bf16[1024,512]{1,0:T(8,128)(2,1)S(1)}, bf16[4608,512]{1,0:T(8,128)(2,1)}) custom-call(s32[2]{0:T(128)S(1)} %copy-done.17, f32[1024,512]{1,0:T(8,128)S(1)} %get-tuple-element.451.refs_1_.refs_7_.pre_ref, f32[4,512]{1,0:T(4,128)S(1)} %add.204.refs_2_.refs_8_.st_ref, ...), custom_call_target="tpu_custom_call" | custom-call | flops 483183808 | bytes 891289 | tf_op jit(solution)/shard_map/pallas_call | solution.py:246
  93.0 4.4 collective-permute-done.30
  110.4 8.0 %shard_map.240 = (f32[1024,512]{1,0:T(8,128)S(1)}, f32[4,512]{1,0:T(4,128)S(1)}, bf16[1024,512]{1,0:T(8,128)(2,1)S(1)}, bf16[4608,512]{1,0:T(8,128)(2,1)}) custom-call(s32[2]{0:T(128)S(1)} %copy-done.17, f32[1024,512]{1,0:T(8,128)S(1)} %get-tuple-element.471.refs_1_.refs_8_.refs_2_, f32[4,512]{1,0:T(4,128)S(1)} %add.209.refs_2_.refs_9_.refs_3_, ...), custom_call_target="tpu_custom_call" | custom-call | flops 483183808 | bytes 891289 | tf_op jit(solution)/shard_map/pallas_call | solution.py:246
  147.3 7.2 %shard_map.242 = (f32[1024,512]{1,0:T(8,128)S(1)}, f32[4,512]{1,0:T(4,128)S(1)}, bf16[4608,512]{1,0:T(8,128)(2,1)}) custom-call(s32[2]{0:T(128)S(1)} %copy-done.17, bf16[1024,512]{1,0:T(8,128)(2,1)S(1)} %shard_map.241.refs_1_, s32[1]{0:T(128)} %bitcast.1.refs_2_.me_ref.refs_5_.refs_0_, bf16[8,288,128]{2,1,0:T(8,128)(2,1)S(1)} %constant_dynamic-update-slice_fusion.21.refs_3_, ...), custom_call_target="tpu_custom_call" | custom-call | flops 483183808 | bytes 891289 | tf_op jit(solution)/shard_map/pallas_call | solution.py:246
  179.3 7.6 %shard_map.243 = (f32[1024,512]{1,0:T(8,128)S(1)}, f32[4,512]{1,0:T(4,128)S(1)}, bf16[1024,512]{1,0:T(8,128)(2,1)S(1)}, bf16[4608,512]{1,0:T(8,128)(2,1)}) custom-call(s32[2]{0:T(128)S(1)} %copy-done.17, f32[1024,512]{1,0:T(8,128)S(1)} %get-tuple-element.505.refs_1_.refs_8_.refs_2_, f32[4,512]{1,0:T(4,128)S(1)} %add.219.refs_2_.refs_9_.refs_3_, ...), custom_call_target="tpu_custom_call" | custom-call | flops 483183808 | bytes 891289 | tf_op jit(solution)/shard_map/pallas_call | solution.py:246
  196.3 4.2 collective-permute-done.75
  210.8 4.9 shard_map.244
  245.2 4.6 collective-permute-done.94
  258.0 4.7 shard_map.251
  267.2 4.2 shard_map.252
  289.8 8.3 %shard_map.257 = (bf16[3,2,18,32,512]{4,3,2,1,0:T(8,128)(2,1)S(1)}, f32[1024,512]{1,0:T(8,128)S(1)}, f32[4,512]{1,0:T(4,128)S(1)}) custom-call(s32[2]{0:T(128)S(1)} %copy-done.17, f32[1024,512]{1,0:T(8,128)S(1)} %copy-done.14, f32[1024,512]{1,0:T(8,128)S(1)} %get-tuple-element.522.refs_1_.refs_7_.refs_2_, f32[4,512]{1,0:T(4,128)S(1)} %add.224.refs_2_.refs_8_.refs_3_, ...), custom_call_target="tpu_custom_call" | custom-call | flops 483183808 | bytes 1520435 | tf_op jit(solution)/shard_map/pallas_call | solution.py:584
  321.4 10.2 %shard_map.263 = (bf16[3,2,18,32,512]{4,3,2,1,0:T(8,128)(2,1)S(1)}, f32[1024,512]{1,0:T(8,128)S(1)}, f32[4,512]{1,0:T(4,128)S(1)}) custom-call(s32[2]{0:T(128)S(1)} %copy-done.17, f32[1024,512]{1,0:T(8,128)S(1)} %get-tuple-element.583.refs_1_, f32[1024,512]{1,0:T(8,128)S(1)} %get-tuple-element.505.refs_1_.refs_8_.refs_2_, ...), custom_call_target="tpu_custom_call" | custom-call | flops 483183808 | bytes 1520435 | tf_op jit(solution)/shard_map/pallas_call | solution.py:584
  366.4 7.9 %shard_map.274 = (bf16[3,2,18,32,512]{4,3,2,1,0:T(8,128)(2,1)S(1)}, f32[1024,512]{1,0:T(8,128)S(1)}, f32[4,512]{1,0:T(4,128)S(1)}) custom-call(s32[2]{0:T(128)S(1)} %copy-done.17, f32[1024,512]{1,0:T(8,128)S(1)} %copy-done.10, f32[1024,512]{1,0:T(8,128)S(1)} %get-tuple-element.731.top_ref.refs_7_.refs_2_, f32[4,512]{1,0:T(4,128)S(1)} %add.214.top_st.refs_8_.refs_3_, ...), custom_call_target="tpu_custom_call" | custom-call | flops 483183808 | bytes 1520435 | tf_op jit(solution)/shard_map/pallas_call | solution.py:584
  387.4 7.0 %collective-permute-done.128.refs_2_ = bf16[8,384,128]{2,1,0:T(8,128)(2,1)S(1)} collective-permute-done((bf16[8,384,128]{2,1,0:T(8,128)(2,1)S(1)}, bf16[8,384,128]{2,1,0:T(8,128)(2,1)S(1)}, u32[]{:S(2)}, u32[]{:S(2)}) %collective-permute-start.128) | collective-permute-done | bytes 786464 | tf_op jit(solution)/shard_map/ppermute | solution.py:978
  399.9 5.3 %shard_map.281 = f32[2,8,3,16,512]{4,3,2,1,0:T(8,128)} custom-call(s32[2]{0:T(128)S(1)} %copy-done.17, f32[1024,512]{1,0:T(8,128)S(1)} %get-tuple-element.731.top_ref.refs_7_.refs_2_, f32[4,512]{1,0:T(4,128)S(1)} %add.214.top_st.refs_8_.refs_3_, f32[1,512]{1,0:T(1,128)S(1)} %get-tuple-element.940.gain_t.refs_9_.refs_5_, ...), custom_call_target="tpu_custom_call" | custom-call | flops 3145728 | bytes 1468006 | tf_op jit(solution)/shard_map/pallas_call | solution.py:372
  409.9 7.9 %shard_map.282 = (bf16[3,2,18,32,512]{4,3,2,1,0:T(8,128)(2,1)S(1)}, f32[1024,512]{1,0:T(8,128)S(1)}, f32[4,512]{1,0:T(4,128)S(1)}) custom-call(s32[2]{0:T(128)S(1)} %copy-done.17, f32[1024,512]{1,0:T(8,128)S(1)} %get-tuple-element.733.refs_1_, f32[1024,512]{1,0:T(8,128)S(1)} %get-tuple-element.471.refs_1_.refs_8_.refs_2_, ...), custom_call_target="tpu_custom_call" | custom-call | flops 483183808 | bytes 1520435 | tf_op jit(solution)/shard_map/pallas_call | solution.py:584
  441.1 7.5 %collective-permute-done.143.refs_1_ = bf16[2,768,128]{2,1,0:T(8,128)(2,1)S(1)} collective-permute-done((bf16[2,768,128]{2,1,0:T(8,128)(2,1)S(1)}, bf16[2,768,128]{2,1,0:T(8,128)(2,1)S(1)}, u32[]{:S(2)}, u32[]{:S(2)}) %collective-permute-start.143) | collective-permute-done | bytes 393248 | tf_op jit(solution)/shard_map/ppermute | solution.py:978
  462.4 5.6 %shard_map.292 = f32[1024,256]{1,0:T(8,128)} custom-call(bf16[3,2,18,32,512]{4,3,2,1,0:T(8,128)(2,1)S(1)} %shard_map.289.refs_2_.win_ref, bf16[2304,512]{1,0:T(8,128)(2,1)} %get-tuple-element.803.kernel_ref), custom_call_target="tpu_custom_call" | custom-call | flops 241591904 | bytes 655360 | tf_op jit(solution)/shard_map/pallas_call | solution.py:648
  470.8 4.6 collective-permute-done.149.refs_2_
  482.1 5.0 collective-permute-done.155.refs_4_
  510.6 4.3 collective-permute-done.161.refs_1_
  (639 shorter events, 373.1 us)
Async XLA Ops:
  49.7 18.2 %collective-permute-start.22 = (bf16[8,304,128]{2,1,0:T(8,128)(2,1)S(1)}, bf16[8,304,128]{2,1,0:T(8,128)(2,1)S(1)}, u32[]{:S(2)}, u32[]{:S(2)}) collective-permute-start(bf16[8,304,128]{2,1,0:T(8,128)(2,1)S(1)} %constant_dynamic-update-slice_fusion.11.refs_2_.refs_8_), channel_id=1, source_target_pairs={{0,4},{1,5},{2,6},{3,7},{4,0},{5,1},{6,2},{7,3},{8,12},{9,13},{10,... | collective-permute-start | bytes 1867784 | tf_op jit(solution)/shard_map/ppermute | solution.py:978
  51.3 12.9 %collective-permute-start.20 = (bf16[8,288,128]{2,1,0:T(8,128)(2,1)S(1)}, bf16[8,288,128]{2,1,0:T(8,128)(2,1)S(1)}, u32[]{:S(2)}, u32[]{:S(2)}) collective-permute-start(bf16[8,288,128]{2,1,0:T(8,128)(2,1)S(1)} %constant_dynamic-update-slice_fusion.9.refs_0_.refs_6_), channel_id=1, source_target_pairs={{0,2},{1,3},{2,0},{3,1},{4,6},{5,7},{6,4},{7,5},{8,10},{9,11},{10,... | collective-permute-start | bytes 1769480 | tf_op jit(solution)/shard_map/ppermute | solution.py:978
  84.7 15.2 %collective-permute-start.35 = (bf16[8,288,128]{2,1,0:T(8,128)(2,1)S(1)}, bf16[8,288,128]{2,1,0:T(8,128)(2,1)S(1)}, u32[]{:S(2)}, u32[]{:S(2)}) collective-permute-start(bf16[8,288,128]{2,1,0:T(8,128)(2,1)S(1)} %constant_dynamic-update-slice_fusion.15.refs_6_), channel_id=1, source_target_pairs={{0,2},{1,3},{2,0},{3,1},{4,6},{5,7},{6,4},{7,5},{8,10},{9,11},{10,... | collective-permute-start | bytes 1769480 | tf_op jit(solution)/shard_map/ppermute | solution.py:978
  86.2 17.3 %collective-permute-start.37 = (bf16[8,288,128]{2,1,0:T(8,128)(2,1)S(1)}, bf16[8,288,128]{2,1,0:T(8,128)(2,1)S(1)}, u32[]{:S(2)}, u32[]{:S(2)}) collective-permute-start(bf16[8,288,128]{2,1,0:T(8,128)(2,1)S(1)} %constant_dynamic-update-slice_fusion.17.refs_8_), channel_id=1, source_target_pairs={{0,4},{1,5},{2,6},{3,7},{4,0},{5,1},{6,2},{7,3},{8,12},{9,13},{10,... | collective-permute-start | bytes 1769480 | tf_op jit(solution)/shard_map/ppermute | solution.py:978
  119.4 14.0 %collective-permute-start.50 = (bf16[8,288,128]{2,1,0:T(8,128)(2,1)S(1)}, bf16[8,288,128]{2,1,0:T(8,128)(2,1)S(1)}, u32[]{:S(2)}, u32[]{:S(2)}) collective-permute-start(bf16[8,288,128]{2,1,0:T(8,128)(2,1)S(1)} %constant_dynamic-update-slice_fusion.21.refs_3_), channel_id=1, source_target_pairs={{0,2},{1,3},{2,0},{3,1},{4,6},{5,7},{6,4},{7,5},{8,10},{9,11},{10,... | collective-permute-start | bytes 1769480 | tf_op jit(solution)/shard_map/ppermute | solution.py:978
  120.5 16.6 %collective-permute-start.52 = (bf16[8,288,128]{2,1,0:T(8,128)(2,1)S(1)}, bf16[8,288,128]{2,1,0:T(8,128)(2,1)S(1)}, u32[]{:S(2)}, u32[]{:S(2)}) collective-permute-start(bf16[8,288,128]{2,1,0:T(8,128)(2,1)S(1)} %constant_dynamic-update-slice_fusion.23.refs_5_), channel_id=1, source_target_pairs={{0,4},{1,5},{2,6},{3,7},{4,0},{5,1},{6,2},{7,3},{8,12},{9,13},{10,... | collective-permute-start | bytes 1769480 | tf_op jit(solution)/shard_map/ppermute | solution.py:978
  141.0 13.5 %collective-permute-start.63 = (bf16[4,288,128]{2,1,0:T(8,128)(2,1)S(1)}, bf16[4,288,128]{2,1,0:T(8,128)(2,1)S(1)}, u32[]{:S(2)}, u32[]{:S(2)}) collective-permute-start(bf16[4,288,128]{2,1,0:T(8,128)(2,1)S(1)} %get-tuple-element.515), channel_id=1, source_target_pairs={{0,2},{1,3},{2,0},{3,1},{4,6},{5,7},{6,4},{7,5},{8,10},{9,11},{10,... | collective-permute-start | bytes 884744 | tf_op jit(solution)/shard_map/ppermute | solution.py:978
  154.6 14.9 %collective-permute-start.65 = (bf16[8,288,128]{2,1,0:T(8,128)(2,1)S(1)}, bf16[8,288,128]{2,1,0:T(8,128)(2,1)S(1)}, u32[]{:S(2)}, u32[]{:S(2)}) collective-permute-start(bf16[8,288,128]{2,1,0:T(8,128)(2,1)S(1)} %constant_dynamic-update-slice_fusion.27.refs_6_), channel_id=1, source_target_pairs={{0,2},{1,3},{2,0},{3,1},{4,6},{5,7},{6,4},{7,5},{8,10},{9,11},{10,... | collective-permute-start | bytes 1769480 | tf_op jit(solution)/shard_map/ppermute | solution.py:978
  156.0 17.3 %collective-permute-start.67 = (bf16[8,288,128]{2,1,0:T(8,128)(2,1)S(1)}, bf16[8,288,128]{2,1,0:T(8,128)(2,1)S(1)}, u32[]{:S(2)}, u32[]{:S(2)}) collective-permute-start(bf16[8,288,128]{2,1,0:T(8,128)(2,1)S(1)} %constant_dynamic-update-slice_fusion.29.refs_8_), channel_id=1, source_target_pairs={{0,4},{1,5},{2,6},{3,7},{4,0},{5,1},{6,2},{7,3},{8,12},{9,13},{10,... | collective-permute-start | bytes 1769480 | tf_op jit(solution)/shard_map/ppermute | solution.py:978
  187.7 14.7 %collective-permute-start.79 = (bf16[8,288,128]{2,1,0:T(8,128)(2,1)S(1)}, bf16[8,288,128]{2,1,0:T(8,128)(2,1)S(1)}, u32[]{:S(2)}, u32[]{:S(2)}) collective-permute-start(bf16[8,288,128]{2,1,0:T(8,128)(2,1)S(1)} %constant_dynamic-update-slice_fusion.33.refs_6_.refs_3_.refs_0_), channel_id=1, source_target_pairs={{0,2},{1,3},{2,0},{3,1},{4,6},{5,7},{6,4},{7,5},{8,10},{9,11},{10,... | collective-permute-start | bytes 1769480 | tf_op jit(solution)/shard_map/ppermute | solution.py:978
  188.6 17.4 %collective-permute-start.81 = (bf16[8,288,128]{2,1,0:T(8,128)(2,1)S(1)}, bf16[8,288,128]{2,1,0:T(8,128)(2,1)S(1)}, u32[]{:S(2)}, u32[]{:S(2)}) collective-permute-start(bf16[8,288,128]{2,1,0:T(8,128)(2,1)S(1)} %constant_dynamic-update-slice_fusion.35.refs_8_.refs_5_.refs_2_), channel_id=1, source_target_pairs={{0,4},{1,5},{2,6},{3,7},{4,0},{5,1},{6,2},{7,3},{8,12},{9,13},{10,... | collective-permute-start | bytes 1769480 | tf_op jit(solution)/shard_map/ppermute | solution.py:978
  332.8 15.2 %collective-permute-start.116 = (bf16[8,288,128]{2,1,0:T(8,128)(2,1)S(1)}, bf16[8,288,128]{2,1,0:T(8,128)(2,1)S(1)}, u32[]{:S(2)}, u32[]{:S(2)}) collective-permute-start(bf16[8,288,128]{2,1,0:T(8,128)(2,1)S(1)} %get-tuple-element.649), channel_id=1, source_target_pairs={{0,2},{1,3},{2,0},{3,1},{4,6},{5,7},{6,4},{7,5},{8,10},{9,11},{10,... | collective-permute-start | bytes 1769480 | tf_op jit(solution)/shard_map/ppermute | solution.py:978
  333.9 14.9 %collective-permute-start.117 = (bf16[2,4,288,128]{3,2,1,0:T(8,128)(2,1)S(1)}, bf16[2,4,288,128]{3,2,1,0:T(8,128)(2,1)S(1)}, u32[]{:S(2)}, u32[]{:S(2)}) collective-permute-start(bf16[2,4,288,128]{3,2,1,0:T(8,128)(2,1)S(1)} %get-tuple-element.651), channel_id=1, source_target_pairs={{0,4},{1,5},{2,6},{3,7},{4,0},{5,1},{6,2},{7,3},{8,12},{9,13},{10,... | collective-permute-start | bytes 1769480 | tf_op jit(solution)/shard_map/ppermute | solution.py:978
  375.2 19.2 %collective-permute-start.128 = (bf16[8,384,128]{2,1,0:T(8,128)(2,1)S(1)}, bf16[8,384,128]{2,1,0:T(8,128)(2,1)S(1)}, u32[]{:S(2)}, u32[]{:S(2)}) collective-permute-start(bf16[8,384,128]{2,1,0:T(8,128)(2,1)S(1)} %get-tuple-element.715), channel_id=1, source_target_pairs={{0,2},{1,3},{2,0},{3,1},{4,6},{5,7},{6,4},{7,5},{8,10},{9,11},{10,... | collective-permute-start | bytes 2359304 | tf_op jit(solution)/shard_map/ppermute | solution.py:978
  376.2 18.8 %collective-permute-start.129 = (bf16[2,4,384,128]{3,2,1,0:T(8,128)(2,1)S(1)}, bf16[2,4,384,128]{3,2,1,0:T(8,128)(2,1)S(1)}, u32[]{:S(2)}, u32[]{:S(2)}) collective-permute-start(bf16[2,4,384,128]{3,2,1,0:T(8,128)(2,1)S(1)} %get-tuple-element.717), channel_id=1, source_target_pairs={{0,4},{1,5},{2,6},{3,7},{4,0},{5,1},{6,2},{7,3},{8,12},{9,13},{10,... | collective-permute-start | bytes 2359304 | tf_op jit(solution)/shard_map/ppermute | solution.py:978
  405.2 12.7 %collective-permute-start.133 = (bf16[2,8,576,128]{3,2,1,0:T(8,128)(2,1)S(1)}, bf16[2,8,576,128]{3,2,1,0:T(8,128)(2,1)S(1)}, u32[]{:S(2)}, u32[]{:S(2)}) collective-permute-start(bf16[2,8,576,128]{3,2,1,0:T(8,128)(2,1)S(1)} %get-tuple-element.739), channel_id=1, source_target_pairs={{0,1},{1,0},{2,3},{3,2},{4,5},{5,4},{6,7},{7,6},{8,9},{9,8},{10,11... | collective-permute-start | bytes 7077896 | tf_op jit(solution)/shard_map/ppermute | solution.py:978
  419.3 14.8 %collective-permute-start.140 = (bf16[8,288,128]{2,1,0:T(8,128)(2,1)S(1)}, bf16[8,288,128]{2,1,0:T(8,128)(2,1)S(1)}, u32[]{:S(2)}, u32[]{:S(2)}) collective-permute-start(bf16[8,288,128]{2,1,0:T(8,128)(2,1)S(1)} %get-tuple-element.774), channel_id=1, source_target_pairs={{0,2},{1,3},{2,0},{3,1},{4,6},{5,7},{6,4},{7,5},{8,10},{9,11},{10,... | collective-permute-start | bytes 1769480 | tf_op jit(solution)/shard_map/ppermute | solution.py:978
  420.4 14.3 %collective-permute-start.141 = (bf16[2,4,288,128]{3,2,1,0:T(8,128)(2,1)S(1)}, bf16[2,4,288,128]{3,2,1,0:T(8,128)(2,1)S(1)}, u32[]{:S(2)}, u32[]{:S(2)}) collective-permute-start(bf16[2,4,288,128]{3,2,1,0:T(8,128)(2,1)S(1)} %get-tuple-element.776), channel_id=1, source_target_pairs={{0,4},{1,5},{2,6},{3,7},{4,0},{5,1},{6,2},{7,3},{8,12},{9,13},{10,... | collective-permute-start | bytes 1769480 | tf_op jit(solution)/shard_map/ppermute | solution.py:978
  437.0 15.4 %collective-permute-start.145 = (bf16[2,8,576,128]{3,2,1,0:T(8,128)(2,1)S(1)}, bf16[2,8,576,128]{3,2,1,0:T(8,128)(2,1)S(1)}, u32[]{:S(2)}, u32[]{:S(2)}) collective-permute-start(bf16[2,8,576,128]{3,2,1,0:T(8,128)(2,1)S(1)} %get-tuple-element.794), channel_id=1, source_target_pairs={{0,1},{1,0},{2,3},{3,2},{4,5},{5,4},{6,7},{7,6},{8,9},{9,8},{10,11... | collective-permute-start | bytes 7077896 | tf_op jit(solution)/shard_map/ppermute | solution.py:978
  453.0 15.1 %collective-permute-start.146 = (bf16[8,288,128]{2,1,0:T(8,128)(2,1)S(1)}, bf16[8,288,128]{2,1,0:T(8,128)(2,1)S(1)}, u32[]{:S(2)}, u32[]{:S(2)}) collective-permute-start(bf16[8,288,128]{2,1,0:T(8,128)(2,1)S(1)} %get-tuple-element.800), channel_id=1, source_target_pairs={{0,2},{1,3},{2,0},{3,1},{4,6},{5,7},{6,4},{7,5},{8,10},{9,11},{10,... | collective-permute-start | bytes 1769480 | tf_op jit(solution)/shard_map/ppermute | solution.py:978
  454.1 14.0 %collective-permute-start.147 = (bf16[2,4,288,128]{3,2,1,0:T(8,128)(2,1)S(1)}, bf16[2,4,288,128]{3,2,1,0:T(8,128)(2,1)S(1)}, u32[]{:S(2)}, u32[]{:S(2)}) collective-permute-start(bf16[2,4,288,128]{3,2,1,0:T(8,128)(2,1)S(1)} %get-tuple-element.801), channel_id=1, source_target_pairs={{0,4},{1,5},{2,6},{3,7},{4,0},{5,1},{6,2},{7,3},{8,12},{9,13},{10,... | collective-permute-start | bytes 1769480 | tf_op jit(solution)/shard_map/ppermute | solution.py:978
  455.0 13.1 %collective-permute-start.148 = (bf16[768,128]{1,0:T(8,128)(2,1)S(1)}, bf16[768,128]{1,0:T(8,128)(2,1)S(1)}, u32[]{:S(2)}, u32[]{:S(2)}) collective-permute-start(bf16[768,128]{1,0:T(8,128)(2,1)S(1)} %get-tuple-element.813), channel_id=1, source_target_pairs={{0,16},{1,17},{2,18},{3,19},{4,20},{5,21},{6,22},{7,23},{8,24},{9,... | collective-permute-start | bytes 589832 | tf_op jit(solution)/shard_map/ppermute | solution.py:978
  480.0 13.5 %collective-permute-start.152 = (bf16[8,144,128]{2,1,0:T(8,128)(2,1)S(1)}, bf16[8,144,128]{2,1,0:T(8,128)(2,1)S(1)}, u32[]{:S(2)}, u32[]{:S(2)}) collective-permute-start(bf16[8,144,128]{2,1,0:T(8,128)(2,1)S(1)} %get-tuple-element.833), channel_id=1, source_target_pairs={{0,2},{1,3},{2,0},{3,1},{4,6},{5,7},{6,4},{7,5},{8,10},{9,11},{10,... | collective-permute-start | bytes 884744 | tf_op jit(solution)/shard_map/ppermute | solution.py:978
  489.3 13.4 %collective-permute-start.159 = (bf16[576,128]{1,0:T(8,128)(2,1)}, bf16[576,128]{1,0:T(8,128)(2,1)}, u32[]{:S(2)}, u32[]{:S(2)}) collective-permute-start(bf16[576,128]{1,0:T(8,128)(2,1)} %get-tuple-element.858), channel_id=1, source_target_pairs={{0,16},{1,17},{2,18},{3,19},{4,20},{5,21},{6,22},{7,23},{8,24},{9,... | collective-permute-start | bytes 442376 | tf_op jit(solution)/shard_map/ppermute | solution.py:978
  (192 other events, 1386.7 us)

commit v5 on v4

--- a/solution.py
+++ b/solution.py
@@ -173,42 +173,53 @@
     act_ref = refs.pop(0) if normed else None
     if pieces:
         matrix_ref = refs.pop(0)
-    win_ref, held_ref, sem = refs
+    *wins, held_ref, sem = refs
 
     if pieces:
         fetch(*pieces, me_ref, sources, held_ref, sem.at[0])
     else:
         pltpu.make_async_copy(kernel_ref, held_ref, sem.at[0]).start()
-    clear_edges(win_ref, rows)
-    for f in range(frames):
+
+    def prepare(f, unrolled):
+        clear_edges(wins[f], rows)
         if normed:
             average, inverse = frame_tables(stats_ref[...], domain_ref[f], counts)
             scale = inverse * gain_ref[...]
             shift = bias_ref[...] - average * scale
 
         def one_row(r, _):
-            at = pl.multiple_of(f * pixels + r * cols, cols)
+            at = f * pixels + r * cols
+            at = at if unrolled else pl.multiple_of(at, cols)
             value = source_ref[pl.ds(at, cols), :].astype(F32)
             if normed:
                 act = value * scale + shift
                 value = act * sigmoid(act)
                 act_ref[pl.ds(at, cols), :] = value.astype(BF16)
-            put_windows(win_ref, f, r, value, cols)
+            put_windows(wins[f], 0, r, value, cols)
             return 0
 
-        lax.fori_loop(0, rows, one_row, 0, unroll=2)
+        if unrolled:
+            for r in range(rows):
+                one_row(r, 0)
+        else:
+            lax.fori_loop(0, rows, one_row, 0, unroll=2)
+
+    def product(f):
+        source = jnp.concatenate([window(wins[f], b, a, rows) for a in range(3) for b in range(3)], 1)
+        out = jnp.dot(source, held_ref[...], preferred_element_type=F32)
+        out_ref[f * pixels : (f + 1) * pixels, :] = out
+        return out
+
+    prepare(0, False)
     arrived(held_ref, sem.at[0])
     if pieces:
         pltpu.make_async_copy(held_ref, matrix_ref, sem.at[1]).start()
-    source = jnp.concatenate([window(win_ref, b, a, rows) for a in range(3) for b in range(3)], 1)
-    out = jnp.dot(source, held_ref[...], preferred_element_type=F32)
-    out_ref[...] = out
-    parts = [out[f * pixels : (f + 1) * pixels] for f in range(frames)]
-    sums_ref[...] = by_domain(
-        [jnp.sum(fold(p), 0, keepdims=True) for p in parts],
-        [jnp.sum(fold(p * p), 0, keepdims=True) for p in parts],
-        domain_ref,
-    )
+    parts = []
+    for f in range(frames):
+        if f + 1 < frames:
+            prepare(f + 1, True)
+        parts.append(product(f))
+    sums_ref[...] = value_sums(parts, domain_ref)
     if pieces:
         pltpu.make_async_copy(held_ref, matrix_ref, sem.at[1]).wait()
 
@@ -237,7 +248,7 @@
     if norm is not None:
         outs.append(sds((pix, chans), BF16))
         out_specs.append(whole((pix, chans)))
-    scratch = [pltpu.VMEM((3, frames, rows + 2, cols, chans), BF16)]
+    scratch = [pltpu.VMEM((3, 1, rows + 2, cols, chans), BF16)] * frames
     scratch += [pltpu.VMEM(kernel.shape, BF16), pltpu.SemaphoreType.DMA((2,))]
     if pieces:
         outs.append(pltpu.HBM(kernel.shape, BF16))
@@ -270,7 +281,7 @@
     half = x.shape[0]
     scr_ref[pl.ds(0, half, stride=2), :] = x
     scr_ref[pl.ds(1, half, stride=2), :] = x
-    return scr_ref[...]
+    return scr_ref[pl.ds(0, 2 * half), :]
 
 
 def top_rows(top_ref, at, cols, lanes, scale, shift):
@@ -355,7 +366,7 @@
                     for h in (0, 1):
                         term = sigmoid(masks[k][0][pl.ds(at[h], cols), lanes] * scale + shift) * held[h]
                         total = term if total is None else total + term
-                    scr_ref[k] = total
+                    scr_ref[k, pl.ds(0, cols), :] = total
                     even = scr_ref[k, pl.ds(0, cols // 2, stride=2), :]
                     odd = scr_ref[k, pl.ds(1, cols // 2, stride=2), :]
                     task_ref[f, i, k, :, lanes] = even + odd
@@ -374,7 +385,7 @@
         in_specs=[SCALARS] + [whole(x.shape) for x in args[1:]],
         out_specs=whole(task_shape),
         out_shape=sds(task_shape, F32),
-        scratch_shapes=[pltpu.VMEM((TASKS, cols, LANES), F32)],
+        scratch_shapes=[pltpu.VMEM((TASKS, cols + 8, LANES), F32)],
         compiler_params=params(),
         cost_estimate=cost(pix * chans * 60, pix * chans * 28),
     )(*args)
@@ -428,7 +439,7 @@
         in_specs=[SCALARS] + [whole(x.shape) for x in args[1:]],
         out_specs=[whole(o.shape) for o in outs],
         out_shape=outs,
-        scratch_shapes=[pltpu.VMEM((cols, LANES), F32)],
+        scratch_shapes=[pltpu.VMEM((cols + 8, LANES), F32)],
         compiler_params=params(),
         cost_estimate=cost(pix * chans * 40, pix * chans * 20),
     )(*args)
@@ -1298,8 +1309,9 @@
         splits = ("six", "gating")
         g1 = Gather(links, weights["one"])
         g1.far()
+        g1.near()
         packed = {n: pack(rows_of_chip(tied(w, g1.got)) if n in splits else w) for n, w in weights.items()}
-        gains, biases = tied((gains, biases), g1.got)
+        gains, biases = tied((gains, biases), g1.z)
         affine = in_three(jnp.stack([gains, biases])).reshape(6, -1)
         affine = jnp.pad(affine, ((0, 2), (0, 2 * LANES - affine.shape[1])))
         affine = jnp.concatenate([affine[:, :LANES], affine[:, LANES:]])
@@ -1317,8 +1329,7 @@
             self.g.append(group)
             self.group.update((n, group) for n in names)
         g2 = self.g[1]
-        g1.near()
-        g2.far(g1.got)
+        g2.far()
         g1.first()
         g2.near(g1.got)
         g1.second()
@@ -1389,12 +1400,15 @@
         def y_done(x):
             if n == 2:
                 self.send(2)
-                (got,) = add_after(x, self.sums[2].first_job())
-                self.sums[2].first(*got)
+                got = add_after(x, self.sums[2].first_job(), self.sums[4].far_job())
+                self.sums[2].first(*got[0])
+                self.sums[4].far(*got[1])
             else:
                 (got,) = add_after(x, self.sums[n + 1].second_job())
                 self.sums[n + 1].second(*got)
 
+        if n == 2:
+            return {Z_FAR: [z_done], Y: [y_done]}
         return {Z_FAR: [z_done], X: [x_done], Y: [y_done]} if n < 5 else {Y: [y_done]}
 
     def add(self, name, act, low):

time: 531 us -> 519 us (0.977); the launches traced: 522 us -> 516 us
    pallas_call x20 -> x19, Pallas kernels: 10.9 us -> 10.9 us  [add_all(): pl.pallas_call(functools.partial(add_kernel, [(work, len(i), len(o)) for...]
  transfers between devices with their start and end apart: 166 -> 166, of which waited for: 86 -> 87; matrix products, arithmetic and copies ran while one was open for 2% -> 3% of each run, Pallas kernels for 27% -> 27%
where the time goes in v5:
time: 519 us; the launch traced here: 516 us
  waiting for transfers between devices  170 us (33%)
  Pallas kernels  170 us (33%)
  starting transfers between devices  153 us (29%)
  local copies, waits for them, and re-layouts  13.1 us (3%)
  other arithmetic  7.59 us (1%)
    ppermute x166, waiting for transfers between devices, swap(): return lax.ppermute(x, AXES, [(i, i ^ 1 << bit) for i in range(n)])  170 us
    ppermute x166, starting transfers between devices, swap(): return lax.ppermute(x, AXES, [(i, i ^ 1 << bit) for i in range(n)])  153 us
    pallas_call x5, Pallas kernels, backward_layer(): pl.pallas_call(functools.partial(backward_kernel, geom, added is not None...  39.1 us
    pallas_call x6, Pallas kernels, forward_layer(): pl.pallas_call(functools.partial(forward_kernel, geom, norm is not None,...  37.9 us
    pallas_call x12, Pallas kernels, weight_piece(): pl.pallas_call(functools.partial(weight_piece_kernel, geom, member, step,...  26.2 us
    pallas_call x4, Pallas kernels, weight_blocks(): pl.pallas_call(functools.partial(weight_blocks_kernel, geom, member, step...  11.5 us
    pallas_call x19, Pallas kernels, add_all(): pl.pallas_call(functools.partial(add_kernel, [(work, len(i), len(o)) for...  10.9 us
  transfers between devices with their start and end apart: 166, of which 87 were waited for; matrix products, arithmetic and copies ran while one was open for 3% of the time, Pallas kernels for 27%

profile of v5, /device:TPU:0, one launch (start us, length us, event | category | flops | bytes accessed | tf_op | source)
XLA Modules:
  0.0 516.0 jit_solution(2746669415158660432)
XLA Ops:
  0.7 4.1 collective-permute-start
  4.8 4.1 collective-permute-done
  29.5 4.4 collective-permute-done.5.refs_4_
  41.3 4.2 shard_map.237
  74.3 7.3 %shard_map.239 = (f32[1024,512]{1,0:T(8,128)S(1)}, f32[4,512]{1,0:T(4,128)S(1)}, bf16[1024,512]{1,0:T(8,128)(2,1)S(1)}, bf16[4608,512]{1,0:T(8,128)(2,1)}) custom-call(s32[2]{0:T(128)S(1)} %copy-done.17, f32[1024,512]{1,0:T(8,128)S(1)} %get-tuple-element.449.refs_1_.refs_7_.pre_ref, f32[4,512]{1,0:T(4,128)S(1)} %add.204.refs_2_.refs_8_.st_ref, ...), custom_call_target="tpu_custom_call" | custom-call | flops 483183808 | bytes 891289 | tf_op jit(solution)/shard_map/pallas_call | solution.py:257
  106.9 7.5 %shard_map.240 = (f32[1024,512]{1,0:T(8,128)S(1)}, f32[4,512]{1,0:T(4,128)S(1)}, bf16[1024,512]{1,0:T(8,128)(2,1)S(1)}, bf16[4608,512]{1,0:T(8,128)(2,1)}) custom-call(s32[2]{0:T(128)S(1)} %copy-done.17, f32[1024,512]{1,0:T(8,128)S(1)} %get-tuple-element.468.refs_1_.refs_8_.refs_2_, f32[4,512]{1,0:T(4,128)S(1)} %add.209.refs_2_.refs_9_.refs_3_, ...), custom_call_target="tpu_custom_call" | custom-call | flops 483183808 | bytes 891289 | tf_op jit(solution)/shard_map/pallas_call | solution.py:257
  144.1 7.3 %shard_map.242 = (f32[1024,512]{1,0:T(8,128)S(1)}, f32[4,512]{1,0:T(4,128)S(1)}, bf16[4608,512]{1,0:T(8,128)(2,1)}) custom-call(s32[2]{0:T(128)S(1)} %copy-done.17, bf16[1024,512]{1,0:T(8,128)(2,1)S(1)} %shard_map.241.refs_1_, s32[1]{0:T(128)} %bitcast.3.refs_2_.me_ref.refs_5_.refs_0_, bf16[8,288,128]{2,1,0:T(8,128)(2,1)S(1)} %constant_dynamic-update-slice_fusion.21.refs_3_, ...), custom_call_target="tpu_custom_call" | custom-call | flops 483183808 | bytes 891289 | tf_op jit(solution)/shard_map/pallas_call | solution.py:257
  176.4 7.3 %shard_map.243 = (f32[1024,512]{1,0:T(8,128)S(1)}, f32[4,512]{1,0:T(4,128)S(1)}, bf16[1024,512]{1,0:T(8,128)(2,1)S(1)}, bf16[4608,512]{1,0:T(8,128)(2,1)}) custom-call(s32[2]{0:T(128)S(1)} %copy-done.17, f32[1024,512]{1,0:T(8,128)S(1)} %get-tuple-element.502.refs_1_.refs_8_.refs_2_, f32[4,512]{1,0:T(4,128)S(1)} %add.219.refs_2_.refs_9_.refs_3_, ...), custom_call_target="tpu_custom_call" | custom-call | flops 483183808 | bytes 891289 | tf_op jit(solution)/shard_map/pallas_call | solution.py:257
  193.4 4.2 collective-permute-done.75
  208.0 4.4 shard_map.244
  242.0 4.6 collective-permute-done.94
  254.8 4.9 shard_map.251
  264.2 4.0 shard_map.252
  286.5 8.3 %shard_map.257 = (bf16[3,2,18,32,512]{4,3,2,1,0:T(8,128)(2,1)S(1)}, f32[1024,512]{1,0:T(8,128)S(1)}, f32[4,512]{1,0:T(4,128)S(1)}) custom-call(s32[2]{0:T(128)S(1)} %copy-done.17, f32[1024,512]{1,0:T(8,128)S(1)} %copy-done.14, f32[1024,512]{1,0:T(8,128)S(1)} %get-tuple-element.519.refs_1_.refs_7_.refs_2_, f32[4,512]{1,0:T(4,128)S(1)} %add.224.refs_2_.refs_8_.refs_3_, ...), custom_call_target="tpu_custom_call" | custom-call | flops 483183808 | bytes 1520435 | tf_op jit(solution)/shard_map/pallas_call | solution.py:595
  318.0 10.2 %shard_map.263 = (bf16[3,2,18,32,512]{4,3,2,1,0:T(8,128)(2,1)S(1)}, f32[1024,512]{1,0:T(8,128)S(1)}, f32[4,512]{1,0:T(4,128)S(1)}) custom-call(s32[2]{0:T(128)S(1)} %copy-done.17, f32[1024,512]{1,0:T(8,128)S(1)} %get-tuple-element.580.refs_1_, f32[1024,512]{1,0:T(8,128)S(1)} %get-tuple-element.502.refs_1_.refs_8_.refs_2_, ...), custom_call_target="tpu_custom_call" | custom-call | flops 483183808 | bytes 1520435 | tf_op jit(solution)/shard_map/pallas_call | solution.py:595
  363.0 7.9 %shard_map.274 = (bf16[3,2,18,32,512]{4,3,2,1,0:T(8,128)(2,1)S(1)}, f32[1024,512]{1,0:T(8,128)S(1)}, f32[4,512]{1,0:T(4,128)S(1)}) custom-call(s32[2]{0:T(128)S(1)} %copy-done.17, f32[1024,512]{1,0:T(8,128)S(1)} %copy-done.10, f32[1024,512]{1,0:T(8,128)S(1)} %get-tuple-element.728.top_ref.refs_7_.refs_2_, f32[4,512]{1,0:T(4,128)S(1)} %add.214.top_st.refs_8_.refs_3_, ...), custom_call_target="tpu_custom_call" | custom-call | flops 483183808 | bytes 1520435 | tf_op jit(solution)/shard_map/pallas_call | solution.py:595
  384.0 7.0 %collective-permute-done.128.refs_2_ = bf16[8,384,128]{2,1,0:T(8,128)(2,1)S(1)} collective-permute-done((bf16[8,384,128]{2,1,0:T(8,128)(2,1)S(1)}, bf16[8,384,128]{2,1,0:T(8,128)(2,1)S(1)}, u32[]{:S(2)}, u32[]{:S(2)}) %collective-permute-start.128) | collective-permute-done | bytes 786464 | tf_op jit(solution)/shard_map/ppermute | solution.py:989
  396.5 5.3 %shard_map.281 = f32[2,8,3,16,512]{4,3,2,1,0:T(8,128)} custom-call(s32[2]{0:T(128)S(1)} %copy-done.17, f32[1024,512]{1,0:T(8,128)S(1)} %get-tuple-element.728.top_ref.refs_7_.refs_2_, f32[4,512]{1,0:T(4,128)S(1)} %add.214.top_st.refs_8_.refs_3_, f32[1,512]{1,0:T(1,128)S(1)} %get-tuple-element.936.gain_t.refs_9_.refs_5_, ...), custom_call_target="tpu_custom_call" | custom-call | flops 3145728 | bytes 1468006 | tf_op jit(solution)/shard_map/pallas_call | solution.py:383
  406.3 7.9 %shard_map.282 = (bf16[3,2,18,32,512]{4,3,2,1,0:T(8,128)(2,1)S(1)}, f32[1024,512]{1,0:T(8,128)S(1)}, f32[4,512]{1,0:T(4,128)S(1)}) custom-call(s32[2]{0:T(128)S(1)} %copy-done.17, f32[1024,512]{1,0:T(8,128)S(1)} %get-tuple-element.730.refs_1_, f32[1024,512]{1,0:T(8,128)S(1)} %get-tuple-element.468.refs_1_.refs_8_.refs_2_, ...), custom_call_target="tpu_custom_call" | custom-call | flops 483183808 | bytes 1520435 | tf_op jit(solution)/shard_map/pallas_call | solution.py:595
  441.4 3.9 collective-permute-done.145.refs_4_
  455.2 5.6 %shard_map.291 = f32[1024,256]{1,0:T(8,128)} custom-call(bf16[3,2,18,32,512]{4,3,2,1,0:T(8,128)(2,1)S(1)} %shard_map.288.refs_2_.win_ref, bf16[2304,512]{1,0:T(8,128)(2,1)} %get-tuple-element.798.kernel_ref), custom_call_target="tpu_custom_call" | custom-call | flops 241591904 | bytes 655360 | tf_op jit(solution)/shard_map/pallas_call | solution.py:659
  464.2 5.4 %collective-permute-done.149.refs_2_ = bf16[4,288,128]{2,1,0:T(8,128)(2,1)S(1)} collective-permute-done((bf16[4,288,128]{2,1,0:T(8,128)(2,1)S(1)}, bf16[4,288,128]{2,1,0:T(8,128)(2,1)S(1)}, u32[]{:S(2)}, u32[]{:S(2)}) %collective-permute-start.149) | collective-permute-done | bytes 294944 | tf_op jit(solution)/shard_map/ppermute | solution.py:989
  476.2 4.8 collective-permute-done.155.refs_4_
  504.9 4.3 collective-permute-done.161.refs_1_
  (640 shorter events, 374.4 us)
Async XLA Ops:
  47.7 16.1 %collective-permute-start.22 = (bf16[8,304,128]{2,1,0:T(8,128)(2,1)S(1)}, bf16[8,304,128]{2,1,0:T(8,128)(2,1)S(1)}, u32[]{:S(2)}, u32[]{:S(2)}) collective-permute-start(bf16[8,304,128]{2,1,0:T(8,128)(2,1)S(1)} %constant_dynamic-update-slice_fusion.11.refs_2_.refs_8_), channel_id=1, source_target_pairs={{0,4},{1,5},{2,6},{3,7},{4,0},{5,1},{6,2},{7,3},{8,12},{9,13},{10,... | collective-permute-start | bytes 1867784 | tf_op jit(solution)/shard_map/ppermute | solution.py:989
  68.2 13.3 %collective-permute-start.33 = (bf16[4,288,128]{2,1,0:T(8,128)(2,1)S(1)}, bf16[4,288,128]{2,1,0:T(8,128)(2,1)S(1)}, u32[]{:S(2)}, u32[]{:S(2)}) collective-permute-start(bf16[4,288,128]{2,1,0:T(8,128)(2,1)S(1)} %get-tuple-element.478), channel_id=1, source_target_pairs={{0,2},{1,3},{2,0},{3,1},{4,6},{5,7},{6,4},{7,5},{8,10},{9,11},{10,... | collective-permute-start | bytes 884744 | tf_op jit(solution)/shard_map/ppermute | solution.py:989
  81.7 15.2 %collective-permute-start.35 = (bf16[8,288,128]{2,1,0:T(8,128)(2,1)S(1)}, bf16[8,288,128]{2,1,0:T(8,128)(2,1)S(1)}, u32[]{:S(2)}, u32[]{:S(2)}) collective-permute-start(bf16[8,288,128]{2,1,0:T(8,128)(2,1)S(1)} %constant_dynamic-update-slice_fusion.15.refs_6_), channel_id=1, source_target_pairs={{0,2},{1,3},{2,0},{3,1},{4,6},{5,7},{6,4},{7,5},{8,10},{9,11},{10,... | collective-permute-start | bytes 1769480 | tf_op jit(solution)/shard_map/ppermute | solution.py:989
  82.4 18.2 %collective-permute-start.37 = (bf16[8,288,128]{2,1,0:T(8,128)(2,1)S(1)}, bf16[8,288,128]{2,1,0:T(8,128)(2,1)S(1)}, u32[]{:S(2)}, u32[]{:S(2)}) collective-permute-start(bf16[8,288,128]{2,1,0:T(8,128)(2,1)S(1)} %constant_dynamic-update-slice_fusion.17.refs_8_), channel_id=1, source_target_pairs={{0,4},{1,5},{2,6},{3,7},{4,0},{5,1},{6,2},{7,3},{8,12},{9,13},{10,... | collective-permute-start | bytes 1769480 | tf_op jit(solution)/shard_map/ppermute | solution.py:989
  116.8 13.7 %collective-permute-start.50 = (bf16[8,288,128]{2,1,0:T(8,128)(2,1)S(1)}, bf16[8,288,128]{2,1,0:T(8,128)(2,1)S(1)}, u32[]{:S(2)}, u32[]{:S(2)}) collective-permute-start(bf16[8,288,128]{2,1,0:T(8,128)(2,1)S(1)} %constant_dynamic-update-slice_fusion.21.refs_3_), channel_id=1, source_target_pairs={{0,2},{1,3},{2,0},{3,1},{4,6},{5,7},{6,4},{7,5},{8,10},{9,11},{10,... | collective-permute-start | bytes 1769480 | tf_op jit(solution)/shard_map/ppermute | solution.py:989
  118.3 15.8 %collective-permute-start.52 = (bf16[8,288,128]{2,1,0:T(8,128)(2,1)S(1)}, bf16[8,288,128]{2,1,0:T(8,128)(2,1)S(1)}, u32[]{:S(2)}, u32[]{:S(2)}) collective-permute-start(bf16[8,288,128]{2,1,0:T(8,128)(2,1)S(1)} %constant_dynamic-update-slice_fusion.23.refs_5_), channel_id=1, source_target_pairs={{0,4},{1,5},{2,6},{3,7},{4,0},{5,1},{6,2},{7,3},{8,12},{9,13},{10,... | collective-permute-start | bytes 1769480 | tf_op jit(solution)/shard_map/ppermute | solution.py:989
  138.0 13.4 %collective-permute-start.63 = (bf16[4,288,128]{2,1,0:T(8,128)(2,1)S(1)}, bf16[4,288,128]{2,1,0:T(8,128)(2,1)S(1)}, u32[]{:S(2)}, u32[]{:S(2)}) collective-permute-start(bf16[4,288,128]{2,1,0:T(8,128)(2,1)S(1)} %get-tuple-element.512), channel_id=1, source_target_pairs={{0,2},{1,3},{2,0},{3,1},{4,6},{5,7},{6,4},{7,5},{8,10},{9,11},{10,... | collective-permute-start | bytes 884744 | tf_op jit(solution)/shard_map/ppermute | solution.py:989
  151.6 15.0 %collective-permute-start.65 = (bf16[8,288,128]{2,1,0:T(8,128)(2,1)S(1)}, bf16[8,288,128]{2,1,0:T(8,128)(2,1)S(1)}, u32[]{:S(2)}, u32[]{:S(2)}) collective-permute-start(bf16[8,288,128]{2,1,0:T(8,128)(2,1)S(1)} %constant_dynamic-update-slice_fusion.27.refs_6_), channel_id=1, source_target_pairs={{0,2},{1,3},{2,0},{3,1},{4,6},{5,7},{6,4},{7,5},{8,10},{9,11},{10,... | collective-permute-start | bytes 1769480 | tf_op jit(solution)/shard_map/ppermute | solution.py:989
  153.1 17.2 %collective-permute-start.67 = (bf16[8,288,128]{2,1,0:T(8,128)(2,1)S(1)}, bf16[8,288,128]{2,1,0:T(8,128)(2,1)S(1)}, u32[]{:S(2)}, u32[]{:S(2)}) collective-permute-start(bf16[8,288,128]{2,1,0:T(8,128)(2,1)S(1)} %constant_dynamic-update-slice_fusion.29.refs_8_), channel_id=1, source_target_pairs={{0,4},{1,5},{2,6},{3,7},{4,0},{5,1},{6,2},{7,3},{8,12},{9,13},{10,... | collective-permute-start | bytes 1769480 | tf_op jit(solution)/shard_map/ppermute | solution.py:989
  184.9 14.7 %collective-permute-start.79 = (bf16[8,288,128]{2,1,0:T(8,128)(2,1)S(1)}, bf16[8,288,128]{2,1,0:T(8,128)(2,1)S(1)}, u32[]{:S(2)}, u32[]{:S(2)}) collective-permute-start(bf16[8,288,128]{2,1,0:T(8,128)(2,1)S(1)} %constant_dynamic-update-slice_fusion.33.refs_6_.refs_3_.refs_0_), channel_id=1, source_target_pairs={{0,2},{1,3},{2,0},{3,1},{4,6},{5,7},{6,4},{7,5},{8,10},{9,11},{10,... | collective-permute-start | bytes 1769480 | tf_op jit(solution)/shard_map/ppermute | solution.py:989
  185.7 17.6 %collective-permute-start.81 = (bf16[8,288,128]{2,1,0:T(8,128)(2,1)S(1)}, bf16[8,288,128]{2,1,0:T(8,128)(2,1)S(1)}, u32[]{:S(2)}, u32[]{:S(2)}) collective-permute-start(bf16[8,288,128]{2,1,0:T(8,128)(2,1)S(1)} %constant_dynamic-update-slice_fusion.35.refs_8_.refs_5_.refs_2_), channel_id=1, source_target_pairs={{0,4},{1,5},{2,6},{3,7},{4,0},{5,1},{6,2},{7,3},{8,12},{9,13},{10,... | collective-permute-start | bytes 1769480 | tf_op jit(solution)/shard_map/ppermute | solution.py:989
  315.7 12.6 %collective-permute-start.113 = (bf16[2,8,576,128]{3,2,1,0:T(8,128)(2,1)S(1)}, bf16[2,8,576,128]{3,2,1,0:T(8,128)(2,1)S(1)}, u32[]{:S(2)}, u32[]{:S(2)}) collective-permute-start(bf16[2,8,576,128]{3,2,1,0:T(8,128)(2,1)S(1)} %get-tuple-element.628), channel_id=1, source_target_pairs={{0,1},{1,0},{2,3},{3,2},{4,5},{5,4},{6,7},{7,6},{8,9},{9,8},{10,11... | collective-permute-start | bytes 7077896 | tf_op jit(solution)/shard_map/ppermute | solution.py:989
  329.5 15.2 %collective-permute-start.116 = (bf16[8,288,128]{2,1,0:T(8,128)(2,1)S(1)}, bf16[8,288,128]{2,1,0:T(8,128)(2,1)S(1)}, u32[]{:S(2)}, u32[]{:S(2)}) collective-permute-start(bf16[8,288,128]{2,1,0:T(8,128)(2,1)S(1)} %get-tuple-element.646), channel_id=1, source_target_pairs={{0,2},{1,3},{2,0},{3,1},{4,6},{5,7},{6,4},{7,5},{8,10},{9,11},{10,... | collective-permute-start | bytes 1769480 | tf_op jit(solution)/shard_map/ppermute | solution.py:989
  330.4 14.9 %collective-permute-start.117 = (bf16[2,4,288,128]{3,2,1,0:T(8,128)(2,1)S(1)}, bf16[2,4,288,128]{3,2,1,0:T(8,128)(2,1)S(1)}, u32[]{:S(2)}, u32[]{:S(2)}) collective-permute-start(bf16[2,4,288,128]{3,2,1,0:T(8,128)(2,1)S(1)} %get-tuple-element.648), channel_id=1, source_target_pairs={{0,4},{1,5},{2,6},{3,7},{4,0},{5,1},{6,2},{7,3},{8,12},{9,13},{10,... | collective-permute-start | bytes 1769480 | tf_op jit(solution)/shard_map/ppermute | solution.py:989
  371.8 19.2 %collective-permute-start.128 = (bf16[8,384,128]{2,1,0:T(8,128)(2,1)S(1)}, bf16[8,384,128]{2,1,0:T(8,128)(2,1)S(1)}, u32[]{:S(2)}, u32[]{:S(2)}) collective-permute-start(bf16[8,384,128]{2,1,0:T(8,128)(2,1)S(1)} %get-tuple-element.712), channel_id=1, source_target_pairs={{0,2},{1,3},{2,0},{3,1},{4,6},{5,7},{6,4},{7,5},{8,10},{9,11},{10,... | collective-permute-start | bytes 2359304 | tf_op jit(solution)/shard_map/ppermute | solution.py:989
  372.9 18.8 %collective-permute-start.129 = (bf16[2,4,384,128]{3,2,1,0:T(8,128)(2,1)S(1)}, bf16[2,4,384,128]{3,2,1,0:T(8,128)(2,1)S(1)}, u32[]{:S(2)}, u32[]{:S(2)}) collective-permute-start(bf16[2,4,384,128]{3,2,1,0:T(8,128)(2,1)S(1)} %get-tuple-element.714), channel_id=1, source_target_pairs={{0,4},{1,5},{2,6},{3,7},{4,0},{5,1},{6,2},{7,3},{8,12},{9,13},{10,... | collective-permute-start | bytes 2359304 | tf_op jit(solution)/shard_map/ppermute | solution.py:989
  401.9 12.8 %collective-permute-start.133 = (bf16[2,8,576,128]{3,2,1,0:T(8,128)(2,1)S(1)}, bf16[2,8,576,128]{3,2,1,0:T(8,128)(2,1)S(1)}, u32[]{:S(2)}, u32[]{:S(2)}) collective-permute-start(bf16[2,8,576,128]{3,2,1,0:T(8,128)(2,1)S(1)} %get-tuple-element.736), channel_id=1, source_target_pairs={{0,1},{1,0},{2,3},{3,2},{4,5},{5,4},{6,7},{7,6},{8,9},{9,8},{10,11... | collective-permute-start | bytes 7077896 | tf_op jit(solution)/shard_map/ppermute | solution.py:989
  416.1 14.6 %collective-permute-start.140 = (bf16[8,288,128]{2,1,0:T(8,128)(2,1)S(1)}, bf16[8,288,128]{2,1,0:T(8,128)(2,1)S(1)}, u32[]{:S(2)}, u32[]{:S(2)}) collective-permute-start(bf16[8,288,128]{2,1,0:T(8,128)(2,1)S(1)} %get-tuple-element.771), channel_id=1, source_target_pairs={{0,2},{1,3},{2,0},{3,1},{4,6},{5,7},{6,4},{7,5},{8,10},{9,11},{10,... | collective-permute-start | bytes 1769480 | tf_op jit(solution)/shard_map/ppermute | solution.py:989
  417.0 14.5 %collective-permute-start.141 = (bf16[2,4,288,128]{3,2,1,0:T(8,128)(2,1)S(1)}, bf16[2,4,288,128]{3,2,1,0:T(8,128)(2,1)S(1)}, u32[]{:S(2)}, u32[]{:S(2)}) collective-permute-start(bf16[2,4,288,128]{3,2,1,0:T(8,128)(2,1)S(1)} %get-tuple-element.773), channel_id=1, source_target_pairs={{0,4},{1,5},{2,6},{3,7},{4,0},{5,1},{6,2},{7,3},{8,12},{9,13},{10,... | collective-permute-start | bytes 1769480 | tf_op jit(solution)/shard_map/ppermute | solution.py:989
  445.9 15.0 %collective-permute-start.146 = (bf16[8,288,128]{2,1,0:T(8,128)(2,1)S(1)}, bf16[8,288,128]{2,1,0:T(8,128)(2,1)S(1)}, u32[]{:S(2)}, u32[]{:S(2)}) collective-permute-start(bf16[8,288,128]{2,1,0:T(8,128)(2,1)S(1)} %get-tuple-element.795), channel_id=1, source_target_pairs={{0,2},{1,3},{2,0},{3,1},{4,6},{5,7},{6,4},{7,5},{8,10},{9,11},{10,... | collective-permute-start | bytes 1769480 | tf_op jit(solution)/shard_map/ppermute | solution.py:989
  446.9 14.6 %collective-permute-start.147 = (bf16[2,4,288,128]{3,2,1,0:T(8,128)(2,1)S(1)}, bf16[2,4,288,128]{3,2,1,0:T(8,128)(2,1)S(1)}, u32[]{:S(2)}, u32[]{:S(2)}) collective-permute-start(bf16[2,4,288,128]{3,2,1,0:T(8,128)(2,1)S(1)} %get-tuple-element.796), channel_id=1, source_target_pairs={{0,4},{1,5},{2,6},{3,7},{4,0},{5,1},{6,2},{7,3},{8,12},{9,13},{10,... | collective-permute-start | bytes 1769480 | tf_op jit(solution)/shard_map/ppermute | solution.py:989
  448.0 12.8 %collective-permute-start.148 = (bf16[768,128]{1,0:T(8,128)(2,1)S(1)}, bf16[768,128]{1,0:T(8,128)(2,1)S(1)}, u32[]{:S(2)}, u32[]{:S(2)}) collective-permute-start(bf16[768,128]{1,0:T(8,128)(2,1)S(1)} %get-tuple-element.809), channel_id=1, source_target_pairs={{0,16},{1,17},{2,18},{3,19},{4,20},{5,21},{6,22},{7,23},{8,24},{9,... | collective-permute-start | bytes 589832 | tf_op jit(solution)/shard_map/ppermute | solution.py:989
  474.0 13.3 %collective-permute-start.152 = (bf16[8,144,128]{2,1,0:T(8,128)(2,1)S(1)}, bf16[8,144,128]{2,1,0:T(8,128)(2,1)S(1)}, u32[]{:S(2)}, u32[]{:S(2)}) collective-permute-start(bf16[8,144,128]{2,1,0:T(8,128)(2,1)S(1)} %get-tuple-element.829), channel_id=1, source_target_pairs={{0,2},{1,3},{2,0},{3,1},{4,6},{5,7},{6,4},{7,5},{8,10},{9,11},{10,... | collective-permute-start | bytes 884744 | tf_op jit(solution)/shard_map/ppermute | solution.py:989
  483.1 13.8 %collective-permute-start.159 = (bf16[576,128]{1,0:T(8,128)(2,1)}, bf16[576,128]{1,0:T(8,128)(2,1)}, u32[]{:S(2)}, u32[]{:S(2)}) collective-permute-start(bf16[576,128]{1,0:T(8,128)(2,1)} %get-tuple-element.854), channel_id=1, source_target_pairs={{0,16},{1,17},{2,18},{3,19},{4,20},{5,21},{6,22},{7,23},{8,24},{9,... | collective-permute-start | bytes 442376 | tf_op jit(solution)/shard_map/ppermute | solution.py:989
  (193 other events, 1402.4 us)

commit v6 on v5

--- a/solution.py
+++ b/solution.py
@@ -1677,7 +1677,7 @@
         tasks.append(task_layer(geom, domain, tied(pre_3, x), *pool_args[3:], masks))
         return tasks[0]
 
-    sm_2 = links.total(local, w.during(11), ORDER, w.pieces("three", act_2, win_3) + [task_part])
+    sm_2 = links.total(local, w.during(11), ORDER, w.pieces("three", act_2, win_3))
     w.send(3, sm_2)
     win_2, g_1, local = backward_layer(
         geom,
@@ -1687,7 +1687,7 @@
         lower=(pre_1, st_1, gain[0], bias[0]),
     )
     w.after_layer(2, local)
-    sm_1 = links.total(local, w.during(12), ORDER, w.pieces("two", act_1, win_2))
+    sm_1 = links.total(local, w.during(12), ORDER, w.pieces("two", act_1, win_2) + [task_part])
     win_1 = low_layer(geom, domain, (tied(g_1, w.now()), pre_1, st_1, sm_1, gain[0]))
     blocks = w.add("one", source, win_1)
     frames_grad, task_maps = w.tail(

time: 519 us -> 516 us (level)
  transfers between devices with their start and end apart: 166 -> 166, of which waited for: 87 -> 85; matrix products, arithmetic and copies ran while one was open for 3% -> 3% of each run, Pallas kernels for 27% -> 27%
where the time goes in v6:
time: 516 us; the launch traced here: 512 us
  Pallas kernels  170 us (33%)
  waiting for transfers between devices  168 us (33%)
  starting transfers between devices  151 us (29%)
  local copies, waits for them, and re-layouts  12.5 us (2%)
  other arithmetic  7.59 us (1%)
    ppermute x166, waiting for transfers between devices, swap(): return lax.ppermute(x, AXES, [(i, i ^ 1 << bit) for i in range(n)])  168 us
    ppermute x166, starting transfers between devices, swap(): return lax.ppermute(x, AXES, [(i, i ^ 1 << bit) for i in range(n)])  151 us
    pallas_call x5, Pallas kernels, backward_layer(): pl.pallas_call(functools.partial(backward_kernel, geom, added is not None...  39.2 us
    pallas_call x6, Pallas kernels, forward_layer(): pl.pallas_call(functools.partial(forward_kernel, geom, norm is not None,...  38.1 us
    pallas_call x12, Pallas kernels, weight_piece(): pl.pallas_call(functools.partial(weight_piece_kernel, geom, member, step,...  26.2 us
    pallas_call x4, Pallas kernels, weight_blocks(): pl.pallas_call(functools.partial(weight_blocks_kernel, geom, member, step...  11.7 us
    pallas_call x19, Pallas kernels, add_all(): pl.pallas_call(functools.partial(add_kernel, [(work, len(i), len(o)) for...  10.9 us
  transfers between devices with their start and end apart: 166, of which 85 were waited for; matrix products, arithmetic and copies ran while one was open for 3% of the time, Pallas kernels for 27%

profile of v6, /device:TPU:0, one launch (start us, length us, event | category | flops | bytes accessed | tf_op | source)
XLA Modules:
  0.0 512.4 jit_solution(2216686657666187810)
XLA Ops:
  0.7 4.1 collective-permute-start
  4.8 4.1 collective-permute-done
  29.5 4.4 collective-permute-done.5.refs_4_
  41.3 4.5 shard_map.237
  74.3 7.3 %shard_map.239 = (f32[1024,512]{1,0:T(8,128)S(1)}, f32[4,512]{1,0:T(4,128)S(1)}, bf16[1024,512]{1,0:T(8,128)(2,1)S(1)}, bf16[4608,512]{1,0:T(8,128)(2,1)}) custom-call(s32[2]{0:T(128)S(1)} %copy-done.23, f32[1024,512]{1,0:T(8,128)S(1)} %get-tuple-element.449.refs_1_.refs_7_.pre_ref, f32[4,512]{1,0:T(4,128)S(1)} %add.204.refs_2_.refs_8_.st_ref, ...), custom_call_target="tpu_custom_call" | custom-call | flops 483183808 | bytes 891289 | tf_op jit(solution)/shard_map/pallas_call | solution.py:257
  106.9 7.4 %shard_map.240 = (f32[1024,512]{1,0:T(8,128)S(1)}, f32[4,512]{1,0:T(4,128)S(1)}, bf16[1024,512]{1,0:T(8,128)(2,1)S(1)}, bf16[4608,512]{1,0:T(8,128)(2,1)}) custom-call(s32[2]{0:T(128)S(1)} %copy-done.23, f32[1024,512]{1,0:T(8,128)S(1)} %get-tuple-element.468.refs_1_.refs_8_.refs_2_, f32[4,512]{1,0:T(4,128)S(1)} %add.209.refs_2_.refs_9_.refs_3_, ...), custom_call_target="tpu_custom_call" | custom-call | flops 483183808 | bytes 891289 | tf_op jit(solution)/shard_map/pallas_call | solution.py:257
  144.1 7.1 %shard_map.242 = (f32[1024,512]{1,0:T(8,128)S(1)}, f32[4,512]{1,0:T(4,128)S(1)}, bf16[4608,512]{1,0:T(8,128)(2,1)}) custom-call(s32[2]{0:T(128)S(1)} %copy-done.23, bf16[1024,512]{1,0:T(8,128)(2,1)S(1)} %shard_map.241.refs_1_, s32[1]{0:T(128)} %bitcast.3.refs_2_.me_ref.refs_5_.refs_0_, bf16[8,288,128]{2,1,0:T(8,128)(2,1)S(1)} %constant_dynamic-update-slice_fusion.21.refs_3_, ...), custom_call_target="tpu_custom_call" | custom-call | flops 483183808 | bytes 891289 | tf_op jit(solution)/shard_map/pallas_call | solution.py:257
  176.1 7.3 %shard_map.243 = (f32[1024,512]{1,0:T(8,128)S(1)}, f32[4,512]{1,0:T(4,128)S(1)}, bf16[1024,512]{1,0:T(8,128)(2,1)S(1)}, bf16[4608,512]{1,0:T(8,128)(2,1)}) custom-call(s32[2]{0:T(128)S(1)} %copy-done.23, f32[1024,512]{1,0:T(8,128)S(1)} %get-tuple-element.502.refs_1_.refs_8_.refs_2_, f32[4,512]{1,0:T(4,128)S(1)} %add.219.refs_2_.refs_9_.refs_3_, ...), custom_call_target="tpu_custom_call" | custom-call | flops 483183808 | bytes 891289 | tf_op jit(solution)/shard_map/pallas_call | solution.py:257
  193.2 4.2 collective-permute-done.75
  207.8 4.5 shard_map.244
  241.8 4.6 collective-permute-done.94
  254.6 5.1 %shard_map.251 = (bf16[3,2,18,32,256]{4,3,2,1,0:T(8,128)(2,1)S(1)}, f32[1024,512]{1,0:T(8,128)S(1)}, f32[4,512]{1,0:T(4,128)S(1)}) custom-call(s32[2]{0:T(128)S(1)} %copy-done.23, f32[1024,256]{1,0:T(8,128)S(1)} %get-tuple-element.550.refs_1_, f32[1024,256]{1,0:T(8,128)S(1)} %get-tuple-element.535.bot_ref.refs_2_, f32[4,256]{1,0:T(4,128)S(1)} %slice.353.bot_st.refs_3_, ...), custom_call_target="tpu_custom_call" | custom-call | flops 241591904 | bytes 1284505 | tf_op jit(solution)/shard_map/pallas_call | solution.py:595
  264.3 4.0 shard_map.252
  286.6 8.1 %shard_map.257 = (bf16[3,2,18,32,512]{4,3,2,1,0:T(8,128)(2,1)S(1)}, f32[1024,512]{1,0:T(8,128)S(1)}, f32[4,512]{1,0:T(4,128)S(1)}) custom-call(s32[2]{0:T(128)S(1)} %copy-done.23, f32[1024,512]{1,0:T(8,128)S(1)} %copy-done.12, f32[1024,512]{1,0:T(8,128)S(1)} %get-tuple-element.519.refs_1_.refs_7_.refs_2_, f32[4,512]{1,0:T(4,128)S(1)} %add.224.refs_2_.refs_8_.refs_3_, ...), custom_call_target="tpu_custom_call" | custom-call | flops 483183808 | bytes 1520435 | tf_op jit(solution)/shard_map/pallas_call | solution.py:595
  317.9 10.2 %shard_map.263 = (bf16[3,2,18,32,512]{4,3,2,1,0:T(8,128)(2,1)S(1)}, f32[1024,512]{1,0:T(8,128)S(1)}, f32[4,512]{1,0:T(4,128)S(1)}) custom-call(s32[2]{0:T(128)S(1)} %copy-done.23, f32[1024,512]{1,0:T(8,128)S(1)} %get-tuple-element.580.refs_1_, f32[1024,512]{1,0:T(8,128)S(1)} %get-tuple-element.502.refs_1_.refs_8_.refs_2_, ...), custom_call_target="tpu_custom_call" | custom-call | flops 483183808 | bytes 1520435 | tf_op jit(solution)/shard_map/pallas_call | solution.py:595
  362.0 7.9 %shard_map.274 = (bf16[3,2,18,32,512]{4,3,2,1,0:T(8,128)(2,1)S(1)}, f32[1024,512]{1,0:T(8,128)S(1)}, f32[4,512]{1,0:T(4,128)S(1)}) custom-call(s32[2]{0:T(128)S(1)} %copy-done.23, f32[1024,512]{1,0:T(8,128)S(1)} %get-tuple-element.676.refs_1_, f32[1024,512]{1,0:T(8,128)S(1)} %get-tuple-element.774.top_ref.refs_7_.refs_2_, ...), custom_call_target="tpu_custom_call" | custom-call | flops 483183808 | bytes 1520435 | tf_op jit(solution)/shard_map/pallas_call | solution.py:595
  383.0 6.9 %collective-permute-done.128.refs_2_ = bf16[8,384,128]{2,1,0:T(8,128)(2,1)S(1)} collective-permute-done((bf16[8,384,128]{2,1,0:T(8,128)(2,1)S(1)}, bf16[8,384,128]{2,1,0:T(8,128)(2,1)S(1)}, u32[]{:S(2)}, u32[]{:S(2)}) %collective-permute-start.128) | collective-permute-done | bytes 786464 | tf_op jit(solution)/shard_map/ppermute | solution.py:989
  402.7 7.9 %shard_map.281 = (bf16[3,2,18,32,512]{4,3,2,1,0:T(8,128)(2,1)S(1)}, f32[1024,512]{1,0:T(8,128)S(1)}, f32[4,512]{1,0:T(4,128)S(1)}) custom-call(s32[2]{0:T(128)S(1)} %copy-done.23, f32[1024,512]{1,0:T(8,128)S(1)} %get-tuple-element.679.refs_1_, f32[1024,512]{1,0:T(8,128)S(1)} %get-tuple-element.468.refs_1_.refs_8_.refs_2_, ...), custom_call_target="tpu_custom_call" | custom-call | flops 483183808 | bytes 1520435 | tf_op jit(solution)/shard_map/pallas_call | solution.py:595
  434.9 5.3 %shard_map.287 = f32[2,8,3,16,512]{4,3,2,1,0:T(8,128)} custom-call(s32[2]{0:T(128)S(1)} %copy-done.23, f32[1024,512]{1,0:T(8,128)S(1)} %get-tuple-element.774.top_ref.refs_7_.refs_2_, f32[4,512]{1,0:T(4,128)S(1)} %add.214.top_st.refs_8_.refs_3_, f32[1,512]{1,0:T(1,128)S(1)} %get-tuple-element.936.gain_t.refs_9_.refs_5_, ...), custom_call_target="tpu_custom_call" | custom-call | flops 3145728 | bytes 1468006 | tf_op jit(solution)/shard_map/pallas_call | solution.py:383
  447.8 4.0 shard_map.289
  451.9 5.4 %shard_map.291 = f32[1024,256]{1,0:T(8,128)} custom-call(bf16[3,2,18,32,512]{4,3,2,1,0:T(8,128)(2,1)S(1)} %shard_map.288.refs_2_.win_ref, bf16[2304,512]{1,0:T(8,128)(2,1)} %get-tuple-element.798.kernel_ref), custom_call_target="tpu_custom_call" | custom-call | flops 241591904 | bytes 655360 | tf_op jit(solution)/shard_map/pallas_call | solution.py:659
  460.5 5.3 %collective-permute-done.149.refs_2_ = bf16[4,288,128]{2,1,0:T(8,128)(2,1)S(1)} collective-permute-done((bf16[4,288,128]{2,1,0:T(8,128)(2,1)S(1)}, bf16[4,288,128]{2,1,0:T(8,128)(2,1)S(1)}, u32[]{:S(2)}, u32[]{:S(2)}) %collective-permute-start.149) | collective-permute-done | bytes 294944 | tf_op jit(solution)/shard_map/ppermute | solution.py:989
  472.1 5.1 collective-permute-done.155.refs_4_
  501.0 4.3 collective-permute-done.161.refs_1_
  (652 shorter events, 370.3 us)
Async XLA Ops:
  47.7 16.4 %collective-permute-start.22 = (bf16[8,304,128]{2,1,0:T(8,128)(2,1)S(1)}, bf16[8,304,128]{2,1,0:T(8,128)(2,1)S(1)}, u32[]{:S(2)}, u32[]{:S(2)}) collective-permute-start(bf16[8,304,128]{2,1,0:T(8,128)(2,1)S(1)} %constant_dynamic-update-slice_fusion.11.refs_2_.refs_8_), channel_id=1, source_target_pairs={{0,4},{1,5},{2,6},{3,7},{4,0},{5,1},{6,2},{7,3},{8,12},{9,13},{10,... | collective-permute-start | bytes 1867784 | tf_op jit(solution)/shard_map/ppermute | solution.py:989
  68.6 13.0 %collective-permute-start.33 = (bf16[4,288,128]{2,1,0:T(8,128)(2,1)S(1)}, bf16[4,288,128]{2,1,0:T(8,128)(2,1)S(1)}, u32[]{:S(2)}, u32[]{:S(2)}) collective-permute-start(bf16[4,288,128]{2,1,0:T(8,128)(2,1)S(1)} %get-tuple-element.478), channel_id=1, source_target_pairs={{0,2},{1,3},{2,0},{3,1},{4,6},{5,7},{6,4},{7,5},{8,10},{9,11},{10,... | collective-permute-start | bytes 884744 | tf_op jit(solution)/shard_map/ppermute | solution.py:989
  81.7 15.2 %collective-permute-start.35 = (bf16[8,288,128]{2,1,0:T(8,128)(2,1)S(1)}, bf16[8,288,128]{2,1,0:T(8,128)(2,1)S(1)}, u32[]{:S(2)}, u32[]{:S(2)}) collective-permute-start(bf16[8,288,128]{2,1,0:T(8,128)(2,1)S(1)} %constant_dynamic-update-slice_fusion.15.refs_6_), channel_id=1, source_target_pairs={{0,2},{1,3},{2,0},{3,1},{4,6},{5,7},{6,4},{7,5},{8,10},{9,11},{10,... | collective-permute-start | bytes 1769480 | tf_op jit(solution)/shard_map/ppermute | solution.py:989
  82.4 18.2 %collective-permute-start.37 = (bf16[8,288,128]{2,1,0:T(8,128)(2,1)S(1)}, bf16[8,288,128]{2,1,0:T(8,128)(2,1)S(1)}, u32[]{:S(2)}, u32[]{:S(2)}) collective-permute-start(bf16[8,288,128]{2,1,0:T(8,128)(2,1)S(1)} %constant_dynamic-update-slice_fusion.17.refs_8_), channel_id=1, source_target_pairs={{0,4},{1,5},{2,6},{3,7},{4,0},{5,1},{6,2},{7,3},{8,12},{9,13},{10,... | collective-permute-start | bytes 1769480 | tf_op jit(solution)/shard_map/ppermute | solution.py:989
  116.8 13.7 %collective-permute-start.50 = (bf16[8,288,128]{2,1,0:T(8,128)(2,1)S(1)}, bf16[8,288,128]{2,1,0:T(8,128)(2,1)S(1)}, u32[]{:S(2)}, u32[]{:S(2)}) collective-permute-start(bf16[8,288,128]{2,1,0:T(8,128)(2,1)S(1)} %constant_dynamic-update-slice_fusion.21.refs_3_), channel_id=1, source_target_pairs={{0,2},{1,3},{2,0},{3,1},{4,6},{5,7},{6,4},{7,5},{8,10},{9,11},{10,... | collective-permute-start | bytes 1769480 | tf_op jit(solution)/shard_map/ppermute | solution.py:989
  118.3 15.8 %collective-permute-start.52 = (bf16[8,288,128]{2,1,0:T(8,128)(2,1)S(1)}, bf16[8,288,128]{2,1,0:T(8,128)(2,1)S(1)}, u32[]{:S(2)}, u32[]{:S(2)}) collective-permute-start(bf16[8,288,128]{2,1,0:T(8,128)(2,1)S(1)} %constant_dynamic-update-slice_fusion.23.refs_5_), channel_id=1, source_target_pairs={{0,4},{1,5},{2,6},{3,7},{4,0},{5,1},{6,2},{7,3},{8,12},{9,13},{10,... | collective-permute-start | bytes 1769480 | tf_op jit(solution)/shard_map/ppermute | solution.py:989
  138.0 13.2 %collective-permute-start.63 = (bf16[4,288,128]{2,1,0:T(8,128)(2,1)S(1)}, bf16[4,288,128]{2,1,0:T(8,128)(2,1)S(1)}, u32[]{:S(2)}, u32[]{:S(2)}) collective-permute-start(bf16[4,288,128]{2,1,0:T(8,128)(2,1)S(1)} %get-tuple-element.512), channel_id=1, source_target_pairs={{0,2},{1,3},{2,0},{3,1},{4,6},{5,7},{6,4},{7,5},{8,10},{9,11},{10,... | collective-permute-start | bytes 884744 | tf_op jit(solution)/shard_map/ppermute | solution.py:989
  151.3 15.0 %collective-permute-start.65 = (bf16[8,288,128]{2,1,0:T(8,128)(2,1)S(1)}, bf16[8,288,128]{2,1,0:T(8,128)(2,1)S(1)}, u32[]{:S(2)}, u32[]{:S(2)}) collective-permute-start(bf16[8,288,128]{2,1,0:T(8,128)(2,1)S(1)} %constant_dynamic-update-slice_fusion.27.refs_6_), channel_id=1, source_target_pairs={{0,2},{1,3},{2,0},{3,1},{4,6},{5,7},{6,4},{7,5},{8,10},{9,11},{10,... | collective-permute-start | bytes 1769480 | tf_op jit(solution)/shard_map/ppermute | solution.py:989
  152.9 17.1 %collective-permute-start.67 = (bf16[8,288,128]{2,1,0:T(8,128)(2,1)S(1)}, bf16[8,288,128]{2,1,0:T(8,128)(2,1)S(1)}, u32[]{:S(2)}, u32[]{:S(2)}) collective-permute-start(bf16[8,288,128]{2,1,0:T(8,128)(2,1)S(1)} %constant_dynamic-update-slice_fusion.29.refs_8_), channel_id=1, source_target_pairs={{0,4},{1,5},{2,6},{3,7},{4,0},{5,1},{6,2},{7,3},{8,12},{9,13},{10,... | collective-permute-start | bytes 1769480 | tf_op jit(solution)/shard_map/ppermute | solution.py:989
  184.6 14.7 %collective-permute-start.79 = (bf16[8,288,128]{2,1,0:T(8,128)(2,1)S(1)}, bf16[8,288,128]{2,1,0:T(8,128)(2,1)S(1)}, u32[]{:S(2)}, u32[]{:S(2)}) collective-permute-start(bf16[8,288,128]{2,1,0:T(8,128)(2,1)S(1)} %constant_dynamic-update-slice_fusion.33.refs_6_.refs_3_.refs_0_), channel_id=1, source_target_pairs={{0,2},{1,3},{2,0},{3,1},{4,6},{5,7},{6,4},{7,5},{8,10},{9,11},{10,... | collective-permute-start | bytes 1769480 | tf_op jit(solution)/shard_map/ppermute | solution.py:989
  185.4 17.6 %collective-permute-start.81 = (bf16[8,288,128]{2,1,0:T(8,128)(2,1)S(1)}, bf16[8,288,128]{2,1,0:T(8,128)(2,1)S(1)}, u32[]{:S(2)}, u32[]{:S(2)}) collective-permute-start(bf16[8,288,128]{2,1,0:T(8,128)(2,1)S(1)} %constant_dynamic-update-slice_fusion.35.refs_8_.refs_5_.refs_2_), channel_id=1, source_target_pairs={{0,4},{1,5},{2,6},{3,7},{4,0},{5,1},{6,2},{7,3},{8,12},{9,13},{10,... | collective-permute-start | bytes 1769480 | tf_op jit(solution)/shard_map/ppermute | solution.py:989
  315.5 12.6 %collective-permute-start.113 = (bf16[2,8,576,128]{3,2,1,0:T(8,128)(2,1)S(1)}, bf16[2,8,576,128]{3,2,1,0:T(8,128)(2,1)S(1)}, u32[]{:S(2)}, u32[]{:S(2)}) collective-permute-start(bf16[2,8,576,128]{3,2,1,0:T(8,128)(2,1)S(1)} %get-tuple-element.628), channel_id=1, source_target_pairs={{0,1},{1,0},{2,3},{3,2},{4,5},{5,4},{6,7},{7,6},{8,9},{9,8},{10,11... | collective-permute-start | bytes 7077896 | tf_op jit(solution)/shard_map/ppermute | solution.py:989
  328.8 15.2 %collective-permute-start.116 = (bf16[8,288,128]{2,1,0:T(8,128)(2,1)S(1)}, bf16[8,288,128]{2,1,0:T(8,128)(2,1)S(1)}, u32[]{:S(2)}, u32[]{:S(2)}) collective-permute-start(bf16[8,288,128]{2,1,0:T(8,128)(2,1)S(1)} %get-tuple-element.646), channel_id=1, source_target_pairs={{0,2},{1,3},{2,0},{3,1},{4,6},{5,7},{6,4},{7,5},{8,10},{9,11},{10,... | collective-permute-start | bytes 1769480 | tf_op jit(solution)/shard_map/ppermute | solution.py:989
  329.7 14.9 %collective-permute-start.117 = (bf16[2,4,288,128]{3,2,1,0:T(8,128)(2,1)S(1)}, bf16[2,4,288,128]{3,2,1,0:T(8,128)(2,1)S(1)}, u32[]{:S(2)}, u32[]{:S(2)}) collective-permute-start(bf16[2,4,288,128]{3,2,1,0:T(8,128)(2,1)S(1)} %get-tuple-element.648), channel_id=1, source_target_pairs={{0,4},{1,5},{2,6},{3,7},{4,0},{5,1},{6,2},{7,3},{8,12},{9,13},{10,... | collective-permute-start | bytes 1769480 | tf_op jit(solution)/shard_map/ppermute | solution.py:989
  370.8 19.1 %collective-permute-start.128 = (bf16[8,384,128]{2,1,0:T(8,128)(2,1)S(1)}, bf16[8,384,128]{2,1,0:T(8,128)(2,1)S(1)}, u32[]{:S(2)}, u32[]{:S(2)}) collective-permute-start(bf16[8,384,128]{2,1,0:T(8,128)(2,1)S(1)} %get-tuple-element.713), channel_id=1, source_target_pairs={{0,2},{1,3},{2,0},{3,1},{4,6},{5,7},{6,4},{7,5},{8,10},{9,11},{10,... | collective-permute-start | bytes 2359304 | tf_op jit(solution)/shard_map/ppermute | solution.py:989
  371.9 18.8 %collective-permute-start.129 = (bf16[2,4,384,128]{3,2,1,0:T(8,128)(2,1)S(1)}, bf16[2,4,384,128]{3,2,1,0:T(8,128)(2,1)S(1)}, u32[]{:S(2)}, u32[]{:S(2)}) collective-permute-start(bf16[2,4,384,128]{3,2,1,0:T(8,128)(2,1)S(1)} %get-tuple-element.715), channel_id=1, source_target_pairs={{0,4},{1,5},{2,6},{3,7},{4,0},{5,1},{6,2},{7,3},{8,12},{9,13},{10,... | collective-permute-start | bytes 2359304 | tf_op jit(solution)/shard_map/ppermute | solution.py:989
  398.2 12.6 %collective-permute-start.136 = (bf16[2,8,576,128]{3,2,1,0:T(8,128)(2,1)S(1)}, bf16[2,8,576,128]{3,2,1,0:T(8,128)(2,1)S(1)}, u32[]{:S(2)}, u32[]{:S(2)}) collective-permute-start(bf16[2,8,576,128]{3,2,1,0:T(8,128)(2,1)S(1)} %get-tuple-element.744), channel_id=1, source_target_pairs={{0,1},{1,0},{2,3},{3,2},{4,5},{5,4},{6,7},{7,6},{8,9},{9,8},{10,11... | collective-permute-start | bytes 7077896 | tf_op jit(solution)/shard_map/ppermute | solution.py:989
  412.2 14.7 %collective-permute-start.140 = (bf16[8,288,128]{2,1,0:T(8,128)(2,1)S(1)}, bf16[8,288,128]{2,1,0:T(8,128)(2,1)S(1)}, u32[]{:S(2)}, u32[]{:S(2)}) collective-permute-start(bf16[8,288,128]{2,1,0:T(8,128)(2,1)S(1)} %get-tuple-element.765), channel_id=1, source_target_pairs={{0,2},{1,3},{2,0},{3,1},{4,6},{5,7},{6,4},{7,5},{8,10},{9,11},{10,... | collective-permute-start | bytes 1769480 | tf_op jit(solution)/shard_map/ppermute | solution.py:989
  413.3 14.3 %collective-permute-start.141 = (bf16[2,4,288,128]{3,2,1,0:T(8,128)(2,1)S(1)}, bf16[2,4,288,128]{3,2,1,0:T(8,128)(2,1)S(1)}, u32[]{:S(2)}, u32[]{:S(2)}) collective-permute-start(bf16[2,4,288,128]{3,2,1,0:T(8,128)(2,1)S(1)} %get-tuple-element.767), channel_id=1, source_target_pairs={{0,4},{1,5},{2,6},{3,7},{4,0},{5,1},{6,2},{7,3},{8,12},{9,13},{10,... | collective-permute-start | bytes 1769480 | tf_op jit(solution)/shard_map/ppermute | solution.py:989
  442.1 15.2 %collective-permute-start.146 = (bf16[8,288,128]{2,1,0:T(8,128)(2,1)S(1)}, bf16[8,288,128]{2,1,0:T(8,128)(2,1)S(1)}, u32[]{:S(2)}, u32[]{:S(2)}) collective-permute-start(bf16[8,288,128]{2,1,0:T(8,128)(2,1)S(1)} %get-tuple-element.795), channel_id=1, source_target_pairs={{0,2},{1,3},{2,0},{3,1},{4,6},{5,7},{6,4},{7,5},{8,10},{9,11},{10,... | collective-permute-start | bytes 1769480 | tf_op jit(solution)/shard_map/ppermute | solution.py:989
  443.2 14.6 %collective-permute-start.147 = (bf16[2,4,288,128]{3,2,1,0:T(8,128)(2,1)S(1)}, bf16[2,4,288,128]{3,2,1,0:T(8,128)(2,1)S(1)}, u32[]{:S(2)}, u32[]{:S(2)}) collective-permute-start(bf16[2,4,288,128]{3,2,1,0:T(8,128)(2,1)S(1)} %get-tuple-element.796), channel_id=1, source_target_pairs={{0,4},{1,5},{2,6},{3,7},{4,0},{5,1},{6,2},{7,3},{8,12},{9,13},{10,... | collective-permute-start | bytes 1769480 | tf_op jit(solution)/shard_map/ppermute | solution.py:989
  444.2 13.1 %collective-permute-start.148 = (bf16[768,128]{1,0:T(8,128)(2,1)S(1)}, bf16[768,128]{1,0:T(8,128)(2,1)S(1)}, u32[]{:S(2)}, u32[]{:S(2)}) collective-permute-start(bf16[768,128]{1,0:T(8,128)(2,1)S(1)} %get-tuple-element.809), channel_id=1, source_target_pairs={{0,16},{1,17},{2,18},{3,19},{4,20},{5,21},{6,22},{7,23},{8,24},{9,... | collective-permute-start | bytes 589832 | tf_op jit(solution)/shard_map/ppermute | solution.py:989
  469.9 13.8 %collective-permute-start.152 = (bf16[8,144,128]{2,1,0:T(8,128)(2,1)S(1)}, bf16[8,144,128]{2,1,0:T(8,128)(2,1)S(1)}, u32[]{:S(2)}, u32[]{:S(2)}) collective-permute-start(bf16[8,144,128]{2,1,0:T(8,128)(2,1)S(1)} %get-tuple-element.829), channel_id=1, source_target_pairs={{0,2},{1,3},{2,0},{3,1},{4,6},{5,7},{6,4},{7,5},{8,10},{9,11},{10,... | collective-permute-start | bytes 884744 | tf_op jit(solution)/shard_map/ppermute | solution.py:989
  479.4 14.0 %collective-permute-start.159 = (bf16[576,128]{1,0:T(8,128)(2,1)}, bf16[576,128]{1,0:T(8,128)(2,1)}, u32[]{:S(2)}, u32[]{:S(2)}) collective-permute-start(bf16[576,128]{1,0:T(8,128)(2,1)} %get-tuple-element.854), channel_id=1, source_target_pairs={{0,16},{1,17},{2,18},{3,19},{4,20},{5,21},{6,22},{7,23},{8,24},{9,... | collective-permute-start | bytes 442376 | tf_op jit(solution)/shard_map/ppermute | solution.py:989
  (199 other events, 1421.3 us)
